TPU v7x, 32 devices: a whole 2x2x4 slice. The times are simulated.
32 devices in a mesh: dev: 32 (over z, y, x, core).
Axes of the slice: x: 2, y: 2, z: 4, core: 2. Of those that a mesh axis runs over, the one named last changes fastest.
Arguments:
- layer_input: bfloat16 [2, 3072, 2048], P(None, 'dev'), may hold values from -6 to 6
- output_cotangent: bfloat16 [2, 3072, 2048], P(None, 'dev'), may hold values from -6 to 6
- segment_ids: int32 [2, 3072], P(None, 'dev'), may hold values from 0 to 2, never falling along the last dimension, each value on 1 to 2048 neighbouring positions
- padding_mask: int32 [2, 3072], P(None, 'dev'), may hold values 0 or 1
- bucket_table: int32 [2047], replicated, may hold values from 0 to 31
- attention_norm_gain: bfloat16 [2048], P('dev'), may hold values from 0.099609375 to 1.8984375
- stacked_query_key_value: bfloat16 [2048, 6144], P('dev'), may hold values from -0.0625 to 0.0625
- attention_out: bfloat16 [2048, 2048], P('dev'), may hold values from -1.5 to 1.5
- position_bias: bfloat16 [1024], P('dev'), may hold values from -4 to 4
- feed_gain: bfloat16 [2048], P('dev'), may hold values from 0.099609375 to 1.8984375
- feed_in: bfloat16 [2048, 10240], P('dev'), may hold values from -0.125 to 0.125
- feed_out: bfloat16 [5120, 2048], P('dev'), may hold values from -0.078125 to 0.078125
Outputs:
- layer_output: bfloat16 [2, 3072, 2048], P(None, 'dev')
- input_grad: bfloat16 [2, 3072, 2048], P(None, 'dev')
- grad_attention_gain: float32 [2048], P('dev')
- grad_query_key_value: float32 [2048, 6144], P('dev')
- grad_attention_out: float32 [2048, 2048], P('dev')
- grad_position_bias: float32 [1024], P('dev')
- grad_feed_gain: float32 [2048], P('dev')
- grad_feed_in: float32 [2048, 10240], P('dev')
- grad_feed_out: float32 [5120, 2048], P('dev')
Inputs may be any that keep to these rules, and one draw needn't show every extreme that they name: `segment_ids`: segment numbers never fall along a micro-batch; every segment holds 1 to 2048 tokens.
All inputs are finite; a program needn't handle non-finite values. No bound on the sum of `padding_mask` on one device may be relied on, other than what follows from the above.
Results may differ from a plain program's by a relative error of at most 0.015.
The roundings to bfloat16 on the way count: a program that leaves them out, or rounds other values in their place, can miss the bound.
Values may be sent and summed in bfloat16 or wider, within the bound.
No kernel may reach another device: no remote copies, remote signals or barrier semaphores. Data moves between devices by JAX's collectives and lax.ppermute only.
A program may use at most 368 MiB of HBM per device.

v0:
```python
import jax
import jax.numpy as jnp
from jax import lax
from jax.sharding import PartitionSpec as P

HEAD_DIM = 64
BUCKETS = 32
WINDOW = 1024


EPS = 1e-06
heads_group = 4


def shifted(block, axis, distance):
    devices = range(lax.axis_size(axis))
    route = [(i - distance, i) for i in devices if i - distance in devices]
    return lax.ppermute(block, axis, route)


def gelu_tanh(value):
    return (
        0.5
        * value
        * (1.0 + jnp.tanh(0.7978845608028654 * (value + 0.044715 * value * value * value)))
    )


def normalize(hidden):
    scale = lax.rsqrt(jnp.mean(hidden * hidden, axis=-1, keepdims=True) + EPS)
    return (hidden * scale, scale)


def norm_back(grad_unit, unit, scale):
    return scale * (grad_unit - unit * jnp.mean(grad_unit * unit, axis=-1, keepdims=True))


def split_heads(matrix):
    length = matrix.shape[0]
    return matrix.reshape(length, -1, heads_group, HEAD_DIM).transpose(1, 2, 0, 3)


def join_heads(blocks):
    length = blocks.shape[2]
    return blocks.transpose(2, 0, 1, 3).reshape(length, -1)


def fetch_attention(attention_norm_gain, stacked_query_key_value, attention_out, position_bias):
    return (
        lax.all_gather(attention_norm_gain, "dev", axis=0, tiled=True),
        lax.all_gather(stacked_query_key_value, "dev", axis=0, tiled=True),
        lax.all_gather(attention_out, "dev", axis=0, tiled=True),
        lax.all_gather(position_bias, "dev", axis=0, tiled=True),
    )


def fetch_feed(feed_gain, feed_in, feed_out):
    return (
        lax.all_gather(feed_gain, "dev", axis=0, tiled=True),
        lax.all_gather(feed_in, "dev", axis=0, tiled=True),
        lax.all_gather(feed_out, "dev", axis=0, tiled=True),
    )


def scatter_feed(parts):
    return (
        lax.psum_scatter(parts[0], "dev", scatter_dimension=0, tiled=True),
        lax.psum_scatter(parts[1], "dev", scatter_dimension=0, tiled=True),
        lax.psum_scatter(parts[2], "dev", scatter_dimension=0, tiled=True),
    )


def gather_neighbors(keys, values, segments, padding):
    rows = keys.shape[1]
    reach = (WINDOW - 2) // rows + 1
    sequence_pieces = []
    for offset in range(reach, -reach - 1, -1):
        if offset == 0:
            sequence_pieces.append((keys, values, segments, padding))
        else:
            sequence_pieces.append(shifted((keys, values, segments, padding), "dev", offset))
    joined = tuple(
        (jnp.concatenate([piece[slot] for piece in sequence_pieces], axis=1) for slot in range(4))
    )
    return (joined, reach)


def return_key_grads(grad_keys, grad_values, reach, rows):
    total_keys = jnp.zeros(grad_keys[:, :rows].shape, jnp.float32)
    total_values = jnp.zeros(grad_values[:, :rows].shape, jnp.float32)
    for offset in range(reach, -reach - 1, -1):
        position = reach - offset
        piece_keys = grad_keys[:, position * rows : (position + 1) * rows]
        piece_values = grad_values[:, position * rows : (position + 1) * rows]
        if offset == 0:
            total_keys = total_keys + piece_keys
            total_values = total_values + piece_values
        else:
            back_keys, back_values = (
                shifted(piece_keys.astype(jnp.bfloat16), "dev", -offset).astype(piece_keys.dtype),
                shifted(piece_values.astype(jnp.bfloat16), "dev", -offset).astype(
                    piece_values.dtype
                ),
            )
            total_keys = total_keys + back_keys
            total_values = total_values + back_values
    return (total_keys, total_values)


def pair_layout(
    seg_query, seg_key, pad_key, leading_query, first_key, bucket_table, relative_bias_table
):
    query_pos = leading_query + jnp.arange(seg_query.shape[0], dtype=jnp.int32)
    key_pos = first_key + jnp.arange(seg_key.shape[0], dtype=jnp.int32)
    distance = key_pos[None, :] - query_pos[:, None]
    allowed = (
        (seg_query[:, None] == seg_key[None, :])
        & (jnp.abs(distance) < WINDOW)
        & ((pad_key[None, :] == 1) | (distance == 0))
    )
    offset = jnp.clip(distance + WINDOW - 1, 0, 2 * WINDOW - 2)
    bucket = jnp.take(bucket_table, offset)
    bucket_indicator_matrix = (
        bucket[None] == jnp.arange(BUCKETS, dtype=jnp.int32)[:, None, None]
    ).astype(jnp.bfloat16)
    bias_all = jnp.einsum(
        "ogd,oc->cgd",
        bucket_indicator_matrix,
        relative_bias_table,
        preferred_element_type=jnp.float32,
    ).astype(jnp.bfloat16)
    return (allowed, bucket_indicator_matrix, bias_all)


def group_scores(query_g, key_g, bias_g, allowed):
    logit_scores = jnp.einsum("hqd,hkd->hqk", query_g, key_g, preferred_element_type=jnp.float32)
    logit_scores = logit_scores + bias_g.astype(jnp.float32)
    return jnp.where(allowed[None], logit_scores, -1000000000.0)


def split_bias(bias_all):
    return bias_all.reshape(-1, heads_group, bias_all.shape[1], bias_all.shape[2])


def attend_forward(queries, keys_all, values_all, bias_all, allowed):

    def one_group(operands):
        query_g, key_g, value_g, bias_g = operands
        logit_scores = group_scores(query_g, key_g, bias_g, allowed)
        top = jnp.max(logit_scores, axis=-1, keepdims=True)
        expo = jnp.exp(logit_scores - top)
        total = jnp.sum(expo, axis=-1, keepdims=True)
        probs = (expo / total).astype(jnp.bfloat16)
        mixed = jnp.einsum("hqk,hkd->hqd", probs, value_g, preferred_element_type=jnp.float32)
        return (mixed.astype(jnp.bfloat16), (top + jnp.log(total))[..., 0])

    mixed, log_total = lax.map(
        one_group,
        (
            split_heads(queries),
            split_heads(keys_all),
            split_heads(values_all),
            split_bias(bias_all),
        ),
    )
    return (join_heads(mixed), log_total)


def attend_backward(
    queries, keys_all, values_all, bias_all, allowed, log_total, mixed_input_gradient
):

    def one_group(operands):
        query_g, key_g, value_g, bias_g, lse_g, grad_g = operands
        logit_scores = group_scores(query_g, key_g, bias_g, allowed)
        probs = jnp.exp(logit_scores - lse_g[..., None])
        grad_probs = jnp.einsum("hqd,hkd->hqk", grad_g, value_g, preferred_element_type=jnp.float32)
        inner = jnp.sum(probs * grad_probs, axis=-1, keepdims=True)
        score_gradient = (probs * (grad_probs - inner)).astype(jnp.bfloat16)
        grad_query = jnp.einsum(
            "hqk,hkd->hqd", score_gradient, key_g, preferred_element_type=jnp.float32
        )
        grad_key = jnp.einsum(
            "hqk,hqd->hkd", score_gradient, query_g, preferred_element_type=jnp.float32
        )
        grad_value = jnp.einsum(
            "hqk,hqd->hkd", probs.astype(jnp.bfloat16), grad_g, preferred_element_type=jnp.float32
        )
        return (grad_query, grad_key, grad_value, score_gradient)

    grad_query, grad_key, grad_value, attention_score_gradient = lax.map(
        one_group,
        (
            split_heads(queries),
            split_heads(keys_all),
            split_heads(values_all),
            split_bias(bias_all),
            log_total,
            split_heads(mixed_input_gradient),
        ),
    )
    return (
        join_heads(grad_query),
        join_heads(grad_key),
        join_heads(grad_value),
        attention_score_gradient,
    )


def run_layer(layer_input, output_cotangent, segment_ids, padding_mask, bucket_table, shards):
    (
        attention_norm_gain,
        stacked_query_key_value,
        attention_out,
        position_bias,
        feed_gain,
        feed_in,
        feed_out,
    ) = shards
    batch_count, rows, width = layer_input.shape
    device = lax.axis_index("dev")
    tokens = layer_input.astype(jnp.float32).reshape(batch_count * rows, width)
    gain_attn, project_full, out_full, bias_full = fetch_attention(
        attention_norm_gain, stacked_query_key_value, attention_out, position_bias
    )
    gain_attn_f = gain_attn.astype(jnp.float32)
    unit_one, scale_one = normalize(tokens)
    normed_one = (unit_one * gain_attn_f).astype(jnp.bfloat16)
    projected = jnp.dot(normed_one, project_full, preferred_element_type=jnp.float32).astype(
        jnp.bfloat16
    )
    projected = projected.reshape(batch_count, rows, 3 * width)
    queries = projected[:, :, :width]
    keys = projected[:, :, width : 2 * width]
    values = projected[:, :, 2 * width :]
    (keys_all, values_all, segs_all, pads_all), reach = gather_neighbors(
        keys, values, segment_ids, padding_mask
    )
    relative_bias_table = bias_full.reshape(BUCKETS, -1)
    leading_query = device * rows
    first_key = (device - reach) * rows
    mixed_parts = []
    totals = []
    for batch in range(batch_count):
        allowed, bucket_indicator_matrix, bias_all = pair_layout(
            segment_ids[batch],
            segs_all[batch],
            pads_all[batch],
            leading_query,
            first_key,
            bucket_table,
            relative_bias_table,
        )
        mixed_one, log_total = attend_forward(
            queries[batch], keys_all[batch], values_all[batch], bias_all, allowed
        )
        mixed_parts.append(mixed_one)
        totals.append(log_total)
    mixed = jnp.concatenate(mixed_parts, axis=0)
    hidden_one = tokens + jnp.dot(mixed, out_full, preferred_element_type=jnp.float32)
    gain_feed, expand_full, down_full = fetch_feed(feed_gain, feed_in, feed_out)
    feed_norm_gain_float = gain_feed.astype(jnp.float32)
    unit_two, scale_two = normalize(hidden_one)
    normed_two = (unit_two * feed_norm_gain_float).astype(jnp.bfloat16)
    gate_up = jnp.dot(normed_two, expand_full, preferred_element_type=jnp.float32)
    hidden_units = expand_full.shape[1] // 2
    gate = gate_up[:, :hidden_units]
    upward = gate_up[:, hidden_units:]
    activated, gelu_pull = jax.vjp(gelu_tanh, gate)
    inner = (activated * upward).astype(jnp.bfloat16)
    final_output = hidden_one + jnp.dot(inner, down_full, preferred_element_type=jnp.float32)
    layer_output = final_output.astype(jnp.bfloat16).reshape(batch_count, rows, width)
    grad_res = output_cotangent.astype(jnp.float32).reshape(-1, width) * padding_mask.reshape(-1)[
        :, None
    ].astype(jnp.float32)
    grad_res_low = grad_res.astype(jnp.bfloat16)
    gain_feed, expand_full, down_full = fetch_feed(feed_gain, feed_in, feed_out)
    feed_norm_gain_float = gain_feed.astype(jnp.float32)
    grad_down = jnp.einsum("nf,nd->fd", inner, grad_res_low, preferred_element_type=jnp.float32)
    grad_inner = jnp.einsum(
        "nd,fd->nf", grad_res_low, down_full, preferred_element_type=jnp.float32
    )
    grad_gate = gelu_pull(grad_inner * upward)[0]
    grad_upward = grad_inner * activated
    grad_gate_up = jnp.concatenate([grad_gate, grad_upward], axis=-1).astype(jnp.bfloat16)
    grad_expand = jnp.einsum(
        "nd,nf->df", normed_two, grad_gate_up, preferred_element_type=jnp.float32
    )
    grad_normed_two = jnp.einsum(
        "nf,df->nd", grad_gate_up, expand_full, preferred_element_type=jnp.float32
    )
    grad_gain_feed = jnp.sum(grad_normed_two * unit_two, axis=0)
    grad_hidden = grad_res + norm_back(grad_normed_two * feed_norm_gain_float, unit_two, scale_two)
    feed_parts = (grad_gain_feed, grad_expand, grad_down)
    gain_attn, project_full, out_full, bias_full = fetch_attention(
        attention_norm_gain, stacked_query_key_value, attention_out, position_bias
    )
    gain_attn_f = gain_attn.astype(jnp.float32)
    relative_bias_table = bias_full.reshape(BUCKETS, -1)
    grad_hidden_low = grad_hidden.astype(jnp.bfloat16)
    grad_out = jnp.einsum("nd,ne->de", mixed, grad_hidden_low, preferred_element_type=jnp.float32)
    mixed_input_gradient = jnp.einsum(
        "ne,de->nd", grad_hidden_low, out_full, preferred_element_type=jnp.float32
    ).astype(jnp.bfloat16)
    mixed_input_gradient = mixed_input_gradient.reshape(batch_count, rows, width)
    query_grads = []
    key_grads = []
    value_grads = []
    table_grad = jnp.zeros((BUCKETS, relative_bias_table.shape[1]), jnp.float32)
    for batch in range(batch_count):
        allowed, bucket_indicator_matrix, bias_all = pair_layout(
            segment_ids[batch],
            segs_all[batch],
            pads_all[batch],
            leading_query,
            first_key,
            bucket_table,
            relative_bias_table,
        )
        grad_query, grad_key, grad_value, attention_score_gradient = attend_backward(
            queries[batch],
            keys_all[batch],
            values_all[batch],
            bias_all,
            allowed,
            totals[batch],
            mixed_input_gradient[batch],
        )
        table_part = jnp.einsum(
            "tads,wds->wta",
            attention_score_gradient,
            bucket_indicator_matrix,
            preferred_element_type=jnp.float32,
        )
        table_grad = table_grad + table_part.reshape(BUCKETS, -1)
        query_grads.append(grad_query)
        key_grads.append(grad_key)
        value_grads.append(grad_value)
    total_keys, total_values = return_key_grads(
        jnp.stack(key_grads, axis=0), jnp.stack(value_grads, axis=0), reach, rows
    )
    grad_projected = jnp.concatenate(
        [jnp.stack(query_grads, axis=0), total_keys, total_values], axis=-1
    )
    grad_projected = grad_projected.astype(jnp.bfloat16).reshape(batch_count * rows, 3 * width)
    grad_project = jnp.einsum(
        "nd,ne->de", normed_one, grad_projected, preferred_element_type=jnp.float32
    )
    grad_normed_one = jnp.einsum(
        "ne,de->nd", grad_projected, project_full, preferred_element_type=jnp.float32
    )
    grad_gain_attn = jnp.sum(grad_normed_one * unit_one, axis=0)
    grad_tokens = grad_hidden + norm_back(grad_normed_one * gain_attn_f, unit_one, scale_one)
    grad_bias = table_grad.reshape(-1)
    input_grad = grad_tokens.astype(jnp.bfloat16).reshape(batch_count, rows, width)
    attention_parts = (grad_gain_attn, grad_project, grad_out, grad_bias)
    return (layer_output, input_grad, attention_parts, feed_parts)


def local(
    layer_input,
    output_cotangent,
    segment_ids,
    padding_mask,
    bucket_table,
    attention_norm_gain,
    stacked_query_key_value,
    attention_out,
    position_bias,
    feed_gain,
    feed_in,
    feed_out,
):
    shards = (
        attention_norm_gain,
        stacked_query_key_value,
        attention_out,
        position_bias,
        feed_gain,
        feed_in,
        feed_out,
    )
    layer_output, input_grad, attention_parts, feed_parts = run_layer(
        layer_input, output_cotangent, segment_ids, padding_mask, bucket_table, shards
    )
    feed_parts = scatter_feed(feed_parts)
    grad_gain_feed, grad_expand, grad_down = feed_parts
    grad_gain_attn, grad_project, grad_out, grad_bias = (
        lax.psum_scatter(attention_parts[0], "dev", scatter_dimension=0, tiled=True),
        lax.psum_scatter(attention_parts[1], "dev", scatter_dimension=0, tiled=True),
        lax.psum_scatter(attention_parts[2], "dev", scatter_dimension=0, tiled=True),
        lax.psum_scatter(attention_parts[3], "dev", scatter_dimension=0, tiled=True),
    )
    return (
        layer_output,
        input_grad,
        grad_gain_attn,
        grad_project,
        grad_out,
        grad_bias,
        grad_gain_feed,
        grad_expand,
        grad_down,
    )


def solution(mesh):
    return jax.shard_map(
        local,
        mesh=mesh,
        in_specs=(
            P(None, "dev", None),
            P(None, "dev", None),
            P(None, "dev"),
            P(None, "dev"),
            P(),
            P("dev"),
            P("dev", None),
            P("dev", None),
            P("dev"),
            P("dev"),
            P("dev", None),
            P("dev", None),
        ),
        out_specs=(
            P(None, "dev", None),
            P(None, "dev", None),
            P("dev"),
            P("dev", None),
            P("dev", None),
            P("dev"),
            P("dev"),
            P("dev", None),
            P("dev", None),
        ),
        check_vma=False,
    )
```

profile of v0, /device:TPU:0, one launch (start us, length us, event | category | flops | bytes accessed | tf_op | source)
XLA Modules:
  0.0 5296.3 jit_solution(2939286379522598094)
XLA Ops:
  30.7 1171.9 %gather_fusion = s32[211968]{0:T(1024)S(1)} fusion(s32[2047]{0:T(1024)S(1)} %copy-done, s32[211968]{0:T(1024)S(1)} %broadcast_clamp_fusion), kind=kCustom, calls=%fused_computation.clone | custom fusion | bytes 2543616 | tf_op jit(solution)/shard_map/jit(_take)/gather | solution.py:122
  1204.5 37.1 all-reduce.7
  1444.8 38.9 collective-permute-start.73
  1488.0 17.4 collective-permute-start.75
  1506.9 28.5 collective-permute-start.45
  1535.5 52.4 collective-permute-start.46
  1589.4 48.8 collective-permute-start.48
  1646.8 28.6 collective-permute-start.51
  1698.4 20.2 collective-permute-done.51
  1753.1 55.9 %collective-permute-done.58 = bf16[2,96,2048]{2,1,0:T(8,128)(2,1)S(1)} collective-permute-done((bf16[2,96,2048]{2,1,0:T(8,128)(2,1)}, bf16[2,96,2048]{2,1,0:T(8,128)(2,1)S(1)}, u32[]{:S(2)}, u32[]{:S(2)}) %collective-permute-start.58) | collective-permute-done | bytes 786464 | tf_op jit(solution)/shard_map/ppermute | solution.py:18
  1814.5 30.1 collective-permute-done.62
  1858.9 23.2 collective-permute-done.64
  1913.9 86.5 %collective-permute-done.81 = bf16[2,96,2048]{2,1,0:T(8,128)(2,1)S(1)} collective-permute-done((bf16[2,96,2048]{2,1,0:T(8,128)(2,1)}, bf16[2,96,2048]{2,1,0:T(8,128)(2,1)S(1)}, u32[]{:S(2)}, u32[]{:S(2)}) %collective-permute-start.81) | collective-permute-done | bytes 786464 | tf_op jit(solution)/shard_map/ppermute | solution.py:18
  2002.7 33.3 collective-permute-done.82
  2051.1 56.2 %collective-permute-done.84 = bf16[2,96,2048]{2,1,0:T(8,128)(2,1)S(1)} collective-permute-done((bf16[2,96,2048]{2,1,0:T(8,128)(2,1)}, bf16[2,96,2048]{2,1,0:T(8,128)(2,1)S(1)}, u32[]{:S(2)}, u32[]{:S(2)}) %collective-permute-start.84) | collective-permute-done | bytes 786464 | tf_op jit(solution)/shard_map/ppermute | solution.py:18
  2108.2 13.1 collective-permute-done.85
  2122.3 25.1 collective-permute-done.86
  2157.4 12.7 fusion.194
  2170.1 12.4 copy.190
  2206.5 50.0 while.61
  2256.6 49.9 while.60
  2313.1 21.4 fusion.187
  2334.5 17.1 fusion.148
  2351.6 22.0 multiply_reduce_fusion.2
  2414.6 113.0 %while.63 = (s32[]{:T(128)}, bf16[8,4,96,64]{2,3,1,0:T(8,128)(2,1)S(1)}, f32[8,4,2208,64]{2,3,1,0:T(8,128)}, f32[8,4,2208,64]{2,3,1,0:T(8,128)}, bf16[8,4,96,220...) while((s32[]{:T(128)}, ...), condition=%wide.region_16.18_spmd.clone, body=%wide.region_14.17_spmd.clone.sunk | while | flops 552812160 | bytes 38305100 | solution.py:191
  2527.5 18.7 copy.200
  2570.4 118.7 %while.62 = (s32[]{:T(128)}, bf16[8,4,96,64]{2,3,1,0:T(8,128)(2,1)S(1)}, f32[8,4,2208,64]{2,3,1,0:T(8,128)}, f32[8,4,2208,64]{2,3,1,0:T(8,128)}, bf16[8,4,96,220...) while((s32[]{:T(128)}, ...), condition=%wide.region_13.15_spmd.clone, body=%wide.region_11.14_spmd.clone.sunk | while | flops 552812160 | bytes 38305100 | solution.py:191
  2689.2 18.5 copy.199
  2707.7 13.4 fusion.132
  2735.6 29.9 collective-permute-start.129
  2765.5 49.8 collective-permute-start.128
  2819.7 17.9 collective-permute-start.126
  2846.6 18.4 collective-permute-start.123
  2865.0 18.5 copy.198
  2883.5 18.5 copy.197
  2902.1 19.6 collective-permute-start.122
  2921.7 15.6 collective-permute-start.121
  2941.3 13.3 fusion.133
  2962.2 14.2 collective-permute-done.119
  2997.5 40.3 collective-permute-done.115
  3039.1 60.4 %collective-permute-start.109 = (bf16[2,96,2048]{2,1,0:T(8,128)(2,1)}, bf16[2,96,2048]{2,1,0:T(8,128)(2,1)S(1)}, u32[]{:S(2)}, u32[]{:S(2)}) collective-permute-start(bf16[2,96,2048]{2,1,0:T(8,128)(2,1)} %get-tuple-element.797), channel_id=1, source_target_pairs={{0,11},{1,12},{2,13},{3,14},{4,15},{5,16},{6,17},{7,18},{8,19},{9,... | collective-permute-start | bytes 2359304 | tf_op jit(solution)/shard_map/ppermute | solution.py:18
  3099.5 17.4 collective-permute-start.108
  3116.9 31.4 collective-permute-start.107
  3148.4 17.4 collective-permute-start.106
  3165.8 23.0 collective-permute-start.105
  3188.8 15.9 collective-permute-start.104
  3214.2 13.7 collective-permute-done.104
  3229.2 26.6 collective-permute-done.103
  3257.1 15.6 collective-permute-done.102
  3297.2 15.2 collective-permute-done.95
  3313.7 34.7 collective-permute-done.94
  3361.2 37.3 collective-permute-done.91
  3404.4 28.2 collective-permute-done.89
  3448.0 21.2 fusion.175
  3470.9 16.2 fusion.199
  3489.1 30.4 fusion.151
  3520.7 22.8 fusion.160
  3543.5 22.7 fusion.170
  3566.5 17.3 fusion.153
  3583.9 17.9 multiply_reduce_fusion.3
  3601.8 115.8 %all-reduce.6 = (f32[2048]{0:T(1024)S(1)}, f32[1024]{0:T(1024)S(1)}, f32[2048]{0:T(1024)S(1)}) all-reduce(f32[2048]{0:T(1024)S(1)} %get-tuple-element.660, f32[1024]{0:T(1024)S(1)} %add.346, f32[2048]{0:T(1024)S(1)} %copy-done.72), channel_id=2, replica_groups=mesh['dev'=32] {'dev'}, use_global_device_ids=true, to_apply=%region_19.21.clone | all-reduce | flops 5120 | bytes 40960
  3722.2 235.3 %reduce-scatter.5.cloned.1.call-done = f32[64,6144]{1,0:T(8,128)} async-done(((f32[2048,6144]{1,0:T(8,128)}), f32[64,6144]{1,0:T(8,128)}) %reduce-scatter.5.cloned.1.call-update) | async-done | bytes 1572880 | tf_op jit(solution)/shard_map/reduce_scatter | solution.py:390
  3957.6 443.8 %reduce-scatter.11.cloned.1.call-done = f32[160,2048]{1,0:T(8,128)} async-done(((f32[5120,2048]{1,0:T(8,128)}), f32[160,2048]{1,0:T(8,128)}) %reduce-scatter.11.cloned.1.call-update) | async-done | bytes 1310736 | tf_op jit(solution)/shard_map/reduce_scatter | solution.py:69
  4401.3 887.8 %reduce-scatter.9.cloned.1.call-done = f32[64,10240]{1,0:T(8,128)} async-done(((f32[2048,10240]{1,0:T(8,128)}), f32[64,10240]{1,0:T(8,128)}) %reduce-scatter.9.cloned.1.call-update) | async-done | bytes 2621456 | tf_op jit(solution)/shard_map/reduce_scatter | solution.py:68
  (755 shorter events, 949.9 us)
Async XLA Ops:
  7.2 1328.2 %all-gather.5.cloned.1.call-start = ((), (), s32[]{:S(2)}) async-start(), calls=%async_computation.4 | async-start | bytes 25952256 | tf_op jit(solution)/shard_map/all_gather | solution.py:51
  7.9 2298.7 %all-gather.7.cloned.1.call-start = ((), (), s32[]{:S(2)}) async-start(), calls=%async_computation.5 | async-start | bytes 8650752 | tf_op jit(solution)/shard_map/all_gather | solution.py:52
  8.7 2304.4 %all-gather.9.cloned.1.call-start = ((), (), s32[]{:S(2)}) async-start(), calls=%async_computation.6 | async-start | bytes 43253760 | tf_op jit(solution)/shard_map/all_gather | solution.py:60
  9.4 2325.1 %all-gather.11.cloned.1.call-start = ((), (), s32[]{:S(2)}) async-start(), calls=%async_computation.7 | async-start | bytes 21626880 | tf_op jit(solution)/shard_map/all_gather | solution.py:61
  9.5 1232.2 %collective-permute-start = (s32[2,96]{1,0:T(2,128)}, s32[2,96]{1,0:T(2,128)}, u32[]{:S(2)}, u32[]{:S(2)}) collective-permute-start(s32[2,96]{1,0:T(2,128)} %param.24), channel_id=1, source_target_pairs={{0,11},{1,12},{2,13},{3,14},{4,15},{5,16},{6,17},{7,18},{8,19},{9,... | collective-permute-start | bytes 2312 | tf_op jit(solution)/shard_map/ppermute | solution.py:18
  15.3 1231.0 %collective-permute-start.1 = (s32[2,96]{1,0:T(2,128)}, s32[2,96]{1,0:T(2,128)}, u32[]{:S(2)}, u32[]{:S(2)}) collective-permute-start(s32[2,96]{1,0:T(2,128)} %param.24), channel_id=1, source_target_pairs={{0,10},{1,11},{2,12},{3,13},{4,14},{5,15},{6,16},{7,17},{8,18},{9,... | collective-permute-start | bytes 2312 | tf_op jit(solution)/shard_map/ppermute | solution.py:18
  20.2 1229.2 %collective-permute-start.2 = (s32[2,96]{1,0:T(2,128)}, s32[2,96]{1,0:T(2,128)}, u32[]{:S(2)}, u32[]{:S(2)}) collective-permute-start(s32[2,96]{1,0:T(2,128)} %param.24), channel_id=1, source_target_pairs={{0,9},{1,10},{2,11},{3,12},{4,13},{5,14},{6,15},{7,16},{8,17},{9,1... | collective-permute-start | bytes 2312 | tf_op jit(solution)/shard_map/ppermute | solution.py:18
  23.8 1229.2 %collective-permute-start.3 = (s32[2,96]{1,0:T(2,128)}, s32[2,96]{1,0:T(2,128)}, u32[]{:S(2)}, u32[]{:S(2)}) collective-permute-start(s32[2,96]{1,0:T(2,128)} %param.24), channel_id=1, source_target_pairs={{0,8},{1,9},{2,10},{3,11},{4,12},{5,13},{6,14},{7,15},{8,16},{9,17... | collective-permute-start | bytes 2312 | tf_op jit(solution)/shard_map/ppermute | solution.py:18
  25.6 1231.5 %collective-permute-start.4 = (s32[2,96]{1,0:T(2,128)}, s32[2,96]{1,0:T(2,128)}, u32[]{:S(2)}, u32[]{:S(2)}) collective-permute-start(s32[2,96]{1,0:T(2,128)} %param.24), channel_id=1, source_target_pairs={{0,7},{1,8},{2,9},{3,10},{4,11},{5,12},{6,13},{7,14},{8,15},{9,16}... | collective-permute-start | bytes 2312 | tf_op jit(solution)/shard_map/ppermute | solution.py:18
  28.4 3693.8 %reduce-scatter.7.cloned.1.call-start = ((), (), s32[]{:S(2)}) async-start(), calls=%async_computation.9 | async-start | bytes 17301504 | tf_op jit(solution)/shard_map/reduce_scatter | solution.py:391
  1402.4 82.5 %collective-permute-start.69 = (bf16[2,96,2048]{2,1,0:T(8,128)(2,1)}, bf16[2,96,2048]{2,1,0:T(8,128)(2,1)}, u32[]{:S(2)}, u32[]{:S(2)}) collective-permute-start(bf16[2,96,2048]{2,1,0:T(8,128)(2,1)} %get-tuple-element.851), channel_id=1, source_target_pairs={{0,8},{1,9},{2,10},{3,11},{4,12},{5,13},{6,14},{7,15},{8,16},{9,17... | collective-permute-start | bytes 2359304 | tf_op jit(solution)/shard_map/ppermute | solution.py:18
  1407.2 80.7 %collective-permute-start.70 = (bf16[2,96,2048]{2,1,0:T(8,128)(2,1)}, bf16[2,96,2048]{2,1,0:T(8,128)(2,1)S(1)}, u32[]{:S(2)}, u32[]{:S(2)}) collective-permute-start(bf16[2,96,2048]{2,1,0:T(8,128)(2,1)} %get-tuple-element.851), channel_id=1, source_target_pairs={{0,7},{1,8},{2,9},{3,10},{4,11},{5,12},{6,13},{7,14},{8,15},{9,16}... | collective-permute-start | bytes 2359304 | tf_op jit(solution)/shard_map/ppermute | solution.py:18
  1411.1 94.3 %collective-permute-start.71 = (bf16[2,96,2048]{2,1,0:T(8,128)(2,1)}, bf16[2,96,2048]{2,1,0:T(8,128)(2,1)S(1)}, u32[]{:S(2)}, u32[]{:S(2)}) collective-permute-start(bf16[2,96,2048]{2,1,0:T(8,128)(2,1)} %get-tuple-element.851), channel_id=1, source_target_pairs={{0,6},{1,7},{2,8},{3,9},{4,10},{5,11},{6,12},{7,13},{8,14},{9,15},... | collective-permute-start | bytes 2359304 | tf_op jit(solution)/shard_map/ppermute | solution.py:18
  1428.0 78.9 %collective-permute-start.72 = (bf16[2,96,2048]{2,1,0:T(8,128)(2,1)}, bf16[2,96,2048]{2,1,0:T(8,128)(2,1)S(1)}, u32[]{:S(2)}, u32[]{:S(2)}) collective-permute-start(bf16[2,96,2048]{2,1,0:T(8,128)(2,1)} %get-tuple-element.851), channel_id=1, source_target_pairs={{0,5},{1,6},{2,7},{3,8},{4,9},{5,10},{6,11},{7,12},{8,13},{9,14},{... | collective-permute-start | bytes 2359304 | tf_op jit(solution)/shard_map/ppermute | solution.py:18
  1444.8 90.7 %collective-permute-start.73 = (bf16[2,96,2048]{2,1,0:T(8,128)(2,1)}, bf16[2,96,2048]{2,1,0:T(8,128)(2,1)S(1)}, u32[]{:S(2)}, u32[]{:S(2)}) collective-permute-start(bf16[2,96,2048]{2,1,0:T(8,128)(2,1)} %get-tuple-element.851), channel_id=1, source_target_pairs={{0,4},{1,5},{2,6},{3,7},{4,8},{5,9},{6,10},{7,11},{8,12},{9,13},{1... | collective-permute-start | bytes 2359304 | tf_op jit(solution)/shard_map/ppermute | solution.py:18
  1484.9 103.0 %collective-permute-start.74 = (bf16[2,96,2048]{2,1,0:T(8,128)(2,1)}, bf16[2,96,2048]{2,1,0:T(8,128)(2,1)S(1)}, u32[]{:S(2)}, u32[]{:S(2)}) collective-permute-start(bf16[2,96,2048]{2,1,0:T(8,128)(2,1)} %get-tuple-element.851), channel_id=1, source_target_pairs={{0,3},{1,4},{2,5},{3,6},{4,7},{5,8},{6,9},{7,10},{8,11},{9,12},{10... | collective-permute-start | bytes 2359304 | tf_op jit(solution)/shard_map/ppermute | solution.py:18
  1488.0 101.4 %collective-permute-start.75 = (bf16[2,96,2048]{2,1,0:T(8,128)(2,1)}, bf16[2,96,2048]{2,1,0:T(8,128)(2,1)S(1)}, u32[]{:S(2)}, u32[]{:S(2)}) collective-permute-start(bf16[2,96,2048]{2,1,0:T(8,128)(2,1)} %get-tuple-element.851), channel_id=1, source_target_pairs={{0,2},{1,3},{2,4},{3,5},{4,6},{5,7},{6,8},{7,9},{8,10},{9,11},{10,... | collective-permute-start | bytes 2359304 | tf_op jit(solution)/shard_map/ppermute | solution.py:18
  1505.5 132.8 %collective-permute-start.76 = (bf16[2,96,2048]{2,1,0:T(8,128)(2,1)}, bf16[2,96,2048]{2,1,0:T(8,128)(2,1)S(1)}, u32[]{:S(2)}, u32[]{:S(2)}) collective-permute-start(bf16[2,96,2048]{2,1,0:T(8,128)(2,1)} %get-tuple-element.851), channel_id=1, source_target_pairs={{0,1},{1,2},{2,3},{3,4},{4,5},{5,6},{6,7},{7,8},{8,9},{9,10},{10,1... | collective-permute-start | bytes 2359304 | tf_op jit(solution)/shard_map/ppermute | solution.py:18
  1506.9 133.6 %collective-permute-start.45 = (bf16[2,96,2048]{2,1,0:T(8,128)(2,1)}, bf16[2,96,2048]{2,1,0:T(8,128)(2,1)S(1)}, u32[]{:S(2)}, u32[]{:S(2)}) collective-permute-start(bf16[2,96,2048]{2,1,0:T(8,128)(2,1)} %get-tuple-element.852), channel_id=1, source_target_pairs={{0,10},{1,11},{2,12},{3,13},{4,14},{5,15},{6,16},{7,17},{8,18},{9,... | collective-permute-start | bytes 2359304 | tf_op jit(solution)/shard_map/ppermute | solution.py:18
  1535.5 111.3 %collective-permute-start.46 = (bf16[2,96,2048]{2,1,0:T(8,128)(2,1)}, bf16[2,96,2048]{2,1,0:T(8,128)(2,1)S(1)}, u32[]{:S(2)}, u32[]{:S(2)}) collective-permute-start(bf16[2,96,2048]{2,1,0:T(8,128)(2,1)} %get-tuple-element.852), channel_id=1, source_target_pairs={{0,9},{1,10},{2,11},{3,12},{4,13},{5,14},{6,15},{7,16},{8,17},{9,1... | collective-permute-start | bytes 2359304 | tf_op jit(solution)/shard_map/ppermute | solution.py:18
  1588.0 87.5 %collective-permute-start.47 = (bf16[2,96,2048]{2,1,0:T(8,128)(2,1)}, bf16[2,96,2048]{2,1,0:T(8,128)(2,1)S(1)}, u32[]{:S(2)}, u32[]{:S(2)}) collective-permute-start(bf16[2,96,2048]{2,1,0:T(8,128)(2,1)} %get-tuple-element.852), channel_id=1, source_target_pairs={{0,8},{1,9},{2,10},{3,11},{4,12},{5,13},{6,14},{7,15},{8,16},{9,17... | collective-permute-start | bytes 2359304 | tf_op jit(solution)/shard_map/ppermute | solution.py:18
  1589.4 87.5 %collective-permute-start.48 = (bf16[2,96,2048]{2,1,0:T(8,128)(2,1)}, bf16[2,96,2048]{2,1,0:T(8,128)(2,1)S(1)}, u32[]{:S(2)}, u32[]{:S(2)}) collective-permute-start(bf16[2,96,2048]{2,1,0:T(8,128)(2,1)} %get-tuple-element.852), channel_id=1, source_target_pairs={{0,7},{1,8},{2,9},{3,10},{4,11},{5,12},{6,13},{7,14},{8,15},{9,16}... | collective-permute-start | bytes 2359304 | tf_op jit(solution)/shard_map/ppermute | solution.py:18
  1646.8 71.8 %collective-permute-start.51 = (bf16[2,96,2048]{2,1,0:T(8,128)(2,1)}, bf16[2,96,2048]{2,1,0:T(8,128)(2,1)S(1)}, u32[]{:S(2)}, u32[]{:S(2)}) collective-permute-start(bf16[2,96,2048]{2,1,0:T(8,128)(2,1)} %get-tuple-element.852), channel_id=1, source_target_pairs={{0,4},{1,5},{2,6},{3,7},{4,8},{5,9},{6,10},{7,11},{8,12},{9,13},{1... | collective-permute-start | bytes 2359304 | tf_op jit(solution)/shard_map/ppermute | solution.py:18
  1721.3 87.6 %collective-permute-start.58 = (bf16[2,96,2048]{2,1,0:T(8,128)(2,1)}, bf16[2,96,2048]{2,1,0:T(8,128)(2,1)S(1)}, u32[]{:S(2)}, u32[]{:S(2)}) collective-permute-start(bf16[2,96,2048]{2,1,0:T(8,128)(2,1)} %get-tuple-element.852), channel_id=1, source_target_pairs={{4,0},{5,1},{6,2},{7,3},{8,4},{9,5},{10,6},{11,7},{12,8},{13,9},{1... | collective-permute-start | bytes 2359304 | tf_op jit(solution)/shard_map/ppermute | solution.py:18
  1722.7 87.6 %collective-permute-start.59 = (bf16[2,96,2048]{2,1,0:T(8,128)(2,1)}, bf16[2,96,2048]{2,1,0:T(8,128)(2,1)S(1)}, u32[]{:S(2)}, u32[]{:S(2)}) collective-permute-start(bf16[2,96,2048]{2,1,0:T(8,128)(2,1)} %get-tuple-element.852), channel_id=1, source_target_pairs={{5,0},{6,1},{7,2},{8,3},{9,4},{10,5},{11,6},{12,7},{13,8},{14,9},{... | collective-permute-start | bytes 2359304 | tf_op jit(solution)/shard_map/ppermute | solution.py:18
  1725.1 86.6 %collective-permute-start.60 = (bf16[2,96,2048]{2,1,0:T(8,128)(2,1)}, bf16[2,96,2048]{2,1,0:T(8,128)(2,1)S(1)}, u32[]{:S(2)}, u32[]{:S(2)}) collective-permute-start(bf16[2,96,2048]{2,1,0:T(8,128)(2,1)} %get-tuple-element.852), channel_id=1, source_target_pairs={{6,0},{7,1},{8,2},{9,3},{10,4},{11,5},{12,6},{13,7},{14,8},{15,9},... | collective-permute-start | bytes 2359304 | tf_op jit(solution)/shard_map/ppermute | solution.py:18
  1738.2 74.9 %collective-permute-start.61 = (bf16[2,96,2048]{2,1,0:T(8,128)(2,1)}, bf16[2,96,2048]{2,1,0:T(8,128)(2,1)S(1)}, u32[]{:S(2)}, u32[]{:S(2)}) collective-permute-start(bf16[2,96,2048]{2,1,0:T(8,128)(2,1)} %get-tuple-element.852), channel_id=1, source_target_pairs={{7,0},{8,1},{9,2},{10,3},{11,4},{12,5},{13,6},{14,7},{15,8},{16,9}... | collective-permute-start | bytes 2359304 | tf_op jit(solution)/shard_map/ppermute | solution.py:18
  1751.7 92.9 %collective-permute-start.62 = (bf16[2,96,2048]{2,1,0:T(8,128)(2,1)}, bf16[2,96,2048]{2,1,0:T(8,128)(2,1)S(1)}, u32[]{:S(2)}, u32[]{:S(2)}) collective-permute-start(bf16[2,96,2048]{2,1,0:T(8,128)(2,1)} %get-tuple-element.852), channel_id=1, source_target_pairs={{8,0},{9,1},{10,2},{11,3},{12,4},{13,5},{14,6},{15,7},{16,8},{17,9... | collective-permute-start | bytes 2359304 | tf_op jit(solution)/shard_map/ppermute | solution.py:18
  1810.3 71.8 %collective-permute-start.64 = (bf16[2,96,2048]{2,1,0:T(8,128)(2,1)}, bf16[2,96,2048]{2,1,0:T(8,128)(2,1)S(1)}, u32[]{:S(2)}, u32[]{:S(2)}) collective-permute-start(bf16[2,96,2048]{2,1,0:T(8,128)(2,1)} %get-tuple-element.852), channel_id=1, source_target_pairs={{10,0},{11,1},{12,2},{13,3},{14,4},{15,5},{16,6},{17,7},{18,8},{19... | collective-permute-start | bytes 2359304 | tf_op jit(solution)/shard_map/ppermute | solution.py:18
  1811.7 78.7 %collective-permute-start.65 = (bf16[2,96,2048]{2,1,0:T(8,128)(2,1)}, bf16[2,96,2048]{2,1,0:T(8,128)(2,1)S(1)}, u32[]{:S(2)}, u32[]{:S(2)}) collective-permute-start(bf16[2,96,2048]{2,1,0:T(8,128)(2,1)} %get-tuple-element.852), channel_id=1, source_target_pairs={{11,0},{12,1},{13,2},{14,3},{15,4},{16,5},{17,6},{18,7},{19,8},{20... | collective-permute-start | bytes 2359304 | tf_op jit(solution)/shard_map/ppermute | solution.py:18
  1813.1 85.3 %collective-permute-start.77 = (bf16[2,96,2048]{2,1,0:T(8,128)(2,1)}, bf16[2,96,2048]{2,1,0:T(8,128)(2,1)S(1)}, u32[]{:S(2)}, u32[]{:S(2)}) collective-permute-start(bf16[2,96,2048]{2,1,0:T(8,128)(2,1)} %get-tuple-element.851), channel_id=1, source_target_pairs={{1,0},{2,1},{3,2},{4,3},{5,4},{6,5},{7,6},{8,7},{9,8},{10,9},{11,1... | collective-permute-start | bytes 2359304 | tf_op jit(solution)/shard_map/ppermute | solution.py:18
  1890.4 109.9 %collective-permute-start.81 = (bf16[2,96,2048]{2,1,0:T(8,128)(2,1)}, bf16[2,96,2048]{2,1,0:T(8,128)(2,1)S(1)}, u32[]{:S(2)}, u32[]{:S(2)}) collective-permute-start(bf16[2,96,2048]{2,1,0:T(8,128)(2,1)} %get-tuple-element.851), channel_id=1, source_target_pairs={{5,0},{6,1},{7,2},{8,3},{9,4},{10,5},{11,6},{12,7},{13,8},{14,9},{... | collective-permute-start | bytes 2359304 | tf_op jit(solution)/shard_map/ppermute | solution.py:18
  1898.4 137.6 %collective-permute-start.82 = (bf16[2,96,2048]{2,1,0:T(8,128)(2,1)}, bf16[2,96,2048]{2,1,0:T(8,128)(2,1)S(1)}, u32[]{:S(2)}, u32[]{:S(2)}) collective-permute-start(bf16[2,96,2048]{2,1,0:T(8,128)(2,1)} %get-tuple-element.851), channel_id=1, source_target_pairs={{6,0},{7,1},{8,2},{9,3},{10,4},{11,5},{12,6},{13,7},{14,8},{15,9},... | collective-permute-start | bytes 2359304 | tf_op jit(solution)/shard_map/ppermute | solution.py:18
  1900.9 137.3 %collective-permute-start.83 = (bf16[2,96,2048]{2,1,0:T(8,128)(2,1)}, bf16[2,96,2048]{2,1,0:T(8,128)(2,1)S(1)}, u32[]{:S(2)}, u32[]{:S(2)}) collective-permute-start(bf16[2,96,2048]{2,1,0:T(8,128)(2,1)} %get-tuple-element.851), channel_id=1, source_target_pairs={{7,0},{8,1},{9,2},{10,3},{11,4},{12,5},{13,6},{14,7},{15,8},{16,9}... | collective-permute-start | bytes 2359304 | tf_op jit(solution)/shard_map/ppermute | solution.py:18
  1909.0 198.3 %collective-permute-start.84 = (bf16[2,96,2048]{2,1,0:T(8,128)(2,1)}, bf16[2,96,2048]{2,1,0:T(8,128)(2,1)S(1)}, u32[]{:S(2)}, u32[]{:S(2)}) collective-permute-start(bf16[2,96,2048]{2,1,0:T(8,128)(2,1)} %get-tuple-element.851), channel_id=1, source_target_pairs={{8,0},{9,1},{10,2},{11,3},{12,4},{13,5},{14,6},{15,7},{16,8},{17,9... | collective-permute-start | bytes 2359304 | tf_op jit(solution)/shard_map/ppermute | solution.py:18
  1911.6 209.7 %collective-permute-start.85 = (bf16[2,96,2048]{2,1,0:T(8,128)(2,1)}, bf16[2,96,2048]{2,1,0:T(8,128)(2,1)S(1)}, u32[]{:S(2)}, u32[]{:S(2)}) collective-permute-start(bf16[2,96,2048]{2,1,0:T(8,128)(2,1)} %get-tuple-element.851), channel_id=1, source_target_pairs={{9,0},{10,1},{11,2},{12,3},{13,4},{14,5},{15,6},{16,7},{17,8},{18,... | collective-permute-start | bytes 2359304 | tf_op jit(solution)/shard_map/ppermute | solution.py:18
  2000.3 147.1 %collective-permute-start.86 = (bf16[2,96,2048]{2,1,0:T(8,128)(2,1)}, bf16[2,96,2048]{2,1,0:T(8,128)(2,1)S(1)}, u32[]{:S(2)}, u32[]{:S(2)}) collective-permute-start(bf16[2,96,2048]{2,1,0:T(8,128)(2,1)} %get-tuple-element.851), channel_id=1, source_target_pairs={{10,0},{11,1},{12,2},{13,3},{14,4},{15,5},{16,6},{17,7},{18,8},{19... | collective-permute-start | bytes 2359304 | tf_op jit(solution)/shard_map/ppermute | solution.py:18
  2036.0 120.4 %collective-permute-start.87 = (bf16[2,96,2048]{2,1,0:T(8,128)(2,1)}, bf16[2,96,2048]{2,1,0:T(8,128)(2,1)S(1)}, u32[]{:S(2)}, u32[]{:S(2)}) collective-permute-start(bf16[2,96,2048]{2,1,0:T(8,128)(2,1)} %get-tuple-element.851), channel_id=1, source_target_pairs={{11,0},{12,1},{13,2},{14,3},{15,4},{16,5},{17,6},{18,7},{19,8},{20... | collective-permute-start | bytes 2359304 | tf_op jit(solution)/shard_map/ppermute | solution.py:18
  2546.5 1411.0 %reduce-scatter.5.cloned.1.call-start = ((), (), s32[]{:S(2)}) async-start(), calls=%async_computation.8 | async-start | bytes 51904512 | tf_op jit(solution)/shard_map/reduce_scatter | solution.py:390
  2730.8 88.9 %collective-permute-start.131 = (bf16[2,96,2048]{2,1,0:T(8,128)(2,1)S(1)}, bf16[2,96,2048]{2,1,0:T(8,128)(2,1)}, u32[]{:S(2)}, u32[]{:S(2)}) collective-permute-start(bf16[2,96,2048]{2,1,0:T(8,128)(2,1)S(1)} %get-tuple-element.819), channel_id=1, source_target_pairs={{0,11},{1,12},{2,13},{3,14},{4,15},{5,16},{6,17},{7,18},{8,19},{9,... | collective-permute-start | bytes 2359304 | tf_op jit(solution)/shard_map/ppermute | solution.py:18
  2733.4 104.2 %collective-permute-start.130 = (bf16[2,96,2048]{2,1,0:T(8,128)(2,1)S(1)}, bf16[2,96,2048]{2,1,0:T(8,128)(2,1)}, u32[]{:S(2)}, u32[]{:S(2)}) collective-permute-start(bf16[2,96,2048]{2,1,0:T(8,128)(2,1)S(1)} %get-tuple-element.820), channel_id=1, source_target_pairs={{0,10},{1,11},{2,12},{3,13},{4,14},{5,15},{6,16},{7,17},{8,18},{9,... | collective-permute-start | bytes 2359304 | tf_op jit(solution)/shard_map/ppermute | solution.py:18
  2735.6 108.9 %collective-permute-start.129 = (bf16[2,96,2048]{2,1,0:T(8,128)(2,1)S(1)}, bf16[2,96,2048]{2,1,0:T(8,128)(2,1)}, u32[]{:S(2)}, u32[]{:S(2)}) collective-permute-start(bf16[2,96,2048]{2,1,0:T(8,128)(2,1)S(1)} %get-tuple-element.821), channel_id=1, source_target_pairs={{0,9},{1,10},{2,11},{3,12},{4,13},{5,14},{6,15},{7,16},{8,17},{9,1... | collective-permute-start | bytes 2359304 | tf_op jit(solution)/shard_map/ppermute | solution.py:18
  2765.5 81.1 %collective-permute-start.128 = (bf16[2,96,2048]{2,1,0:T(8,128)(2,1)S(1)}, bf16[2,96,2048]{2,1,0:T(8,128)(2,1)}, u32[]{:S(2)}, u32[]{:S(2)}) collective-permute-start(bf16[2,96,2048]{2,1,0:T(8,128)(2,1)S(1)} %get-tuple-element.822), channel_id=1, source_target_pairs={{0,8},{1,9},{2,10},{3,11},{4,12},{5,13},{6,14},{7,15},{8,16},{9,17... | collective-permute-start | bytes 2359304 | tf_op jit(solution)/shard_map/ppermute | solution.py:18
  2815.2 86.8 %collective-permute-start.127 = (bf16[2,96,2048]{2,1,0:T(8,128)(2,1)}, bf16[2,96,2048]{2,1,0:T(8,128)(2,1)S(1)}, u32[]{:S(2)}, u32[]{:S(2)}) collective-permute-start(bf16[2,96,2048]{2,1,0:T(8,128)(2,1)} %get-tuple-element.823), channel_id=1, source_target_pairs={{0,7},{1,8},{2,9},{3,10},{4,11},{5,12},{6,13},{7,14},{8,15},{9,16}... | collective-permute-start | bytes 2359304 | tf_op jit(solution)/shard_map/ppermute | solution.py:18
  2819.7 102.0 %collective-permute-start.126 = (bf16[2,96,2048]{2,1,0:T(8,128)(2,1)}, bf16[2,96,2048]{2,1,0:T(8,128)(2,1)S(1)}, u32[]{:S(2)}, u32[]{:S(2)}) collective-permute-start(bf16[2,96,2048]{2,1,0:T(8,128)(2,1)} %get-tuple-element.824), channel_id=1, source_target_pairs={{0,6},{1,7},{2,8},{3,9},{4,10},{5,11},{6,12},{7,13},{8,14},{9,15},... | collective-permute-start | bytes 2359304 | tf_op jit(solution)/shard_map/ppermute | solution.py:18
  2837.6 99.8 %collective-permute-start.125 = (bf16[2,96,2048]{2,1,0:T(8,128)(2,1)}, bf16[2,96,2048]{2,1,0:T(8,128)(2,1)S(1)}, u32[]{:S(2)}, u32[]{:S(2)}) collective-permute-start(bf16[2,96,2048]{2,1,0:T(8,128)(2,1)} %get-tuple-element.825), channel_id=1, source_target_pairs={{0,5},{1,6},{2,7},{3,8},{4,9},{5,10},{6,11},{7,12},{8,13},{9,14},{... | collective-permute-start | bytes 2359304 | tf_op jit(solution)/shard_map/ppermute | solution.py:18
  2844.4 94.3 %collective-permute-start.124 = (bf16[2,96,2048]{2,1,0:T(8,128)(2,1)}, bf16[2,96,2048]{2,1,0:T(8,128)(2,1)}, u32[]{:S(2)}, u32[]{:S(2)}) collective-permute-start(bf16[2,96,2048]{2,1,0:T(8,128)(2,1)} %get-tuple-element.826), channel_id=1, source_target_pairs={{0,4},{1,5},{2,6},{3,7},{4,8},{5,9},{6,10},{7,11},{8,12},{9,13},{1... | collective-permute-start | bytes 2359304 | tf_op jit(solution)/shard_map/ppermute | solution.py:18
  2846.6 93.4 %collective-permute-start.123 = (bf16[2,96,2048]{2,1,0:T(8,128)(2,1)}, bf16[2,96,2048]{2,1,0:T(8,128)(2,1)}, u32[]{:S(2)}, u32[]{:S(2)}) collective-permute-start(bf16[2,96,2048]{2,1,0:T(8,128)(2,1)} %get-tuple-element.827), channel_id=1, source_target_pairs={{0,3},{1,4},{2,5},{3,6},{4,7},{5,8},{6,9},{7,10},{8,11},{9,12},{10... | collective-permute-start | bytes 2359304 | tf_op jit(solution)/shard_map/ppermute | solution.py:18
  2960.9 76.9 %collective-permute-start.115 = (bf16[2,96,2048]{2,1,0:T(8,128)(2,1)}, bf16[2,96,2048]{2,1,0:T(8,128)(2,1)S(1)}, u32[]{:S(2)}, u32[]{:S(2)}) collective-permute-start(bf16[2,96,2048]{2,1,0:T(8,128)(2,1)} %get-tuple-element.835), channel_id=1, source_target_pairs={{6,0},{7,1},{8,2},{9,3},{10,4},{11,5},{12,6},{13,7},{14,8},{15,9},... | collective-permute-start | bytes 2359304 | tf_op jit(solution)/shard_map/ppermute | solution.py:18
  2988.1 111.4 %collective-permute-start.113 = (bf16[2,96,2048]{2,1,0:T(8,128)(2,1)S(1)}, bf16[2,96,2048]{2,1,0:T(8,128)(2,1)}, u32[]{:S(2)}, u32[]{:S(2)}) collective-permute-start(bf16[2,96,2048]{2,1,0:T(8,128)(2,1)S(1)} %get-tuple-element.838), channel_id=1, source_target_pairs={{8,0},{9,1},{10,2},{11,3},{12,4},{13,5},{14,6},{15,7},{16,8},{17,9... | collective-permute-start | bytes 2359304 | tf_op jit(solution)/shard_map/ppermute | solution.py:18
  2994.9 122.0 %collective-permute-start.112 = (bf16[2,96,2048]{2,1,0:T(8,128)(2,1)S(1)}, bf16[2,96,2048]{2,1,0:T(8,128)(2,1)S(1)}, u32[]{:S(2)}, u32[]{:S(2)}) collective-permute-start(bf16[2,96,2048]{2,1,0:T(8,128)(2,1)S(1)} %get-tuple-element.839), channel_id=1, source_target_pairs={{9,0},{10,1},{11,2},{12,3},{13,4},{14,5},{15,6},{16,7},{17,8},{18,... | collective-permute-start | bytes 2359304 | tf_op jit(solution)/shard_map/ppermute | solution.py:18
  2996.2 152.2 %collective-permute-start.111 = (bf16[2,96,2048]{2,1,0:T(8,128)(2,1)S(1)}, bf16[2,96,2048]{2,1,0:T(8,128)(2,1)S(1)}, u32[]{:S(2)}, u32[]{:S(2)}) collective-permute-start(bf16[2,96,2048]{2,1,0:T(8,128)(2,1)S(1)} %get-tuple-element.837), channel_id=1, source_target_pairs={{10,0},{11,1},{12,2},{13,3},{14,4},{15,5},{16,6},{17,7},{18,8},{19... | collective-permute-start | bytes 2359304 | tf_op jit(solution)/shard_map/ppermute | solution.py:18
  3037.8 128.0 %collective-permute-start.110 = (bf16[2,96,2048]{2,1,0:T(8,128)(2,1)}, bf16[2,96,2048]{2,1,0:T(8,128)(2,1)S(1)}, u32[]{:S(2)}, u32[]{:S(2)}) collective-permute-start(bf16[2,96,2048]{2,1,0:T(8,128)(2,1)} %get-tuple-element.818), channel_id=1, source_target_pairs={{11,0},{12,1},{13,2},{14,3},{15,4},{16,5},{17,6},{18,7},{19,8},{20... | collective-permute-start | bytes 2359304 | tf_op jit(solution)/shard_map/ppermute | solution.py:18
  3039.1 149.7 %collective-permute-start.109 = (bf16[2,96,2048]{2,1,0:T(8,128)(2,1)}, bf16[2,96,2048]{2,1,0:T(8,128)(2,1)S(1)}, u32[]{:S(2)}, u32[]{:S(2)}) collective-permute-start(bf16[2,96,2048]{2,1,0:T(8,128)(2,1)} %get-tuple-element.797), channel_id=1, source_target_pairs={{0,11},{1,12},{2,13},{3,14},{4,15},{5,16},{6,17},{7,18},{8,19},{9,... | collective-permute-start | bytes 2359304 | tf_op jit(solution)/shard_map/ppermute | solution.py:18
  3099.5 105.3 %collective-permute-start.108 = (bf16[2,96,2048]{2,1,0:T(8,128)(2,1)}, bf16[2,96,2048]{2,1,0:T(8,128)(2,1)S(1)}, u32[]{:S(2)}, u32[]{:S(2)}) collective-permute-start(bf16[2,96,2048]{2,1,0:T(8,128)(2,1)} %get-tuple-element.798), channel_id=1, source_target_pairs={{0,10},{1,11},{2,12},{3,13},{4,14},{5,15},{6,16},{7,17},{8,18},{9,... | collective-permute-start | bytes 2359304 | tf_op jit(solution)/shard_map/ppermute | solution.py:18
  3116.9 89.2 %collective-permute-start.107 = (bf16[2,96,2048]{2,1,0:T(8,128)(2,1)}, bf16[2,96,2048]{2,1,0:T(8,128)(2,1)S(1)}, u32[]{:S(2)}, u32[]{:S(2)}) collective-permute-start(bf16[2,96,2048]{2,1,0:T(8,128)(2,1)} %get-tuple-element.799), channel_id=1, source_target_pairs={{0,9},{1,10},{2,11},{3,12},{4,13},{5,14},{6,15},{7,16},{8,17},{9,1... | collective-permute-start | bytes 2359304 | tf_op jit(solution)/shard_map/ppermute | solution.py:18
  3276.7 71.8 %collective-permute-start.94 = (bf16[2,96,2048]{2,1,0:T(8,128)(2,1)}, bf16[2,96,2048]{2,1,0:T(8,128)(2,1)}, u32[]{:S(2)}, u32[]{:S(2)}) collective-permute-start(bf16[2,96,2048]{2,1,0:T(8,128)(2,1)} %get-tuple-element.812), channel_id=1, source_target_pairs={{5,0},{6,1},{7,2},{8,3},{9,4},{10,5},{11,6},{12,7},{13,8},{14,9},{... | collective-permute-start | bytes 2359304 | tf_op jit(solution)/shard_map/ppermute | solution.py:18
  3278.0 71.7 %collective-permute-start.93 = (bf16[2,96,2048]{2,1,0:T(8,128)(2,1)}, bf16[2,96,2048]{2,1,0:T(8,128)(2,1)}, u32[]{:S(2)}, u32[]{:S(2)}) collective-permute-start(bf16[2,96,2048]{2,1,0:T(8,128)(2,1)} %get-tuple-element.813), channel_id=1, source_target_pairs={{6,0},{7,1},{8,2},{9,3},{10,4},{11,5},{12,6},{13,7},{14,8},{15,9},... | collective-permute-start | bytes 2359304 | tf_op jit(solution)/shard_map/ppermute | solution.py:18
  3295.9 102.6 %collective-permute-start.91 = (bf16[2,96,2048]{2,1,0:T(8,128)(2,1)}, bf16[2,96,2048]{2,1,0:T(8,128)(2,1)}, u32[]{:S(2)}, u32[]{:S(2)}) collective-permute-start(bf16[2,96,2048]{2,1,0:T(8,128)(2,1)} %get-tuple-element.816), channel_id=1, source_target_pairs={{8,0},{9,1},{10,2},{11,3},{12,4},{13,5},{14,6},{15,7},{16,8},{17,9... | collective-permute-start | bytes 2359304 | tf_op jit(solution)/shard_map/ppermute | solution.py:18
  3312.4 91.9 %collective-permute-start.90 = (bf16[2,96,2048]{2,1,0:T(8,128)(2,1)}, bf16[2,96,2048]{2,1,0:T(8,128)(2,1)}, u32[]{:S(2)}, u32[]{:S(2)}) collective-permute-start(bf16[2,96,2048]{2,1,0:T(8,128)(2,1)} %get-tuple-element.817), channel_id=1, source_target_pairs={{9,0},{10,1},{11,2},{12,3},{13,4},{14,5},{15,6},{16,7},{17,8},{18,... | collective-permute-start | bytes 2359304 | tf_op jit(solution)/shard_map/ppermute | solution.py:18
  3348.4 84.1 %collective-permute-start.89 = (bf16[2,96,2048]{2,1,0:T(8,128)(2,1)}, bf16[2,96,2048]{2,1,0:T(8,128)(2,1)}, u32[]{:S(2)}, u32[]{:S(2)}) collective-permute-start(bf16[2,96,2048]{2,1,0:T(8,128)(2,1)} %get-tuple-element.815), channel_id=1, source_target_pairs={{10,0},{11,1},{12,2},{13,3},{14,4},{15,5},{16,6},{17,7},{18,8},{19... | collective-permute-start | bytes 2359304 | tf_op jit(solution)/shard_map/ppermute | solution.py:18
  3349.8 89.4 %collective-permute-start.88 = (bf16[2,96,2048]{2,1,0:T(8,128)(2,1)}, bf16[2,96,2048]{2,1,0:T(8,128)(2,1)}, u32[]{:S(2)}, u32[]{:S(2)}) collective-permute-start(bf16[2,96,2048]{2,1,0:T(8,128)(2,1)} %get-tuple-element.796), channel_id=1, source_target_pairs={{11,0},{12,1},{13,2},{14,3},{15,4},{16,5},{17,6},{18,7},{19,8},{20... | collective-permute-start | bytes 2359304 | tf_op jit(solution)/shard_map/ppermute | solution.py:18
  3469.2 932.1 %reduce-scatter.11.cloned.1.call-start = ((), (), s32[]{:S(2)}) async-start(), calls=%async_computation.11 | async-start | bytes 43253760 | tf_op jit(solution)/shard_map/reduce_scatter | solution.py:69
  3487.1 1802.0 %reduce-scatter.9.cloned.1.call-start = ((), (), s32[]{:S(2)}) async-start(), calls=%async_computation.10 | async-start | bytes 86507520 | tf_op jit(solution)/shard_map/reduce_scatter | solution.py:68
  (164 other events, 16235.6 us)
Sparse Core Ops, SparseCore 0:
  10.9 157.3 all-gather.4
  171.1 75.6 all-gather.6
  249.6 233.7 all-gather.8
  486.2 132.6 all-gather.10
  2546.6 428.8 reduce-scatter.6
  3469.3 488.1 reduce-scatter.4
  3960.4 440.8 reduce-scatter.10
  4404.2 884.8 reduce-scatter.8
where the time goes:
time: 5320 us; the launch traced here: 5300 us
  waiting for transfers between devices  2260 us (42%)
  local copies, waits for them, and re-layouts  1440 us (27%)
  starting transfers between devices  800 us (15%)
  matrix products  522 us (10%)
  blocking collectives  153 us (3%)
  other arithmetic  106 us (2%)
    gather x2, local copies, waits for them, and re-layouts, pair_layout(): bucket = jnp.take(bucket_table, offset)  1170 us
    reduce_scatter x1, waiting for transfers between devices, scatter_feed(): lax.psum_scatter(parts[1], 'dev', scatter_dimension=0, tiled=True)  888 us
    ppermute x132, starting transfers between devices, shifted(): return lax.ppermute(block, axis, route)  800 us
    ppermute x132, waiting for transfers between devices, shifted(): return lax.ppermute(block, axis, route)  690 us
    reduce_scatter x1, waiting for transfers between devices, scatter_feed(): lax.psum_scatter(parts[2], 'dev', scatter_dimension=0, tiled=True)  444 us
    reduce_scatter x1, waiting for transfers between devices, local(): lax.psum_scatter(attention_parts[1], 'dev', scatter_dimension=0, tiled=True)  235 us
    unnamed x2, blocking collectives  153 us
  transfers between devices with their start and end apart: 140, of which 47 were waited for; matrix products, arithmetic and copies ran while one was open for 35% of the time, Pallas kernels for 0%

commit v1 on v0

v1 whole, which is shorter than its diff:
```python
import jax
import jax.numpy as jnp
from jax import lax
from jax.experimental import pallas as pl
from jax.experimental.pallas import tpu as pltpu
from jax.sharding import Mesh, PartitionSpec as P

EPS = 1e-06
AXES = ("b", "h", "p", "q", "r", "c")
CUBE = ("p", "q", "r")
SWAP = [(0, 1), (1, 0)]
LOW = jnp.bfloat16
F32 = jnp.float32
HEAD_DIM = 64
BUCKETS = 32
WINDOW = 1024
BLK = 256
FAR = float(2**30)
NT = (((1,), (1,)), ((), ()))
NN = (((1,), (0,)), ((), ()))
DIAGS = 2 * (WINDOW // BLK) + 1
MID = WINDOW // BLK


def dot(a, b, dims=NN):
    return lax.dot_general(a, b, dims, preferred_element_type=jnp.float32)


def fill_rows(table, own, other, rows, targets):
    pieces = own.shape[0] // rows
    for side, src in enumerate((own, other)):
        for i in range(pieces):
            at = pl.multiple_of(table[side * pieces + i], rows)
            col = 0
            for dst in targets:
                wide = dst.shape[-1]
                dst[pl.ds(at, rows), :] = src[i * rows : (i + 1) * rows, col : col + wide]
                col += wide


def drain_rows(table, src, own, other, rows, col):
    pieces = own.shape[0] // rows
    wide = src.shape[-1]
    for side, dst in enumerate((own, other)):
        for i in range(pieces):
            at = pl.multiple_of(table[side * pieces + i], rows)
            dst[i * rows : (i + 1) * rows, col : col + wide] = src[pl.ds(at, rows), :]


def make_tiles(diag_ref, tiles):
    for n in range(2):
        for d in range(DIAGS):
            line = diag_ref[n * DIAGS + d : n * DIAGS + d + 1, :]
            wide = jnp.broadcast_to(line, (BLK, 2 * BLK))
            skew = pltpu.roll(wide, 0, 1, stride=1, stride_axis=0)
            tiles[n * (DIAGS + 1) + d] = skew[:, BLK:]


def make_own_tile(pad_ref, tiles, at):
    rows = lax.broadcasted_iota(jnp.int32, (BLK, BLK), 0)
    cols = lax.broadcasted_iota(jnp.int32, (BLK, BLK), 1)
    gone = jnp.where(rows == cols, 0.0, pad_ref[pl.ds(at, BLK), :])
    for n in range(2):
        tiles[n * (DIAGS + 1) + DIAGS] = tiles[n * (DIAGS + 1) + MID] + gone


def build_pairs(q, k, qa_ref, ka_ref, qx, kx):
    def fill_q(i, _):
        rows = pl.ds(pl.multiple_of(i * BLK, BLK), BLK)
        for n in range(2):
            part = q[rows, n * HEAD_DIM : (n + 1) * HEAD_DIM]
            qx[2 * n, rows, :] = jnp.concatenate([part, qa_ref[rows, :HEAD_DIM]], axis=1)
            qx[2 * n + 1, rows, :] = jnp.concatenate([part, qa_ref[rows, HEAD_DIM:]], axis=1)
        return 0

    def fill_k(i, _):
        rows = pl.ds(pl.multiple_of(i * BLK, BLK), BLK)
        for n in range(2):
            part = k[rows, n * HEAD_DIM : (n + 1) * HEAD_DIM]
            kx[n, rows, :] = jnp.concatenate([part, ka_ref[rows, :]], axis=1)
        return 0

    lax.fori_loop(0, q.shape[0] // BLK, fill_q, 0)
    lax.fori_loop(0, k.shape[0] // BLK, fill_k, 0)


def forward_kernel(local, halo, *refs):
    if local:
        (pos, pos_out, rng, own, other, qa, ka, pad, diag, out_own, out_other, mixed_t, lse,
         q, k, v, qx, kx, vt, tiles, joined) = refs
        fill_rows(pos, own, other, own.shape[0] // 48, (q, k, v))
    else:
        (rng, q, k, v, qa, ka, pad, diag, joined, mixed_t, lse, qx, kx, vt, tiles) = refs
    make_tiles(diag, tiles)
    build_pairs(q, k, qa, ka, qx, kx)

    def turn(i, _):
        rows = pl.ds(pl.multiple_of(i * BLK, BLK), BLK)
        vt[:, rows] = v[rows, :].T
        return 0

    lax.fori_loop(0, v.shape[0] // BLK, turn, 0)

    def query_block(i, _):
        at = pl.multiple_of(i * BLK, BLK)
        here = i + halo // BLK
        make_own_tile(pad, tiles, pl.multiple_of(here * BLK, BLK))

        def key_block(j, carry):
            span = pl.ds(pl.multiple_of(j * BLK, BLK), BLK)
            same = (j == here).astype(jnp.int32)
            slot = jnp.where(j == here, DIAGS, j - here + MID)
            out = []
            for n in range(2):
                top, total, acc = carry[n]
                s = dot(kx[n, span, :], qx[2 * n + 1 - same, pl.ds(at, BLK), :], NT)
                s = s + tiles[n * (DIAGS + 1) + slot]
                high = jnp.maximum(top, jnp.max(s, axis=0, keepdims=True))
                p = jnp.exp(s - high)
                shrink = jnp.exp(top - high)
                total = total * shrink + jnp.sum(p, axis=0, keepdims=True)
                acc = acc * shrink + dot(
                    vt[n * HEAD_DIM : (n + 1) * HEAD_DIM, span], p.astype(jnp.bfloat16)
                )
                out.append((high, total, acc))
            return tuple(out)

        start = (
            jnp.full((1, BLK), -1e30, jnp.float32),
            jnp.zeros((1, BLK), jnp.float32),
            jnp.zeros((HEAD_DIM, BLK), jnp.float32),
        )
        done = lax.fori_loop(rng[0, i], rng[1, i], key_block, (start, start))
        for n in range(2):
            top, total, acc = done[n]
            mixed_t[n * HEAD_DIM : (n + 1) * HEAD_DIM, pl.ds(at, BLK)] = acc / total
            lse[n : n + 1, pl.ds(at, BLK)] = top + jnp.log(total)
        joined[pl.ds(at, BLK), :] = mixed_t[:, pl.ds(at, BLK)].T.astype(jnp.bfloat16)
        return 0

    lax.fori_loop(0, q.shape[0] // BLK, query_block, 0)
    if local:
        drain_rows(pos_out, joined, out_own, out_other, out_own.shape[0] // 16, 0)


def backward_kernel(local, halo, *refs):
    if local:
        (pos, pos_out, rng, own, other, qa, ka, pad, diag, g_own, g_other, mixed_t, lse,
         dqkv_own, dqkv_other, d_diag,
         q, k, v, g, dq, dk_low, dv_low, qx, kx, vx, gx, kt, tiles, dk, dv, dtiles) = refs
        fill_rows(pos, own, other, own.shape[0] // 48, (q, k, v))
        fill_rows(pos_out, g_own, g_other, g_own.shape[0] // 16, (g,))
    else:
        (rng, q, k, v, qa, ka, pad, diag, g, mixed_t, lse,
         dq, dk_out, dv_out, d_diag, qx, kx, vx, gx, kt, tiles, dk, dv, dtiles) = refs
    make_tiles(diag, tiles)
    build_pairs(q, k, qa, ka, qx, kx)
    blank = jnp.zeros((BLK, HEAD_DIM), jnp.bfloat16)

    def turn(i, _):
        rows = pl.ds(pl.multiple_of(i * BLK, BLK), BLK)
        kt[:, rows] = k[rows, :].T
        for n in range(2):
            part = v[rows, n * HEAD_DIM : (n + 1) * HEAD_DIM]
            vx[n, rows, :] = jnp.concatenate([part, blank], axis=1)
            dk[n, rows, :] = jnp.zeros((BLK, 2 * HEAD_DIM), jnp.float32)
            dv[n, rows, :] = jnp.zeros((BLK, 2 * HEAD_DIM), jnp.float32)
        return 0

    def spread(i, _):
        rows = pl.ds(pl.multiple_of(i * BLK, BLK), BLK)
        for n in range(2):
            part = g[rows, n * HEAD_DIM : (n + 1) * HEAD_DIM]
            gx[n, rows, :] = jnp.concatenate([part, blank], axis=1)
        return 0

    lax.fori_loop(0, k.shape[0] // BLK, turn, 0)
    lax.fori_loop(0, q.shape[0] // BLK, spread, 0)
    for slot in range(2 * DIAGS):
        dtiles[slot] = jnp.zeros((BLK, BLK), jnp.float32)

    def query_block(i, _):
        at = pl.multiple_of(i * BLK, BLK)
        rows = pl.ds(at, BLK)
        here = i + halo // BLK
        make_own_tile(pad, tiles, pl.multiple_of(here * BLK, BLK))
        turned = g[rows, :].astype(jnp.float32).T * mixed_t[:, rows]
        delta = [
            jnp.sum(turned[n * HEAD_DIM : (n + 1) * HEAD_DIM], axis=0, keepdims=True)
            for n in range(2)
        ]
        level = [lse[n : n + 1, rows] for n in range(2)]

        def key_block(j, carry):
            span = pl.ds(pl.multiple_of(j * BLK, BLK), BLK)
            same = (j == here).astype(jnp.int32)
            away = j - here + MID
            slot = jnp.where(j == here, DIAGS, away)
            out = []
            for n in range(2):
                variant = 2 * n + 1 - same
                s = dot(kx[n, span, :], qx[variant, rows, :], NT)
                p = jnp.exp(s + tiles[n * (DIAGS + 1) + slot] - level[n])
                dp = dot(vx[n, span, :], gx[n, rows, :], NT)
                ds = (p * (dp - delta[n])).astype(jnp.bfloat16)
                dtiles[n * DIAGS + away] += ds.astype(jnp.float32)
                dv[n, span, :] += dot(p.astype(jnp.bfloat16), gx[n, rows, :])
                dk[n, span, :] += dot(ds, qx[variant, rows, :])
                out.append(
                    carry[n] + dot(kt[n * HEAD_DIM : (n + 1) * HEAD_DIM, span], ds)
                )
            return tuple(out)

        zero = jnp.zeros((HEAD_DIM, BLK), jnp.float32)
        done = lax.fori_loop(rng[0, i], rng[1, i], key_block, (zero, zero))
        joined = jnp.concatenate(done, axis=0).T
        dq[rows, :] = joined.astype(dq.dtype)
        return 0

    lax.fori_loop(0, q.shape[0] // BLK, query_block, 0)

    flip = (
        lax.broadcasted_iota(jnp.int32, (BLK, BLK), 0)
        + lax.broadcasted_iota(jnp.int32, (BLK, BLK), 1)
        == BLK - 1
    ).astype(jnp.float32)
    nothing = jnp.zeros((BLK, BLK), jnp.float32)
    for slot in range(2 * DIAGS):
        turned = lax.dot_general(
            flip, dtiles[slot], NN, precision=lax.Precision.HIGHEST,
            preferred_element_type=jnp.float32,
        )
        wide = jnp.concatenate([nothing, turned], axis=1)
        skew = pltpu.roll(wide, BLK + 1, 1, stride=1, stride_axis=0)
        d_diag[slot : slot + 1, :] = jnp.sum(skew, axis=0, keepdims=True)

    def finish(i, _):
        rows = pl.ds(pl.multiple_of(i * BLK, BLK), BLK)
        both_k = jnp.concatenate([dk[n, rows, :HEAD_DIM] for n in range(2)], axis=1)
        both_v = jnp.concatenate([dv[n, rows, :HEAD_DIM] for n in range(2)], axis=1)
        if local:
            dk_low[rows, :] = both_k.astype(jnp.bfloat16)
            dv_low[rows, :] = both_v.astype(jnp.bfloat16)
        else:
            dk_out[rows, :] = both_k
            dv_out[rows, :] = both_v
        return 0

    lax.fori_loop(0, k.shape[0] // BLK, finish, 0)
    if local:
        rows = own.shape[0] // 48
        for col, src in enumerate((dq, dk_low, dv_low)):
            drain_rows(pos, src, dqkv_own, dqkv_other, rows, col * 2 * HEAD_DIM)


def specs(smem, vmem):
    return [pl.BlockSpec(memory_space=pltpu.SMEM)] * smem + [pl.BlockSpec(memory_space=pltpu.VMEM)] * vmem


def common_scratch(length, reach):
    return [
        pltpu.VMEM((4, length, 128), jnp.bfloat16),
        pltpu.VMEM((2, reach, 128), jnp.bfloat16),
    ]


def costs(length, times):
    pairs = 2 * length * 1400
    return pl.CostEstimate(flops=pairs * 256 * times, bytes_accessed=8 << 20, transcendentals=pairs)


def attend_forward(local, halo, tables, tokens, extras):
    length = extras[0].shape[0]
    reach = extras[1].shape[0]
    both = 2 * HEAD_DIM
    shape = jax.ShapeDtypeStruct
    saved = [shape((both, length), jnp.float32), shape((2, length), jnp.float32)]
    tiles = pltpu.VMEM((2 * (DIAGS + 1), BLK, BLK), jnp.float32)
    low = jnp.bfloat16
    if local:
        outs = [shape((length // 2, both), low)] * 2 + saved
        scratch = [pltpu.VMEM((length, both), low)] + [pltpu.VMEM((reach, both), low)] * 2
    else:
        outs = [shape((length, both), low)] + saved
        scratch = []
    scratch += common_scratch(length, reach) + [pltpu.VMEM((both, reach), low), tiles]
    if local:
        scratch += [pltpu.VMEM((length, both), low)]
    return pl.pallas_call(
        lambda *refs: forward_kernel(local, halo, *refs),
        out_shape=outs,
        in_specs=specs(len(tables), len(tokens) + len(extras)),
        out_specs=specs(0, len(outs)),
        scratch_shapes=scratch,
        compiler_params=pltpu.CompilerParams(vmem_limit_bytes=56 << 20),
        cost_estimate=costs(length, 2),
    )(*tables, *tokens, *extras)


def attend_backward(local, halo, tables, tokens, extras, grads, saved):
    length = extras[0].shape[0]
    reach = extras[1].shape[0]
    both = 2 * HEAD_DIM
    shape = jax.ShapeDtypeStruct
    low = jnp.bfloat16
    d_diag = shape((2 * DIAGS, 2 * BLK), jnp.float32)
    if local:
        outs = [shape((length // 2, 3 * both), low)] * 2 + [d_diag]
        scratch = [pltpu.VMEM((length, both), low), pltpu.VMEM((reach, both), low), pltpu.VMEM((reach, both), low),
                   pltpu.VMEM((length, both), low), pltpu.VMEM((length, both), low), pltpu.VMEM((reach, both), low),
                   pltpu.VMEM((reach, both), low)]
    else:
        outs = [shape((length, both), jnp.float32)] + [shape((reach, both), jnp.float32)] * 2 + [d_diag]
        scratch = []
    scratch += common_scratch(length, reach) + [
        pltpu.VMEM((2, reach, both), low),
        pltpu.VMEM((2, length, both), low),
        pltpu.VMEM((both, reach), low),
        pltpu.VMEM((2 * (DIAGS + 1), BLK, BLK), jnp.float32),
        pltpu.VMEM((2, reach, both), jnp.float32),
        pltpu.VMEM((2, reach, both), jnp.float32),
        pltpu.VMEM((2 * DIAGS, BLK, BLK), jnp.float32),
    ]
    return pl.pallas_call(
        lambda *refs: backward_kernel(local, halo, *refs),
        out_shape=outs,
        in_specs=specs(len(tables), len(tokens) + len(extras) + len(grads) + len(saved)),
        out_specs=specs(0, len(outs)),
        scratch_shapes=scratch,
        compiler_params=pltpu.CompilerParams(vmem_limit_bytes=60 << 20),
        cost_estimate=costs(length, 5),
    )(*tables, *tokens, *extras, *grads, *saved)


def skewed_bias(bias):
    edge = jnp.full((2, 2 * BLK), -FAR, jnp.float32)
    wide = jnp.concatenate([edge, bias, edge], axis=1)
    lines = []
    for n in range(2):
        for d in range(DIAGS):
            first = BLK * (d - MID + 1) - (2 * BLK - 1) + WINDOW - 1 + 2 * BLK
            lines.append(wide[n, first : first + 2 * BLK][::-1])
    return jnp.stack(lines)


def unskew(d_diag):
    total = jnp.zeros((2, 2 * WINDOW - 1 + 4 * BLK), jnp.float32)
    for n in range(2):
        for d in range(DIAGS):
            first = BLK * (d - MID + 1) - (2 * BLK - 1) + WINDOW - 1 + 2 * BLK
            total = total.at[n, first : first + 2 * BLK].add(d_diag[n * DIAGS + d][::-1])
    return total[:, 2 * BLK : 2 * BLK + 2 * WINDOW - 1]


def pair_extras(segments, padding, halo, count):
    reach = segments.shape[0]
    length = reach - 2 * halo
    names = jnp.arange(16, dtype=jnp.int32)
    key_hot = segments[:, None] == names
    query_hot = key_hot[halo : halo + length]
    barred = jnp.where(query_hot, 0.0, -FAR).astype(jnp.bfloat16)
    one = jnp.ones((length, 1), jnp.bfloat16)
    rest = jnp.zeros((length, HEAD_DIM - 17), jnp.bfloat16)
    qa = jnp.concatenate([barred, 0 * one, rest, barred, one, rest], axis=1)
    gone = jnp.where(padding == 1, 0.0, -FAR)[:, None]
    ka = jnp.concatenate(
        [key_hot.astype(jnp.bfloat16), gone.astype(jnp.bfloat16), jnp.zeros((reach, HEAD_DIM - 17), jnp.bfloat16)],
        axis=1,
    )

    blocks = length // BLK
    first = halo + BLK * jnp.arange(blocks, dtype=jnp.int32)
    last = first + BLK - 1
    low = jnp.sum(segments[None, :] < segments[first][:, None], axis=1)
    high = jnp.sum(segments[None, :] <= segments[last][:, None], axis=1)
    low = jnp.maximum(low, jnp.maximum(first - WINDOW + 1, 0))
    high = jnp.minimum(high, jnp.minimum(last + WINDOW, reach))
    rng = jnp.stack([low // BLK, (high + BLK - 1) // BLK]).astype(jnp.int32)
    return rng, (qa, ka, gone)


def swap(value, axis):
    return lax.ppermute(value, axis, SWAP)


def pick(value, index, axis=0):
    return lax.dynamic_index_in_dim(value, index, axis, keepdims=False)


def both(mine, theirs, bit, axis, joined=False):
    put = jnp.concatenate if joined else jnp.stack
    return jnp.where(bit == 0, put([mine, theirs], axis), put([theirs, mine], axis))


def matmul(left, right, dims=NN):
    return lax.dot_general(left, right, dims, preferred_element_type=F32)


TN = (((0,), (0,)), ((), ()))


def spread(rows):
    third = rows.shape[0] // 3
    parts = [rows[k * third : (k + 1) * third][None] for k in range(3)]
    for step in range(3):
        got = [swap(parts[k], CUBE[(k + step) % 3]) for k in range(3)]
        parts = [jnp.concatenate([a, b], axis=0) for a, b in zip(parts, got)]
    return jnp.concatenate([part.reshape(-1, rows.shape[1]) for part in parts], axis=0)


def collect(rows):
    width = rows.shape[1]
    parts = list(rows.astype(LOW).reshape(3, 8, -1, width))
    for step in (2, 1, 0):
        half = parts[0].shape[0] // 2
        got = [swap(parts[k][half:], CUBE[(k + step) % 3]) for k in range(3)]
        parts = [(a[:half].astype(F32) + b.astype(F32)).astype(LOW) for a, b in zip(parts, got)]
    return jnp.concatenate([part[0] for part in parts], axis=0).astype(F32)


def exchange(chunks):
    return lax.all_to_all(chunks, CUBE, 0, 0)


def tell_all(line):
    count = lax.axis_size(AXES)
    return lax.all_to_all(jnp.broadcast_to(line, (count,) + line.shape), AXES, 0, 0)


def sum_line(line):
    count = lax.axis_size(AXES)
    return jnp.sum(lax.all_to_all(line.reshape(count, -1), AXES, 0, 0), axis=0)


def over_halves(shard, at):
    if lax.axis_size("b") == 1:
        return both(shard, swap(shard, "h"), at["h"], 0)
    return lax.all_gather(shard, ("b", "h"), axis=0)


def sum_halves(parts, at):
    if lax.axis_size("b") == 1:
        got = swap(pick(parts, 1 - at["h"]).astype(LOW), "h")
        return pick(parts, at["h"]).astype(F32) + got.astype(F32)
    return lax.psum_scatter(parts.astype(F32), ("b", "h"), scatter_dimension=0, tiled=False)


def fetch_columns(chunks, at):
    halves = over_halves(exchange(chunks), at)
    full = both(halves, swap(halves, "c"), at["c"], 2)
    return full.reshape(-1, full.shape[-1])


def return_columns(grad, at, turn=None):
    count = lax.axis_size("b") * 2
    grad = grad.astype(LOW).reshape(count, 8, 2, -1, grad.shape[-1])
    got = swap(pick(grad, 1 - at["c"], 2), "c")
    if turn is not None:
        got = turn(got)
    mine = pick(grad, at["c"], 2).astype(F32) + got.astype(F32)
    return exchange(sum_halves(mine.astype(LOW), at).astype(LOW))


def fetch_out(shard, at):
    if lax.axis_size("b") > 1:
        whole = lax.all_gather(shard, AXES, axis=0, tiled=True)
        width = whole.shape[1]
        return whole.reshape(2, 8, 2, HEAD_DIM, width).transpose(1, 2, 0, 3, 4).reshape(-1, width)
    rows, width = shard.shape
    shard = both(shard, swap(shard, "h"), at["h"], 0)
    cuts = [(0, 640), (640, 1408), (1408, 2048)]
    wholes = []
    for k, (low, high) in enumerate(cuts):
        part = shard[:, :, low:high].reshape(1, 1, 1, 2, rows, high - low)
        for step in range(3):
            axis = (k + step) % 3
            part = both(part, swap(part, CUBE[axis]), at[CUBE[axis]], axis, joined=True)
        part = both(part, swap(part, "c"), at["c"], 3)
        wholes.append(part.reshape(-1, high - low))
    return jnp.concatenate(wholes, axis=1)


def return_out(grad, at):
    width = grad.shape[1]
    if lax.axis_size("b") > 1:
        whole = grad.reshape(8, 2, 2, HEAD_DIM, width).transpose(2, 0, 1, 3, 4).reshape(-1, width)
        return lax.psum_scatter(whole, AXES, scatter_dimension=0, tiled=True)
    grad = grad.astype(LOW).reshape(2, 2, 2, 2, 2, HEAD_DIM, width)
    got = swap(pick(grad, 1 - at["c"], 3), "c")
    grad = (pick(grad, at["c"], 3).astype(F32) + got.astype(F32)).astype(LOW)
    done = []
    for k, (low, high) in enumerate([(0, 640), (640, 1408), (1408, 2048)]):
        part = grad[..., low:high]
        for step in range(3):
            axis = (k + step) % 3
            name = CUBE[axis]
            got = swap(lax.dynamic_index_in_dim(part, 1 - at[name], axis), name)
            mine = lax.dynamic_index_in_dim(part, at[name], axis)
            part = (mine.astype(F32) + got.astype(F32)).astype(LOW)
        part = part.reshape(2, HEAD_DIM, high - low)
        got = swap(pick(part, 1 - at["h"]), "h")
        done.append(pick(part, at["h"]).astype(F32) + got.astype(F32))
    return jnp.concatenate(done, axis=1)


def gelu_tanh(value):
    return (
        0.5
        * value
        * (1.0 + jnp.tanh(0.7978845608028654 * (value + 0.044715 * value * value * value)))
    )


def normalize(hidden):
    scale = lax.rsqrt(jnp.mean(hidden * hidden, axis=-1, keepdims=True) + EPS)
    return (hidden * scale, scale)


def norm_back(grad_unit, unit, scale):
    return scale * (grad_unit - unit * jnp.mean(grad_unit * unit, axis=-1, keepdims=True))


def piece_tables(rows, at):
    third = rows // 3
    spread_at, chunk_at = [], []
    for core in (at["c"], 1 - at["c"]):
        for other in range(2):
            half = at["h"] ^ other
            for k in range(3):
                for i in range(8):
                    mask = 0
                    for step in range(3):
                        if i >> step & 1:
                            mask |= 4 >> (k + step) % 3
                    spread_at.append((16 * half + 2 * (at["cube"] ^ mask) + core) * rows + k * third)
        for place in range(8):
            for other in range(2):
                chunk_at.append((16 * (at["h"] ^ other) + 2 * place + core) * rows)
    return jnp.stack(spread_at).astype(jnp.int32), jnp.stack(chunk_at).astype(jnp.int32)


def in_order(pieces, table):
    count = table.shape[0]
    cut = pieces.reshape(count, -1, pieces.shape[-1])
    return jnp.take(cut, jnp.argsort(table), axis=0).reshape(pieces.shape)


def as_pieces(rows, table):
    count = table.shape[0]
    cut = rows.reshape(count, -1, rows.shape[-1])
    return jnp.take(cut, table // cut.shape[1], axis=0).reshape(rows.shape)


def with_sides(rows, halo):
    count = lax.axis_size("b")
    before = lax.ppermute(rows[-halo:], "b", [(i, i + 1) for i in range(count - 1)])
    after = lax.ppermute(rows[:halo], "b", [(i + 1, i) for i in range(count - 1)])
    return jnp.concatenate([before, rows, after], axis=0)


def add_sides(rows, halo):
    count = lax.axis_size("b")
    after = lax.ppermute(rows[:halo], "b", [(i + 1, i) for i in range(count - 1)])
    before = lax.ppermute(rows[-halo:], "b", [(i, i + 1) for i in range(count - 1)])
    mine = rows[halo:-halo]
    return mine.at[-halo:].add(after).at[:halo].add(before)


def bucket_lines(bucket_table):
    edge = jnp.full((2 * BLK,), -1, jnp.int32)
    wide = jnp.concatenate([edge, bucket_table, edge])[::-1]
    size = wide.shape[0]
    lines = []
    for d in range(DIAGS):
        last = BLK * (d - MID + 1) + WINDOW - 1 + 2 * BLK
        lines.append(wide[size - 1 - last : size - 1 - last + 2 * BLK])
    return jnp.stack(lines)


def local(
    layer_input,
    output_cotangent,
    segment_ids,
    padding_mask,
    bucket_table,
    attention_norm_gain,
    stacked_query_key_value,
    attention_out,
    position_bias,
    feed_gain,
    feed_in,
    feed_out,
):
    at = {name: lax.axis_index(name) for name in AXES}
    at["cube"] = 4 * at["p"] + 2 * at["q"] + at["r"]
    blocks = lax.axis_size("b")
    halves = 2 * blocks
    _, rows, width = layer_input.shape
    shard_rows = stacked_query_key_value.shape[0]
    hidden_shard = feed_out.shape[0]
    hidden_here = hidden_shard * halves * 2
    halo = 0 if blocks == 1 else WINDOW
    length = 32 * rows
    near = at["h"]
    far = 1 - near

    x_near = pick(layer_input, near)
    x_far = swap(pick(layer_input, far), "h")

    code = (segment_ids * 2 + padding_mask).astype(LOW).reshape(-1)
    gains = attention_norm_gain.shape[0]
    line = jnp.concatenate([attention_norm_gain, feed_gain, position_bias, code])
    lines = tell_all(line)
    gain_attn = lines[:, :gains].reshape(-1).astype(F32)
    gain_feed = lines[:, gains : 2 * gains].reshape(-1).astype(F32)
    bias_end = 2 * gains + position_bias.shape[0]
    bias_full = lines[:, 2 * gains : bias_end].reshape(BUCKETS, -1).astype(F32)
    codes = pick(lines[:, bias_end:].astype(jnp.int32).reshape(-1, 2, rows), near, 1).reshape(-1)
    if halo:
        rim = jnp.full((halo,), -2, jnp.int32)
        codes = jnp.concatenate([rim, codes, rim])
        codes = lax.dynamic_slice_in_dim(codes, at["b"] * length, length + 2 * halo)
    segments = jnp.where(codes < 0, -1, codes // 2)
    padding = jnp.where(codes < 0, 0, codes % 2)

    parts = stacked_query_key_value.reshape(shard_rows, 3, 2, 8, 2, HEAD_DIM)
    parts = parts.transpose(3, 0, 4, 1, 2, 5).reshape(8, shard_rows, -1)
    project = fetch_columns(parts, at)
    third = project.shape[1] // 2
    project = jnp.where(
        at["c"] == 0, project, jnp.concatenate([project[:, third:], project[:, :third]], axis=1)
    )
    out_full = fetch_out(attention_out, at)
    parts = feed_in.reshape(shard_rows, 2, halves, 8, 2, hidden_shard)
    parts = parts.transpose(3, 0, 1, 2, 4, 5).reshape(8, shard_rows, -1)
    expand = fetch_columns(parts, at)
    down = over_halves(feed_out, at)
    down = both(down, swap(down, "c"), at["c"], 1).reshape(hidden_here, width)

    gathered = [spread(x_near), spread(x_far)]
    gathered = jnp.concatenate(gathered, axis=0).astype(F32)
    normed_one = (normalize(gathered)[0] * gain_attn).astype(LOW)
    projected = matmul(normed_one, project).astype(LOW)
    own, other = projected[:, :third], swap(projected[:, third:], "c")

    spread_at, chunk_at = piece_tables(rows, at)
    lane = 2 * at["cube"] + at["c"]
    bias_here = pick(bias_full.reshape(BUCKETS, 2, -1), lane, 2)
    chosen = bucket_table[None] == jnp.arange(BUCKETS, dtype=jnp.int32)[:, None]
    bias_line = jnp.sum(jnp.where(chosen[:, None], bias_here[:, :, None], 0.0), axis=0)
    diag = skewed_bias(bias_line)
    rng, extras = pair_extras(segments, padding, halo, None)
    extras = (*extras, diag)
    span = 2 * HEAD_DIM
    if halo == 0:
        tables = (spread_at, chunk_at, rng)
        tokens = (own, other)
        mixed_own, mixed_other, mixed_t, level = attend_forward(True, 0, tables, tokens, extras)
    else:
        tables = (rng,)
        ordered = in_order(jnp.concatenate([own, other], axis=0), spread_at)
        sides = with_sides(ordered[:, span:], halo)
        tokens = (ordered[:, :span], sides[:, :span], sides[:, span:])
        mixed_all, mixed_t, level = attend_forward(False, halo, tables, tokens, extras)
        mixed_all = as_pieces(mixed_all, chunk_at)
        mixed_own, mixed_other = jnp.split(mixed_all, 2, axis=0)
    mixed = both(mixed_own, swap(mixed_other, "c"), at["c"], 1, joined=True)
    mixed = exchange(mixed.reshape(8, 2 * rows, 2 * span))
    mixed = mixed.transpose(1, 0, 2).reshape(2 * rows, -1)
    tokens_here = jnp.concatenate([x_near, x_far], axis=0).astype(F32)
    hidden_one = tokens_here + matmul(mixed, out_full)

    unit_two, scale_two = normalize(hidden_one)
    normed_two = (unit_two * gain_feed).astype(LOW)
    fed = jnp.concatenate([spread(normed_two[:rows]), spread(normed_two[rows:])], axis=0)
    gate_up = matmul(fed, expand)
    gate = gate_up[:, :hidden_here]
    upward = gate_up[:, hidden_here:]
    activated, gelu_pull = jax.vjp(gelu_tanh, gate)
    inner = (activated * upward).astype(LOW)
    final = matmul(inner, down).astype(LOW)
    final_far = hidden_one[rows:] + collect(final[8 * rows :])
    final_far = swap(final_far.astype(LOW), "h")
    final_near = (hidden_one[:rows] + collect(final[: 8 * rows])).astype(LOW)
    layer_output = both(final_near, final_far, near, 0)

    masked = output_cotangent * padding_mask[..., None].astype(LOW)
    res_near = pick(masked, near)
    res_far = swap(pick(masked, far), "h")
    res_all = jnp.concatenate([spread(res_near), spread(res_far)], axis=0)
    grad_res = jnp.concatenate([res_near, res_far], axis=0).astype(F32)
    grad_inner = matmul(res_all, down, NT)
    grad_gate = gelu_pull(grad_inner * upward)[0]
    grad_gate_up = jnp.concatenate([grad_gate, grad_inner * activated], axis=1).astype(LOW)
    grad_fed = matmul(grad_gate_up, expand, NT).astype(LOW)
    grad_normed_two = jnp.concatenate(
        [collect(grad_fed[: 8 * rows]), collect(grad_fed[8 * rows :])], axis=0
    )
    grad_down = matmul(inner, res_all, TN)
    grad_expand = matmul(fed, grad_gate_up, TN)
    grad_feed_gain = sum_line(jnp.sum(grad_normed_two * unit_two, axis=0))
    grad_hidden = grad_res + norm_back(grad_normed_two * gain_feed, unit_two, scale_two)

    grad_hidden_low = grad_hidden.astype(LOW)
    grad_mixed = matmul(grad_hidden_low, out_full, NT).astype(LOW)
    grad_mixed = exchange(grad_mixed.reshape(2 * rows, 8, -1).transpose(1, 0, 2))
    grad_mixed = grad_mixed.reshape(16 * rows, 2, span)
    g_own = pick(grad_mixed, at["c"], 1)
    g_other = swap(pick(grad_mixed, 1 - at["c"], 1), "c")
    grad_out = matmul(mixed, grad_hidden_low, TN)
    if halo == 0:
        d_own, d_other, d_diag = attend_backward(
            True, 0, tables, tokens, extras, (g_own, g_other), (mixed_t, level)
        )
    else:
        g_all = in_order(jnp.concatenate([g_own, g_other], axis=0), chunk_at)
        dq, dk, dv, d_diag = attend_backward(
            False, halo, tables, tokens, extras, (g_all,), (mixed_t, level)
        )
        d_all = jnp.concatenate([dq, add_sides(dk, halo), add_sides(dv, halo)], axis=1)
        d_own, d_other = jnp.split(as_pieces(d_all.astype(LOW), spread_at), 2, axis=0)
    grad_projected = jnp.concatenate([d_own, swap(d_other, "c")], axis=1)
    grad_normed_one = matmul(grad_projected, project, NT).astype(LOW)
    g_far = collect(grad_normed_one[8 * rows :])
    g_near = collect(grad_normed_one[: 8 * rows])
    unit_one, scale_one = normalize(tokens_here)
    grad_gain_rows = 0.0
    results = []
    for part, low in ((g_far, rows), (g_near, 0)):
        cut = slice(low, low + rows)
        grad_gain_rows = grad_gain_rows + jnp.sum(part * unit_one[cut], axis=0)
        whole = grad_hidden[cut] + norm_back(part * gain_attn, unit_one[cut], scale_one[cut])
        results.append(whole.astype(LOW))
    input_grad = both(results[1], swap(results[0], "h"), near, 0)
    grad_attention_gain = sum_line(grad_gain_rows)

    hot = bucket_lines(bucket_table)[None] == jnp.arange(BUCKETS, dtype=jnp.int32)[:, None, None]
    sums = d_diag.reshape(2, DIAGS, 2 * BLK)
    sums = jnp.sum(jnp.where(hot[None], sums[:, None], 0.0), axis=(2, 3)).T
    lanes = (jnp.arange(16, dtype=jnp.int32) == lane).astype(F32)
    grad_position_bias = sum_line((sums[:, :, None] * lanes).reshape(-1))

    grad_project = matmul(normed_one, grad_projected, TN)

    def turn(got):
        return jnp.concatenate([got[..., third:], got[..., :third]], axis=-1)

    grad_project = return_columns(grad_project, at, turn)
    grad_project = jnp.where(at["c"] == 0, grad_project, turn(grad_project))
    grad_project = grad_project.reshape(8, shard_rows, 2, 3, 2, HEAD_DIM)
    grad_project = grad_project.transpose(1, 3, 4, 0, 2, 5).reshape(shard_rows, -1).astype(F32)
    grad_expand = return_columns(grad_expand, at)
    grad_expand = grad_expand.reshape(8, shard_rows, 2, halves, 2, hidden_shard)
    grad_expand = grad_expand.transpose(1, 2, 3, 0, 4, 5).reshape(shard_rows, -1).astype(F32)
    grad_down = grad_down.astype(LOW).reshape(halves, 2, hidden_shard, width)
    got = swap(pick(grad_down, 1 - at["c"], 1), "c")
    grad_down = pick(grad_down, at["c"], 1).astype(F32) + got.astype(F32)
    grad_down = sum_halves(grad_down.astype(LOW), at).astype(F32)
    grad_out = return_out(grad_out, at)
    return (
        layer_output,
        input_grad,
        grad_attention_gain,
        grad_project,
        grad_out,
        grad_position_bias,
        grad_feed_gain,
        grad_expand,
        grad_down,
    )


def solution(mesh):
    wide = Mesh(mesh.devices.reshape(-1, 2, 2, 2, 2, 2), AXES)
    lead, tokens, rows = P(AXES), P(None, AXES), P(AXES, None)
    return jax.shard_map(
        local,
        mesh=wide,
        in_specs=(tokens, tokens, tokens, tokens, P(), lead, rows, rows, lead, lead, rows, rows),
        out_specs=(tokens, tokens, lead, rows, rows, lead, lead, rows, rows),
        check_vma=False,
    )
```

time: 5320 us -> 1120 us (0.21)
  waiting for transfers between devices: 2260 us -> 404 us
  local copies, waits for them, and re-layouts: 1440 us -> 146 us
  starting transfers between devices: 800 us -> 214 us
  matrix products: 522 us -> 95.8 us
  blocking collectives: 153 us -> 0 us
  Pallas kernels: 0 us -> 119 us
    reduce_scatter x4 -> x0, waiting for transfers between devices: 1570 us -> none  [the longest x1 888 us: scatter_feed(): lax.psum_scatter(parts[1], 'dev', scatter_dimension=0, tiled=True)]
    gather x2, local copies, waits for them, and re-layouts: 1170 us -> 1.31 us  [the longest x1 0.66 us: pair_extras(): high = jnp.sum(segments[None, :] <= segments[last][:, None], axis=1)]
    ppermute x132 -> x154, starting transfers between devices: 800 us -> 172 us  [swap(): return lax.ppermute(value, axis, SWAP)]
    dot_general x127 -> x12, matrix products: 522 us -> 95.8 us  [matmul(): return lax.dot_general(left, right, dims, preferred_element_type=F32)]
    ppermute x132 -> x154, waiting for transfers between devices: 690 us -> 349 us  [swap(): return lax.ppermute(value, axis, SWAP)]
    unnamed x2 -> x0, blocking collectives: 153 us -> none
    another operation x17 -> x5, local copies, waits for them, and re-layouts: 124 us -> 3.4 us  [the longest x1 1.88 us: skewed_bias(): return jnp.stack(lines)]
    pallas_call x0 -> x2, Pallas kernels: none -> 119 us  [the longest x1 61.4 us: attend_backward(): pl.pallas_call(lambda *refs: backward_kernel(local, halo, *refs), out_sha...]
  transfers between devices with their start and end apart: 140 -> 164, of which waited for: 47 -> 61; matrix products, arithmetic and copies ran while one was open for 35% -> 25% of each run, Pallas kernels for 0% -> 11%
where the time goes in v1:
time: 1120 us; the launch traced here: 1110 us
  waiting for transfers between devices  404 us (36%)
  starting transfers between devices  214 us (19%)
  local copies, waits for them, and re-layouts  146 us (13%)
  other arithmetic  129 us (12%)
  Pallas kernels  119 us (11%)
  matrix products  95.8 us (9%)
    ppermute x154, waiting for transfers between devices, swap(): return lax.ppermute(value, axis, SWAP)  349 us
    ppermute x154, starting transfers between devices, swap(): return lax.ppermute(value, axis, SWAP)  172 us
    dot_general x12, matrix products, matmul(): return lax.dot_general(left, right, dims, preferred_element_type=F32)  95.8 us
    pallas_call x1, Pallas kernels, attend_backward(): pl.pallas_call(lambda *refs: backward_kernel(local, halo, *refs), out_sha...  61.4 us
    pallas_call x1, Pallas kernels, attend_forward(): pl.pallas_call(lambda *refs: forward_kernel(local, halo, *refs), out_shap...  58 us
    all_to_all x3, waiting for transfers between devices, sum_line(): return jnp.sum(lax.all_to_all(line.reshape(count, -1), AXES, 0, 0), axis=0)  55 us
    select_n x29, other arithmetic, both(): jnp.where(bit == 0, put([mine, theirs], axis), put([theirs, mine], axis))  42.9 us
    unnamed x211, local copies, waits for them, and re-layouts  27.5 us
  transfers between devices with their start and end apart: 164, of which 61 were waited for; matrix products, arithmetic and copies ran while one was open for 25% of the time, Pallas kernels for 11%

profile of v1, /device:TPU:0, one launch (start us, length us, event | category | flops | bytes accessed | tf_op | source)
XLA Modules:
  0.0 1112.1 jit_solution(9178517456335945110)
XLA Ops:
  43.6 4.9 all-to-all-start.1
  67.9 5.6 concatenate.762.refs_5_
  97.0 14.6 %collective-permute-done.8 = bf16[2,32,2048]{2,1,0:T(8,128)(2,1)S(1)} collective-permute-done((bf16[2,32,2048]{2,1,0:T(8,128)(2,1)S(1)}, bf16[2,32,2048]{2,1,0:T(8,128)(2,1)S(1)}, u32[]{:S(2)}, u32[]{:S(2)}) %collective-permute-start.8) | collective-permute-done | bytes 262176 | tf_op jit(solution)/shard_map/ppermute | solution.py:383
  119.1 17.8 %collective-permute-done.85 = bf16[2,32,2048]{2,1,0:T(8,128)(2,1)S(1)} collective-permute-done((bf16[2,32,2048]{2,1,0:T(8,128)(2,1)S(1)}, bf16[2,32,2048]{2,1,0:T(8,128)(2,1)S(1)}, u32[]{:S(2)}, u32[]{:S(2)}) %collective-permute-start.85) | collective-permute-done | bytes 262176 | tf_op jit(solution)/shard_map/ppermute | solution.py:383
  145.9 11.2 %collective-permute-done.10 = bf16[1,32,2048]{2,1,0:T(8,128)(2,1)S(1)} collective-permute-done((bf16[1,32,2048]{2,1,0:T(8,128)(2,1)S(1)}, bf16[1,32,2048]{2,1,0:T(8,128)(2,1)S(1)}, u32[]{:S(2)}, u32[]{:S(2)}) %collective-permute-start.10) | collective-permute-done | bytes 131104 | tf_op jit(solution)/shard_map/ppermute | solution.py:383
  158.2 3.9 collective-permute-done.13
  163.1 3.9 collective-permute-done.16
  168.1 3.9 collective-permute-done.87
  173.1 3.9 collective-permute-done.90
  178.1 3.9 collective-permute-done.93
  202.5 4.0 collective-permute-done.17
  210.8 4.9 collective-permute-done.91
  219.5 4.1 collective-permute-done.29
  240.6 6.6 collective-permute-done.12
  253.1 7.9 collective-permute-done.18
  262.1 4.1 all-to-all-start.3
  272.1 4.1 fusion
  276.2 25.4 %collective-permute-done.19 = bf16[8,64,768]{2,1,0:T(8,128)(2,1)S(1)} collective-permute-done((bf16[8,64,768]{2,1,0:T(8,128)(2,1)S(1)}, bf16[8,64,768]{2,1,0:T(8,128)(2,1)S(1)}, u32[]{:S(2)}, u32[]{:S(2)}) %collective-permute-start.19) | collective-permute-done | bytes 786464 | tf_op jit(solution)/shard_map/ppermute | solution.py:383
  311.2 8.6 convolution_convert_fusion.5
  332.8 58.0 %shard_map.187 = (bf16[1536,128]{1,0:T(8,128)(2,1)}, bf16[1536,128]{1,0:T(8,128)(2,1)}, f32[128,3072]{1,0:T(8,128)}, f32[2,3072]{1,0:T(2,128)}) custom-call(s32[96]{0:T(128)} %stack.758.refs_0_, s32[32]{0:T(128)} %stack.791.refs_1_, s32[2,12]{1,0:T(2,128)} %pad_add_fusion.refs_2_, bf16[1536,384]{1,0:T(8,128)(2,1)} %get-tuple-element.83.refs_3_, ...), custom_call_target="tpu_custom_call" | custom-call | flops 4404019200 | bytes 8388608 | tf_op jit(solution)/shard_map/pallas_call | solution.py:289
  399.2 4.4 all-to-all-start.2
  403.7 4.2 maximum_select_fusion.4
  420.8 4.7 multiply_reduce_fusion
  443.9 4.9 collective-permute-done.52
  451.1 7.0 collective-permute-done.37
  462.6 9.9 collective-permute-done.38
  476.8 4.9 collective-permute-done.44
  485.8 13.0 %fusion.124 = f32[1536,1280]{0,1:T(8,128)} fusion(bf16[1536,2048]{1,0:T(8,128)(2,1)} %copy-done.79, bf16[2048,1280]{1,0:T(8,128)(2,1)S(1)} %bitcast.536), kind=kOutput, calls=%fused_computation.456 | convolution fusion | flops 8053063680 | bytes 19398656 | tf_op jit(solution)/shard_map/dot_general | solution.py:396
  498.8 10.6 fusion.8
  511.3 10.5 convolution_convert_fusion.1
  521.8 11.6 %convolution_convert_fusion.2 = bf16[1536,2048]{1,0:T(8,128)(2,1)S(1)} fusion(bf16[2048,1280]{1,0:T(8,128)(2,1)S(1)} %bitcast.537, bf16[1536,640]{0,1:T(8,128)(2,1)} %copy-done.92, bf16[1536,640]{0,1:T(8,128)(2,1)} %copy-done.91), kind=kOutput, calls=%fused_computation.12 | convolution fusion | flops 8064073728 | bytes 15466496 | tf_op jit(solution)/shard_map/dot_general | solution.py:396
  533.4 7.5 convolution_convert_fusion.7
  541.0 5.4 convolution_convert_fusion.3
  554.7 10.1 collective-permute-done.111
  568.0 9.7 collective-permute-done.102
  581.3 8.7 collective-permute-done.67
  595.2 6.1 collective-permute-done.58
  613.3 4.3 collective-permute-done.97
  622.0 4.1 collective-permute-done.100
  648.1 4.1 collective-permute-done.101
  652.2 6.2 collective-permute-done.104
  659.4 4.0 collective-permute-done.107
  668.1 4.1 fusion.17
  672.2 5.7 convolution_convert_fusion.4
  678.6 4.1 all-to-all-start.8
  698.2 4.2 all-to-all-start.4
  714.7 25.7 %collective-permute-done.76 = bf16[96,2048]{1,0:T(8,128)(2,1)S(1)} collective-permute-done((bf16[96,2048]{1,0:T(8,128)(2,1)}, bf16[96,2048]{1,0:T(8,128)(2,1)S(1)}, u32[]{:S(2)}, u32[]{:S(2)}) %collective-permute-start.76) | collective-permute-done | bytes 393248 | tf_op jit(solution)/shard_map/ppermute | solution.py:383
  745.2 7.6 collective-permute-done.153
  756.7 61.4 %shard_map.188 = (bf16[1536,384]{1,0:T(8,128)(2,1)}, bf16[1536,384]{1,0:T(8,128)(2,1)}, f32[18,512]{1,0:T(8,128)}) custom-call(s32[96]{0:T(128)} %stack.758.refs_0_, s32[32]{0:T(128)} %stack.791.refs_1_, s32[2,12]{1,0:T(2,128)} %pad_add_fusion.refs_2_, bf16[1536,384]{1,0:T(8,128)(2,1)} %get-tuple-element.83.refs_3_, ...), custom_call_target="tpu_custom_call" | custom-call | flops 11010048000 | bytes 8388608 | tf_op jit(solution)/shard_map/pallas_call | solution.py:324
  825.1 6.3 all-to-all-start.7
  833.8 52.8 %all-to-all-done.7 = f32[32,1,32]{2,1,0:T(1,128)S(1)} async-done(((f32[32,1,32]{2,1,0:T(1,128)}), f32[32,1,32]{2,1,0:T(1,128)S(1)}, u32[]{:S(2)}, u32[]{:S(2)}) %all-to-all-start.7) | async-done | bytes 4128 | tf_op jit(solution)/shard_map/all_to_all | solution.py:432
  889.8 8.7 convolution_convert_fusion.6
  902.1 5.4 convolution_convert_fusion
  911.9 10.5 collective-permute-done.116
  924.7 10.4 collective-permute-done.125
  979.3 5.4 fusion.3
  995.2 37.6 %collective-permute-done.138 = bf16[1,2,2,2,64,640]{5,4,3,2,1,0:T(8,128)(2,1)S(1)} collective-permute-done((bf16[1,2,2,2,64,640]{5,4,3,2,1,0:T(8,128)(2,1)S(1)}, bf16[1,2,2,2,64,640]{5,4,3,2,1,0:T(8,128)(2,1)S(1)}, u32[]{:S(2)}, u32[]{:S(2)}) %collective-permute-start.138) | collective-permute-done | bytes 655392 | tf_op jit(solution)/shard_map/ppermute | solution.py:383
  1037.7 4.0 collective-permute-done.139
  1046.4 7.8 reshape.2091
  1054.2 6.6 copy.182
  1060.8 7.9 reshape.2087
  1085.9 5.1 collective-permute-done.144
  1091.2 6.3 collective-permute-done.145
  1106.5 5.2 reshape.2080
  (855 shorter events, 458.0 us)
Async XLA Ops:
  2.5 73.5 %collective-permute-start.1 = (bf16[1,32,2048]{2,1,0:T(8,128)(2,1)}, bf16[1,32,2048]{2,1,0:T(8,128)(2,1)}, u32[]{:S(2)}, u32[]{:S(2)}) collective-permute-start(bf16[1,32,2048]{2,1,0:T(8,128)(2,1)} %get-tuple-element.109), channel_id=1, source_target_pairs={{0,8},{8,0},{1,9},{9,1},{2,10},{10,2},{3,11},{11,3},{4,12},{12,4},... | collective-permute-start | bytes 393224 | tf_op jit(solution)/shard_map/ppermute | solution.py:383
  5.5 73.5 %collective-permute-start.4 = (bf16[1,32,2048]{2,1,0:T(8,128)(2,1)}, bf16[1,32,2048]{2,1,0:T(8,128)(2,1)}, u32[]{:S(2)}, u32[]{:S(2)}) collective-permute-start(bf16[1,32,2048]{2,1,0:T(8,128)(2,1)} %get-tuple-element.108), channel_id=1, source_target_pairs={{0,4},{4,0},{1,5},{5,1},{2,6},{6,2},{3,7},{7,3},{8,12},{12,8},{9,1... | collective-permute-start | bytes 393224 | tf_op jit(solution)/shard_map/ppermute | solution.py:383
  7.1 74.5 %collective-permute-start.7 = (bf16[1,32,2048]{2,1,0:T(8,128)(2,1)}, bf16[1,32,2048]{2,1,0:T(8,128)(2,1)}, u32[]{:S(2)}, u32[]{:S(2)}) collective-permute-start(bf16[1,32,2048]{2,1,0:T(8,128)(2,1)} %get-tuple-element.107), channel_id=1, source_target_pairs={{0,2},{2,0},{1,3},{3,1},{4,6},{6,4},{5,7},{7,5},{8,10},{10,8},{9,1... | collective-permute-start | bytes 393224 | tf_op jit(solution)/shard_map/ppermute | solution.py:383
  10.6 126.4 %collective-permute-start = (bf16[96,2048]{1,0:T(8,128)(2,1)}, bf16[96,2048]{1,0:T(8,128)(2,1)S(1)}, u32[]{:S(2)}, u32[]{:S(2)}) collective-permute-start(bf16[96,2048]{1,0:T(8,128)(2,1)} %get-tuple-element.106), channel_id=1, source_target_pairs={{0,16},{16,0},{1,17},{17,1},{2,18},{18,2},{3,19},{19,3},{4,20},{20... | collective-permute-start | bytes 1179656 | tf_op jit(solution)/shard_map/ppermute | solution.py:383
  16.9 26.7 %all-to-all-start = ((bf16[32,2,176]{2,1,0:T(2,128)(2,1)}), bf16[32,2,176]{2,1,0:T(2,128)(2,1)}, u32[]{:S(2)}, u32[]{:S(2)}) async-start(bf16[32,2,176]{2,1,0:T(2,128)(2,1)} %reshape.2123), calls=%async_computation | async-start | bytes 65536 | tf_op jit(solution)/shard_map/all_to_all | solution.py:427
  20.1 67.8 %collective-permute-start.23 = (bf16[64,2048]{1,0:T(8,128)(2,1)}, bf16[64,2048]{1,0:T(8,128)(2,1)}, u32[]{:S(2)}, u32[]{:S(2)}) collective-permute-start(bf16[64,2048]{1,0:T(8,128)(2,1)} %param.19), channel_id=1, source_target_pairs={{0,16},{16,0},{1,17},{17,1},{2,18},{18,2},{3,19},{19,3},{4,20},{20... | collective-permute-start | bytes 786440 | tf_op jit(solution)/shard_map/ppermute | solution.py:383
  43.6 218.5 %all-to-all-start.1 = ((bf16[8,64,768]{2,1,0:T(8,128)(2,1)}), bf16[8,64,768]{2,1,0:T(8,128)(2,1)S(1)}, u32[]{:S(2)}, u32[]{:S(2)}) async-start(bf16[8,64,768]{2,1,0:T(8,128)(2,1)} %reshape.2026), calls=%async_computation.1 | async-start | bytes 1572864 | tf_op jit(solution)/shard_map/all_to_all | solution.py:422
  84.1 53.8 %collective-permute-start.77 = (bf16[96,2048]{1,0:T(8,128)(2,1)}, bf16[96,2048]{1,0:T(8,128)(2,1)S(1)}, u32[]{:S(2)}, u32[]{:S(2)}) collective-permute-start(bf16[96,2048]{1,0:T(8,128)(2,1)} %get-tuple-element.95), channel_id=1, source_target_pairs={{0,16},{16,0},{1,17},{17,1},{2,18},{18,2},{3,19},{19,3},{4,20},{20... | collective-permute-start | bytes 1179656 | tf_op jit(solution)/shard_map/ppermute | solution.py:383
  84.7 98.4 %collective-permute-start.56 = (bf16[160,2048]{1,0:T(8,128)(2,1)}, bf16[160,2048]{1,0:T(8,128)(2,1)S(1)}, u32[]{:S(2)}, u32[]{:S(2)}) collective-permute-start(bf16[160,2048]{1,0:T(8,128)(2,1)} %param.23), channel_id=1, source_target_pairs={{0,16},{16,0},{1,17},{17,1},{2,18},{18,2},{3,19},{19,3},{4,20},{20... | collective-permute-start | bytes 1966088 | tf_op jit(solution)/shard_map/ppermute | solution.py:383
  93.7 17.8 %collective-permute-start.8 = (bf16[2,32,2048]{2,1,0:T(8,128)(2,1)S(1)}, bf16[2,32,2048]{2,1,0:T(8,128)(2,1)S(1)}, u32[]{:S(2)}, u32[]{:S(2)}) collective-permute-start(bf16[2,32,2048]{2,1,0:T(8,128)(2,1)S(1)} %pad_maximum_fusion.56), channel_id=1, source_target_pairs={{0,8},{8,0},{1,9},{9,1},{2,10},{10,2},{3,11},{11,3},{4,12},{12,4},... | collective-permute-start | bytes 786440 | tf_op jit(solution)/shard_map/ppermute | solution.py:383
  95.3 17.8 %collective-permute-start.79 = (bf16[2,32,2048]{2,1,0:T(8,128)(2,1)S(1)}, bf16[2,32,2048]{2,1,0:T(8,128)(2,1)S(1)}, u32[]{:S(2)}, u32[]{:S(2)}) collective-permute-start(bf16[2,32,2048]{2,1,0:T(8,128)(2,1)S(1)} %pad_maximum_fusion.66), channel_id=1, source_target_pairs={{0,4},{4,0},{1,5},{5,1},{2,6},{6,2},{3,7},{7,3},{8,12},{12,8},{9,1... | collective-permute-start | bytes 786440 | tf_op jit(solution)/shard_map/ppermute | solution.py:383
  113.2 23.8 %collective-permute-start.85 = (bf16[2,32,2048]{2,1,0:T(8,128)(2,1)S(1)}, bf16[2,32,2048]{2,1,0:T(8,128)(2,1)S(1)}, u32[]{:S(2)}, u32[]{:S(2)}) collective-permute-start(bf16[2,32,2048]{2,1,0:T(8,128)(2,1)S(1)} %pad_maximum_fusion.68), channel_id=1, source_target_pairs={{0,8},{8,0},{1,9},{9,1},{2,10},{10,2},{3,11},{11,3},{4,12},{12,4},... | collective-permute-start | bytes 786440 | tf_op jit(solution)/shard_map/ppermute | solution.py:383
  118.5 21.8 %collective-permute-start.32 = (bf16[1,1,1,2,64,640]{5,4,3,2,1,0:T(8,128)(2,1)S(1)}, bf16[1,1,1,2,64,640]{5,4,3,2,1,0:T(8,128)(2,1)S(1)}, u32[]{:S(2)}, u32[]{:S(2)}) collective-permute-start(bf16[1,1,1,2,64,640]{5,4,3,2,1,0:T(8,128)(2,1)S(1)} %get-tuple-element.112), channel_id=1, source_target_pairs={{0,2},{2,0},{1,3},{3,1},{4,6},{6,4},{5,7},{7,5},{8,10},{10,8},{9,1... | collective-permute-start | bytes 491528 | tf_op jit(solution)/shard_map/ppermute | solution.py:383
  137.9 88.6 %collective-permute-start.3 = (bf16[4,32,2048]{2,1,0:T(8,128)(2,1)S(1)}, bf16[4,32,2048]{2,1,0:T(8,128)(2,1)S(1)}, u32[]{:S(2)}, u32[]{:S(2)}) collective-permute-start(bf16[4,32,2048]{2,1,0:T(8,128)(2,1)S(1)} %pad_maximum_fusion.33), channel_id=1, source_target_pairs={{0,2},{2,0},{1,3},{3,1},{4,6},{6,4},{5,7},{7,5},{8,10},{10,8},{9,1... | collective-permute-start | bytes 1572872 | tf_op jit(solution)/shard_map/ppermute | solution.py:383
  140.3 90.3 %collective-permute-start.6 = (bf16[4,32,2048]{2,1,0:T(8,128)(2,1)S(1)}, bf16[4,32,2048]{2,1,0:T(8,128)(2,1)S(1)}, u32[]{:S(2)}, u32[]{:S(2)}) collective-permute-start(bf16[4,32,2048]{2,1,0:T(8,128)(2,1)S(1)} %pad_maximum_fusion.34), channel_id=1, source_target_pairs={{0,8},{8,0},{1,9},{9,1},{2,10},{10,2},{3,11},{11,3},{4,12},{12,4},... | collective-permute-start | bytes 1572872 | tf_op jit(solution)/shard_map/ppermute | solution.py:383
  143.7 89.5 %collective-permute-start.9 = (bf16[4,32,2048]{2,1,0:T(8,128)(2,1)S(1)}, bf16[4,32,2048]{2,1,0:T(8,128)(2,1)S(1)}, u32[]{:S(2)}, u32[]{:S(2)}) collective-permute-start(bf16[4,32,2048]{2,1,0:T(8,128)(2,1)S(1)} %pad_maximum_fusion.35), channel_id=1, source_target_pairs={{0,4},{4,0},{1,5},{5,1},{2,6},{6,2},{3,7},{7,3},{8,12},{12,8},{9,1... | collective-permute-start | bytes 1572872 | tf_op jit(solution)/shard_map/ppermute | solution.py:383
  230.4 160.4 %collective-permute-start.57 = (bf16[2,160,2048]{2,1,0:T(8,128)(2,1)}, bf16[2,160,2048]{2,1,0:T(8,128)(2,1)}, u32[]{:S(2)}, u32[]{:S(2)}) collective-permute-start(bf16[2,160,2048]{2,1,0:T(8,128)(2,1)} %maximum_select_fusion.17), channel_id=1, source_target_pairs={{0,1},{1,0},{2,3},{3,2},{4,5},{5,4},{6,7},{7,6},{8,9},{9,8},{10,11... | collective-permute-start | bytes 3932168 | tf_op jit(solution)/shard_map/ppermute | solution.py:383
  230.6 91.1 %collective-permute-start.34 = (bf16[2,1,2,2,64,640]{5,4,3,2,0,1:T(8,128)(2,1)}, bf16[2,1,2,2,64,640]{5,4,3,2,0,1:T(8,128)(2,1)S(1)}, u32[]{:S(2)}, u32[]{:S(2)}) collective-permute-start(bf16[2,1,2,2,64,640]{5,4,3,2,0,1:T(8,128)(2,1)} %fusion.142), channel_id=1, source_target_pairs={{0,4},{4,0},{1,5},{5,1},{2,6},{6,2},{3,7},{7,3},{8,12},{12,8},{9,1... | collective-permute-start | bytes 1966088 | tf_op jit(solution)/shard_map/ppermute | solution.py:383
  238.3 22.7 %collective-permute-start.18 = (bf16[4,32,2048]{2,1,0:T(8,128)(2,1)S(1)}, bf16[4,32,2048]{2,1,0:T(8,128)(2,1)S(1)}, u32[]{:S(2)}, u32[]{:S(2)}) collective-permute-start(bf16[4,32,2048]{2,1,0:T(8,128)(2,1)S(1)} %pad_maximum_fusion.38), channel_id=1, source_target_pairs={{0,4},{4,0},{1,5},{5,1},{2,6},{6,2},{3,7},{7,3},{8,12},{12,8},{9,1... | collective-permute-start | bytes 1572872 | tf_op jit(solution)/shard_map/ppermute | solution.py:383
  247.2 21.6 %collective-permute-start.89 = (bf16[4,32,2048]{2,1,0:T(8,128)(2,1)}, bf16[4,32,2048]{2,1,0:T(8,128)(2,1)}, u32[]{:S(2)}, u32[]{:S(2)}) collective-permute-start(bf16[4,32,2048]{2,1,0:T(8,128)(2,1)} %pad_maximum_fusion.48), channel_id=1, source_target_pairs={{0,2},{2,0},{1,3},{3,1},{4,6},{6,4},{5,7},{7,5},{8,10},{10,8},{9,1... | collective-permute-start | bytes 1572872 | tf_op jit(solution)/shard_map/ppermute | solution.py:383
  250.9 52.3 %collective-permute-start.92 = (bf16[4,32,2048]{2,1,0:T(8,128)(2,1)}, bf16[4,32,2048]{2,1,0:T(8,128)(2,1)}, u32[]{:S(2)}, u32[]{:S(2)}) collective-permute-start(bf16[4,32,2048]{2,1,0:T(8,128)(2,1)} %pad_maximum_fusion.49), channel_id=1, source_target_pairs={{0,8},{8,0},{1,9},{9,1},{2,10},{10,2},{3,11},{11,3},{4,12},{12,4},... | collective-permute-start | bytes 1572872 | tf_op jit(solution)/shard_map/ppermute | solution.py:383
  262.1 68.9 %all-to-all-start.3 = ((bf16[8,64,1280]{2,1,0:T(8,128)(2,1)}), bf16[8,64,1280]{2,1,0:T(8,128)(2,1)S(1)}, u32[]{:S(2)}, u32[]{:S(2)}) async-start(bf16[8,64,1280]{2,1,0:T(8,128)(2,1)} %reshape.2041), calls=%async_computation.3 | async-start | bytes 2621440 | tf_op jit(solution)/shard_map/all_to_all | solution.py:422
  266.2 35.5 %collective-permute-start.19 = (bf16[8,64,768]{2,1,0:T(8,128)(2,1)S(1)}, bf16[8,64,768]{2,1,0:T(8,128)(2,1)S(1)}, u32[]{:S(2)}, u32[]{:S(2)}) collective-permute-start(bf16[8,64,768]{2,1,0:T(8,128)(2,1)S(1)} %all-to-all-done.1), channel_id=1, source_target_pairs={{0,16},{16,0},{1,17},{17,1},{2,18},{18,2},{3,19},{19,3},{4,20},{20... | collective-permute-start | bytes 2359304 | tf_op jit(solution)/shard_map/ppermute | solution.py:383
  268.9 38.2 %collective-permute-start.95 = (bf16[4,32,2048]{2,1,0:T(8,128)(2,1)}, bf16[4,32,2048]{2,1,0:T(8,128)(2,1)S(1)}, u32[]{:S(2)}, u32[]{:S(2)}) collective-permute-start(bf16[4,32,2048]{2,1,0:T(8,128)(2,1)} %pad_maximum_fusion.50), channel_id=1, source_target_pairs={{0,4},{4,0},{1,5},{5,1},{2,6},{6,2},{3,7},{7,3},{8,12},{12,8},{9,1... | collective-permute-start | bytes 1572872 | tf_op jit(solution)/shard_map/ppermute | solution.py:383
  303.2 21.4 %collective-permute-start.26 = (bf16[2,2,1,2,64,640]{5,4,3,2,1,0:T(8,128)(2,1)S(1)}, bf16[2,2,1,2,64,640]{5,4,3,2,1,0:T(8,128)(2,1)S(1)}, u32[]{:S(2)}, u32[]{:S(2)}) collective-permute-start(bf16[2,2,1,2,64,640]{5,4,3,2,1,0:T(8,128)(2,1)S(1)} %copy-done.29), channel_id=1, source_target_pairs={{0,2},{2,0},{1,3},{3,1},{4,6},{6,4},{5,7},{7,5},{8,10},{10,8},{9,1... | collective-permute-start | bytes 1966088 | tf_op jit(solution)/shard_map/ppermute | solution.py:383
  307.1 21.9 %collective-permute-start.30 = (bf16[1,2,2,2,64,768]{5,4,3,2,1,0:T(8,128)(2,1)S(1)}, bf16[1,2,2,2,64,768]{5,4,3,2,1,0:T(8,128)(2,1)S(1)}, u32[]{:S(2)}, u32[]{:S(2)}) collective-permute-start(bf16[1,2,2,2,64,768]{5,4,3,2,1,0:T(8,128)(2,1)S(1)} %copy-done.21), channel_id=1, source_target_pairs={{0,8},{8,0},{1,9},{9,1},{2,10},{10,2},{3,11},{11,3},{4,12},{12,4},... | collective-permute-start | bytes 2359304 | tf_op jit(solution)/shard_map/ppermute | solution.py:383
  324.3 69.9 %collective-permute-start.35 = (bf16[2,2,2,2,64,640]{5,4,3,2,1,0:T(8,128)(2,1)}, bf16[2,2,2,2,64,640]{5,4,3,2,1,0:T(8,128)(2,1)}, u32[]{:S(2)}, u32[]{:S(2)}) collective-permute-start(bf16[2,2,2,2,64,640]{5,4,3,2,1,0:T(8,128)(2,1)} %maximum_select_fusion.15), channel_id=1, source_target_pairs={{0,1},{1,0},{2,3},{3,2},{4,5},{5,4},{6,7},{7,6},{8,9},{9,8},{10,11... | collective-permute-start | bytes 3932168 | tf_op jit(solution)/shard_map/ppermute | solution.py:383
  325.9 77.7 %collective-permute-start.27 = (bf16[2,2,2,2,64,640]{5,4,3,2,1,0:T(8,128)(2,1)}, bf16[2,2,2,2,64,640]{5,4,3,2,1,0:T(8,128)(2,1)}, u32[]{:S(2)}, u32[]{:S(2)}) collective-permute-start(bf16[2,2,2,2,64,640]{5,4,3,2,1,0:T(8,128)(2,1)} %maximum_select_fusion.13), channel_id=1, source_target_pairs={{0,1},{1,0},{2,3},{3,2},{4,5},{5,4},{6,7},{7,6},{8,9},{9,8},{10,11... | collective-permute-start | bytes 3932168 | tf_op jit(solution)/shard_map/ppermute | solution.py:383
  330.4 81.5 %collective-permute-start.31 = (bf16[2,2,2,2,64,768]{5,4,3,2,1,0:T(8,128)(2,1)}, bf16[2,2,2,2,64,768]{5,4,3,2,1,0:T(8,128)(2,1)}, u32[]{:S(2)}, u32[]{:S(2)}) collective-permute-start(bf16[2,2,2,2,64,768]{5,4,3,2,1,0:T(8,128)(2,1)} %maximum_select_fusion.12), channel_id=1, source_target_pairs={{0,1},{1,0},{2,3},{3,2},{4,5},{5,4},{6,7},{7,6},{8,9},{9,8},{10,11... | collective-permute-start | bytes 4718600 | tf_op jit(solution)/shard_map/ppermute | solution.py:383
  330.9 77.0 %collective-permute-start.54 = (bf16[8,64,1280]{2,1,0:T(8,128)(2,1)S(1)}, bf16[8,64,1280]{2,1,0:T(8,128)(2,1)}, u32[]{:S(2)}, u32[]{:S(2)}) collective-permute-start(bf16[8,64,1280]{2,1,0:T(8,128)(2,1)S(1)} %all-to-all-done.3), channel_id=1, source_target_pairs={{0,16},{16,0},{1,17},{17,1},{2,18},{18,2},{3,19},{19,3},{4,20},{20... | collective-permute-start | bytes 3932168 | tf_op jit(solution)/shard_map/ppermute | solution.py:383
  399.2 20.3 %all-to-all-start.2 = ((bf16[8,192,256]{2,1,0:T(8,128)(2,1)}), bf16[8,192,256]{2,1,0:T(8,128)(2,1)}, u32[]{:S(2)}, u32[]{:S(2)}) async-start(bf16[8,192,256]{2,1,0:T(8,128)(2,1)} %maximum_select_fusion.18), calls=%async_computation.2 | async-start | bytes 1572864 | tf_op jit(solution)/shard_map/all_to_all | solution.py:422
  411.4 16.2 %collective-permute-start.55 = (bf16[2,8,64,1280]{3,2,1,0:T(8,128)(2,1)}, bf16[2,8,64,1280]{3,2,1,0:T(8,128)(2,1)}, u32[]{:S(2)}, u32[]{:S(2)}) collective-permute-start(bf16[2,8,64,1280]{3,2,1,0:T(8,128)(2,1)} %maximum_select_fusion.7), channel_id=1, source_target_pairs={{0,1},{1,0},{2,3},{3,2},{4,5},{5,4},{6,7},{7,6},{8,9},{9,8},{10,11... | collective-permute-start | bytes 7864328 | tf_op jit(solution)/shard_map/ppermute | solution.py:383
  441.2 17.8 %collective-permute-start.46 = (bf16[2,32,2048]{2,1,0:T(8,128)(2,1)S(1)}, bf16[2,32,2048]{2,1,0:T(8,128)(2,1)S(1)}, u32[]{:S(2)}, u32[]{:S(2)}) collective-permute-start(bf16[2,32,2048]{2,1,0:T(8,128)(2,1)S(1)} %pad_maximum_fusion.63), channel_id=1, source_target_pairs={{0,4},{4,0},{1,5},{5,1},{2,6},{6,2},{3,7},{7,3},{8,12},{12,8},{9,1... | collective-permute-start | bytes 786440 | tf_op jit(solution)/shard_map/ppermute | solution.py:383
  442.8 18.5 %collective-permute-start.43 = (bf16[2,32,2048]{2,1,0:T(8,128)(2,1)S(1)}, bf16[2,32,2048]{2,1,0:T(8,128)(2,1)S(1)}, u32[]{:S(2)}, u32[]{:S(2)}) collective-permute-start(bf16[2,32,2048]{2,1,0:T(8,128)(2,1)S(1)} %pad_maximum_fusion.62), channel_id=1, source_target_pairs={{0,8},{8,0},{1,9},{9,1},{2,10},{10,2},{3,11},{11,3},{4,12},{12,4},... | collective-permute-start | bytes 786440 | tf_op jit(solution)/shard_map/ppermute | solution.py:383
  443.5 17.0 %collective-permute-start.40 = (bf16[2,32,2048]{2,1,0:T(8,128)(2,1)S(1)}, bf16[2,32,2048]{2,1,0:T(8,128)(2,1)S(1)}, u32[]{:S(2)}, u32[]{:S(2)}) collective-permute-start(bf16[2,32,2048]{2,1,0:T(8,128)(2,1)S(1)} %pad_maximum_fusion.61), channel_id=1, source_target_pairs={{0,2},{2,0},{1,3},{3,1},{4,6},{6,4},{5,7},{7,5},{8,10},{10,8},{9,1... | collective-permute-start | bytes 786440 | tf_op jit(solution)/shard_map/ppermute | solution.py:383
  450.4 32.0 %collective-permute-start.53 = (bf16[4,32,2048]{2,1,0:T(8,128)(2,1)S(1)}, bf16[4,32,2048]{2,1,0:T(8,128)(2,1)S(1)}, u32[]{:S(2)}, u32[]{:S(2)}) collective-permute-start(bf16[4,32,2048]{2,1,0:T(8,128)(2,1)S(1)} %pad_maximum_fusion.44), channel_id=1, source_target_pairs={{0,4},{4,0},{1,5},{5,1},{2,6},{6,2},{3,7},{7,3},{8,12},{12,8},{9,1... | collective-permute-start | bytes 1572872 | tf_op jit(solution)/shard_map/ppermute | solution.py:383
  458.1 24.0 %collective-permute-start.50 = (bf16[4,32,2048]{2,1,0:T(8,128)(2,1)S(1)}, bf16[4,32,2048]{2,1,0:T(8,128)(2,1)S(1)}, u32[]{:S(2)}, u32[]{:S(2)}) collective-permute-start(bf16[4,32,2048]{2,1,0:T(8,128)(2,1)S(1)} %pad_maximum_fusion.43), channel_id=1, source_target_pairs={{0,8},{8,0},{1,9},{9,1},{2,10},{10,2},{3,11},{11,3},{4,12},{12,4},... | collective-permute-start | bytes 1572872 | tf_op jit(solution)/shard_map/ppermute | solution.py:383
  460.5 21.4 %collective-permute-start.47 = (bf16[4,32,2048]{2,1,0:T(8,128)(2,1)S(1)}, bf16[4,32,2048]{2,1,0:T(8,128)(2,1)S(1)}, u32[]{:S(2)}, u32[]{:S(2)}) collective-permute-start(bf16[4,32,2048]{2,1,0:T(8,128)(2,1)S(1)} %pad_maximum_fusion.42), channel_id=1, source_target_pairs={{0,2},{2,0},{1,3},{3,1},{4,6},{6,4},{5,7},{7,5},{8,10},{10,8},{9,1... | collective-permute-start | bytes 1572872 | tf_op jit(solution)/shard_map/ppermute | solution.py:383
  547.6 159.6 %collective-permute-start.152 = (bf16[2,160,2048]{2,1,0:T(8,128)(2,1)}, bf16[2,160,2048]{2,1,0:T(8,128)(2,1)}, u32[]{:S(2)}, u32[]{:S(2)}) collective-permute-start(bf16[2,160,2048]{2,1,0:T(8,128)(2,1)} %dynamic-slice_bitcast_fusion.3), channel_id=1, source_target_pairs={{0,1},{1,0},{2,3},{3,2},{4,5},{5,4},{6,7},{7,6},{8,9},{9,8},{10,11... | collective-permute-start | bytes 3932168 | tf_op jit(solution)/shard_map/ppermute | solution.py:383
  549.3 268.8 %collective-permute-start.150 = (bf16[2,8,64,1280]{3,2,1,0:T(8,128)(2,1)}, bf16[2,8,64,1280]{3,2,1,0:T(8,128)(2,1)}, u32[]{:S(2)}, u32[]{:S(2)}) collective-permute-start(bf16[2,8,64,1280]{3,2,1,0:T(8,128)(2,1)} %dynamic-slice_bitcast_fusion.1), channel_id=1, source_target_pairs={{0,1},{1,0},{2,3},{3,2},{4,5},{5,4},{6,7},{7,6},{8,9},{9,8},{10,11... | collective-permute-start | bytes 7864328 | tf_op jit(solution)/shard_map/ppermute | solution.py:383
  636.2 28.3 %collective-permute-start.113 = (bf16[1,32,2048]{2,1,0:T(8,128)(2,1)S(1)}, bf16[1,32,2048]{2,1,0:T(8,128)(2,1)S(1)}, u32[]{:S(2)}, u32[]{:S(2)}) collective-permute-start(bf16[1,32,2048]{2,1,0:T(8,128)(2,1)S(1)} %slice.1075), channel_id=1, source_target_pairs={{0,2},{2,0},{1,3},{3,1},{4,6},{6,4},{5,7},{7,5},{8,10},{10,8},{9,1... | collective-permute-start | bytes 393224 | tf_op jit(solution)/shard_map/ppermute | solution.py:383
  636.9 27.4 %collective-permute-start.110 = (bf16[1,32,2048]{2,1,0:T(8,128)(2,1)S(1)}, bf16[1,32,2048]{2,1,0:T(8,128)(2,1)S(1)}, u32[]{:S(2)}, u32[]{:S(2)}) collective-permute-start(bf16[1,32,2048]{2,1,0:T(8,128)(2,1)S(1)} %slice.1069), channel_id=1, source_target_pairs={{0,4},{4,0},{1,5},{5,1},{2,6},{6,2},{3,7},{7,3},{8,12},{12,8},{9,1... | collective-permute-start | bytes 393224 | tf_op jit(solution)/shard_map/ppermute | solution.py:383
  663.4 19.3 %collective-permute-start.69 = (bf16[1,32,2048]{2,1,0:T(8,128)(2,1)}, bf16[1,32,2048]{2,1,0:T(8,128)(2,1)}, u32[]{:S(2)}, u32[]{:S(2)}) collective-permute-start(bf16[1,32,2048]{2,1,0:T(8,128)(2,1)} %slice.1024), channel_id=1, source_target_pairs={{0,8},{8,0},{1,9},{9,1},{2,10},{10,2},{3,11},{11,3},{4,12},{12,4},... | collective-permute-start | bytes 393224 | tf_op jit(solution)/shard_map/ppermute | solution.py:383
  664.3 21.9 %collective-permute-start.72 = (bf16[1,32,2048]{2,1,0:T(8,128)(2,1)}, bf16[1,32,2048]{2,1,0:T(8,128)(2,1)}, u32[]{:S(2)}, u32[]{:S(2)}) collective-permute-start(bf16[1,32,2048]{2,1,0:T(8,128)(2,1)} %slice.1030), channel_id=1, source_target_pairs={{0,4},{4,0},{1,5},{5,1},{2,6},{6,2},{3,7},{7,3},{8,12},{12,8},{9,1... | collective-permute-start | bytes 393224 | tf_op jit(solution)/shard_map/ppermute | solution.py:383
  664.5 24.9 %collective-permute-start.75 = (bf16[1,32,2048]{2,1,0:T(8,128)(2,1)}, bf16[1,32,2048]{2,1,0:T(8,128)(2,1)}, u32[]{:S(2)}, u32[]{:S(2)}) collective-permute-start(bf16[1,32,2048]{2,1,0:T(8,128)(2,1)} %slice.1036), channel_id=1, source_target_pairs={{0,2},{2,0},{1,3},{3,1},{4,6},{6,4},{5,7},{7,5},{8,10},{10,8},{9,1... | collective-permute-start | bytes 393224 | tf_op jit(solution)/shard_map/ppermute | solution.py:383
  678.6 19.6 %all-to-all-start.8 = ((f32[32,1,64]{2,1,0:T(1,128)}), f32[32,1,64]{2,1,0:T(1,128)S(1)}, u32[]{:S(2)}, u32[]{:S(2)}) async-start(f32[32,1,64]{2,1,0:T(1,128)} %all_to_all.47), calls=%async_computation.8 | async-start | bytes 32768 | tf_op jit(solution)/shard_map/all_to_all | solution.py:432
  698.2 43.1 %all-to-all-start.4 = ((bf16[8,192,256]{2,1,0:T(8,128)(2,1)}), bf16[8,192,256]{2,1,0:T(8,128)(2,1)}, u32[]{:S(2)}, u32[]{:S(2)}) async-start(bf16[8,192,256]{2,1,0:T(8,128)(2,1)} %bitcast.562), calls=%async_computation.4 | async-start | bytes 1572864 | tf_op jit(solution)/shard_map/all_to_all | solution.py:422
  704.7 35.6 %collective-permute-start.76 = (bf16[96,2048]{1,0:T(8,128)(2,1)}, bf16[96,2048]{1,0:T(8,128)(2,1)S(1)}, u32[]{:S(2)}, u32[]{:S(2)}) collective-permute-start(bf16[96,2048]{1,0:T(8,128)(2,1)} %get-tuple-element.87), channel_id=1, source_target_pairs={{0,16},{16,0},{1,17},{17,1},{2,18},{18,2},{3,19},{19,3},{4,20},{20... | collective-permute-start | bytes 1179656 | tf_op jit(solution)/shard_map/ppermute | solution.py:383
  711.3 41.5 %collective-permute-start.153 = (bf16[160,2048]{1,0:T(8,128)(2,1)}, bf16[160,2048]{1,0:T(8,128)(2,1)}, u32[]{:S(2)}, u32[]{:S(2)}) collective-permute-start(bf16[160,2048]{1,0:T(8,128)(2,1)} %dynamic-slice_bitcast_fusion.6), channel_id=1, source_target_pairs={{0,16},{16,0},{1,17},{17,1},{2,18},{18,2},{3,19},{19,3},{4,20},{20... | collective-permute-start | bytes 1966088 | tf_op jit(solution)/shard_map/ppermute | solution.py:383
  714.2 265.2 %collective-permute-start.137 = (bf16[2,2,2,2,64,2048]{5,4,3,2,1,0:T(8,128)(2,1)}, bf16[2,2,2,2,64,2048]{5,4,3,2,1,0:T(8,128)(2,1)}, u32[]{:S(2)}, u32[]{:S(2)}) collective-permute-start(bf16[2,2,2,2,64,2048]{5,4,3,2,1,0:T(8,128)(2,1)} %dynamic-slice_bitcast_fusion), channel_id=1, source_target_pairs={{0,1},{1,0},{2,3},{3,2},{4,5},{5,4},{6,7},{7,6},{8,9},{9,8},{10,11... | collective-permute-start | bytes 12582920 | tf_op jit(solution)/shard_map/ppermute | solution.py:383
  818.1 69.2 %collective-permute-start.115 = (bf16[1536,384]{1,0:T(8,128)(2,1)}, bf16[1536,384]{1,0:T(8,128)(2,1)}, u32[]{:S(2)}, u32[]{:S(2)}) collective-permute-start(bf16[1536,384]{1,0:T(8,128)(2,1)} %get-tuple-element.21), channel_id=1, source_target_pairs={{0,1},{1,0},{2,3},{3,2},{4,5},{5,4},{6,7},{7,6},{8,9},{9,8},{10,11... | collective-permute-start | bytes 3538952 | tf_op jit(solution)/shard_map/ppermute | solution.py:383
  824.1 85.8 %collective-permute-start.151 = (bf16[8,64,1280]{2,1,0:T(8,128)(2,1)}, bf16[8,64,1280]{2,1,0:T(8,128)(2,1)S(1)}, u32[]{:S(2)}, u32[]{:S(2)}) collective-permute-start(bf16[8,64,1280]{2,1,0:T(8,128)(2,1)} %dynamic-slice_bitcast_fusion.4), channel_id=1, source_target_pairs={{0,16},{16,0},{1,17},{17,1},{2,18},{18,2},{3,19},{19,3},{4,20},{20... | collective-permute-start | bytes 3932168 | tf_op jit(solution)/shard_map/ppermute | solution.py:383
  825.1 61.6 %all-to-all-start.7 = ((f32[32,1,32]{2,1,0:T(1,128)}), f32[32,1,32]{2,1,0:T(1,128)S(1)}, u32[]{:S(2)}, u32[]{:S(2)}) async-start(f32[32,1,32]{2,1,0:T(1,128)} %copy.160), calls=%async_computation.7 | async-start | bytes 32768 | tf_op jit(solution)/shard_map/all_to_all | solution.py:432
  900.9 90.8 %collective-permute-start.135 = (bf16[2,8,64,768]{3,2,1,0:T(8,128)(2,1)}, bf16[2,8,64,768]{3,2,1,0:T(8,128)(2,1)}, u32[]{:S(2)}, u32[]{:S(2)}) collective-permute-start(bf16[2,8,64,768]{3,2,1,0:T(8,128)(2,1)} %dynamic-slice_bitcast_fusion.2), channel_id=1, source_target_pairs={{0,1},{1,0},{2,3},{3,2},{4,5},{5,4},{6,7},{7,6},{8,9},{9,8},{10,11... | collective-permute-start | bytes 4718600 | tf_op jit(solution)/shard_map/ppermute | solution.py:383
  969.5 21.2 %collective-permute-start.134 = (bf16[96,2048]{1,0:T(8,128)(2,1)}, bf16[96,2048]{1,0:T(8,128)(2,1)S(1)}, u32[]{:S(2)}, u32[]{:S(2)}) collective-permute-start(bf16[96,2048]{1,0:T(8,128)(2,1)} %get-tuple-element.79), channel_id=1, source_target_pairs={{0,16},{16,0},{1,17},{17,1},{2,18},{18,2},{3,19},{19,3},{4,20},{20... | collective-permute-start | bytes 1179656 | tf_op jit(solution)/shard_map/ppermute | solution.py:383
  974.3 72.1 %all-to-all-start.9 = ((bf16[8,64,1280]{2,1,0:T(8,128)(2,1)}), bf16[8,64,1280]{2,1,0:T(8,128)(2,1)S(1)}, u32[]{:S(2)}, u32[]{:S(2)}) async-start(bf16[8,64,1280]{2,1,0:T(8,128)(2,1)} %fusion.15), calls=%async_computation.9 | async-start | bytes 2621440 | tf_op jit(solution)/shard_map/all_to_all | solution.py:422
  985.4 47.4 %collective-permute-start.138 = (bf16[1,2,2,2,64,640]{5,4,3,2,1,0:T(8,128)(2,1)S(1)}, bf16[1,2,2,2,64,640]{5,4,3,2,1,0:T(8,128)(2,1)S(1)}, u32[]{:S(2)}, u32[]{:S(2)}) collective-permute-start(bf16[1,2,2,2,64,640]{5,4,3,2,1,0:T(8,128)(2,1)S(1)} %constant_dynamic-slice_fusion.14), channel_id=1, source_target_pairs={{0,8},{8,0},{1,9},{9,1},{2,10},{10,2},{3,11},{11,3},{4,12},{12,4},... | collective-permute-start | bytes 1966088 | tf_op jit(solution)/shard_map/ppermute | solution.py:383
  987.5 47.6 %collective-permute-start.142 = (bf16[2,1,2,2,64,768]{5,4,3,2,1,0:T(8,128)(2,1)S(1)}, bf16[2,1,2,2,64,768]{5,4,3,2,1,0:T(8,128)(2,1)S(1)}, u32[]{:S(2)}, u32[]{:S(2)}) collective-permute-start(bf16[2,1,2,2,64,768]{5,4,3,2,1,0:T(8,128)(2,1)S(1)} %constant_dynamic-slice_fusion.11), channel_id=1, source_target_pairs={{0,4},{4,0},{1,5},{5,1},{2,6},{6,2},{3,7},{7,3},{8,12},{12,8},{9,1... | collective-permute-start | bytes 2359304 | tf_op jit(solution)/shard_map/ppermute | solution.py:383
  989.1 45.7 %collective-permute-start.146 = (bf16[2,2,1,2,64,640]{5,4,3,2,1,0:T(8,128)(2,1)S(1)}, bf16[2,2,1,2,64,640]{5,4,3,2,1,0:T(8,128)(2,1)S(1)}, u32[]{:S(2)}, u32[]{:S(2)}) collective-permute-start(bf16[2,2,1,2,64,640]{5,4,3,2,1,0:T(8,128)(2,1)S(1)} %constant_dynamic-slice_fusion.8), channel_id=1, source_target_pairs={{0,2},{2,0},{1,3},{3,1},{4,6},{6,4},{5,7},{7,5},{8,10},{10,8},{9,1... | collective-permute-start | bytes 1966088 | tf_op jit(solution)/shard_map/ppermute | solution.py:383
  994.6 74.0 %collective-permute-start.136 = (bf16[8,64,768]{2,1,0:T(8,128)(2,1)}, bf16[8,64,768]{2,1,0:T(8,128)(2,1)}, u32[]{:S(2)}, u32[]{:S(2)}) collective-permute-start(bf16[8,64,768]{2,1,0:T(8,128)(2,1)} %dynamic-slice_bitcast_fusion.5), channel_id=1, source_target_pairs={{0,16},{16,0},{1,17},{17,1},{2,18},{18,2},{3,19},{19,3},{4,20},{20... | collective-permute-start | bytes 2359304 | tf_op jit(solution)/shard_map/ppermute | solution.py:383
  1036.2 43.3 %collective-permute-start.143 = (bf16[2,1,1,2,64,768]{5,4,3,2,1,0:T(8,128)(2,1)}, bf16[2,1,1,2,64,768]{5,4,3,2,1,0:T(8,128)(2,1)}, u32[]{:S(2)}, u32[]{:S(2)}) collective-permute-start(bf16[2,1,1,2,64,768]{5,4,3,2,1,0:T(8,128)(2,1)} %constant_dynamic-slice_fusion.10), channel_id=1, source_target_pairs={{0,2},{2,0},{1,3},{3,1},{4,6},{6,4},{5,7},{7,5},{8,10},{10,8},{9,1... | collective-permute-start | bytes 1179656 | tf_op jit(solution)/shard_map/ppermute | solution.py:383
  1042.4 32.1 %collective-permute-start.140 = (bf16[1,1,1,2,64,640]{5,4,3,2,1,0:T(8,128)(2,1)}, bf16[1,1,1,2,64,640]{5,4,3,2,1,0:T(8,128)(2,1)}, u32[]{:S(2)}, u32[]{:S(2)}) collective-permute-start(bf16[1,1,1,2,64,640]{5,4,3,2,1,0:T(8,128)(2,1)} %constant_dynamic-slice_fusion.12), channel_id=1, source_target_pairs={{0,2},{2,0},{1,3},{3,1},{4,6},{6,4},{5,7},{7,5},{8,10},{10,8},{9,1... | collective-permute-start | bytes 491528 | tf_op jit(solution)/shard_map/ppermute | solution.py:383
  1044.8 30.7 %collective-permute-start.148 = (bf16[1,1,1,2,64,640]{5,4,3,2,1,0:T(8,128)(2,1)}, bf16[1,1,1,2,64,640]{5,4,3,2,1,0:T(8,128)(2,1)}, u32[]{:S(2)}, u32[]{:S(2)}) collective-permute-start(bf16[1,1,1,2,64,640]{5,4,3,2,1,0:T(8,128)(2,1)} %constant_dynamic-slice_fusion.6), channel_id=1, source_target_pairs={{0,4},{4,0},{1,5},{5,1},{2,6},{6,2},{3,7},{7,3},{8,12},{12,8},{9,1... | collective-permute-start | bytes 491528 | tf_op jit(solution)/shard_map/ppermute | solution.py:383
  1070.9 27.4 %all-to-all-start.6 = ((bf16[8,64,768]{2,1,0:T(8,128)(2,1)}), bf16[8,64,768]{2,1,0:T(8,128)(2,1)S(1)}, u32[]{:S(2)}, u32[]{:S(2)}) async-start(bf16[8,64,768]{2,1,0:T(8,128)(2,1)} %fusion.29), calls=%async_computation.6 | async-start | bytes 1572864 | tf_op jit(solution)/shard_map/all_to_all | solution.py:422
  (195 other events, 2476.3 us)

commit v2 on v1

v2 whole, which is shorter than its diff:
```python
import jax
import jax.numpy as jnp
import numpy as np
from jax import lax
from jax.experimental import pallas as pl
from jax.experimental.pallas import tpu as pltpu
from jax.sharding import Mesh, PartitionSpec as P

EPS = 1e-06
AXES = ("b", "h", "p", "q", "r", "c")
CUBE = ("p", "q", "r")
SWAP = [(0, 1), (1, 0)]
LOW = jnp.bfloat16
F32 = jnp.float32
HEAD_DIM = 64
BUCKETS = 32
WINDOW = 1024
BLK = 256
FAR = float(2**30)
NT = (((1,), (1,)), ((), ()))
NN = (((1,), (0,)), ((), ()))
DIAGS = 2 * (WINDOW // BLK) + 1
MID = WINDOW // BLK
PAD_LANE = 16
LINE = (DIAGS + 1) * BLK
FORWARD_COST = 1
BACKWARD_COST = 1


def dot(a, b, dims=NN):
    return lax.dot_general(a, b, dims, preferred_element_type=jnp.float32)


def fill_rows(table, own, other, rows, targets):
    pieces = own.shape[0] // rows
    for side, src in enumerate((own, other)):
        for i in range(pieces):
            at = pl.multiple_of(table[side * pieces + i], rows)
            col = 0
            for dst in targets:
                wide = dst.shape[-1]
                dst[pl.ds(at, rows), :] = src[i * rows : (i + 1) * rows, col : col + wide]
                col += wide


def drain_rows(table, src, own, other, rows, col):
    pieces = own.shape[0] // rows
    wide = src.shape[-1]
    for side, dst in enumerate((own, other)):
        for i in range(pieces):
            at = pl.multiple_of(table[side * pieces + i], rows)
            dst[i * rows : (i + 1) * rows, col : col + wide] = src[pl.ds(at, rows), :]


def make_tiles(line, tiles):
    strip = jnp.broadcast_to(line[...], (8, LINE))
    strip = pltpu.roll(strip, 0, 1, stride=1, stride_axis=0)
    for g in range(BLK // 8):
        moved = strip if g == 0 else pltpu.roll(strip, 8 * g, 1)
        for d in range(DIAGS):
            first = BLK * (DIAGS - d)
            tiles[d, 8 * g : 8 * g + 8, :] = moved[:, first : first + BLK]
    tiles[DIAGS + 1] = jnp.full((BLK, BLK), -FAR, jnp.float32)


def sum_tiles(tiles, line):
    total = jnp.zeros((8, LINE), jnp.float32)
    edge = jnp.zeros((8, BLK), jnp.float32)
    for g in range(BLK // 8):
        parts = [tiles[d, 8 * g : 8 * g + 8, :] for d in reversed(range(DIAGS))]
        strip = jnp.concatenate([edge] + parts, axis=1)
        total = total + (strip if g == 0 else pltpu.roll(strip, LINE - 8 * g, 1))
    out = total[0:1]
    for r in range(1, 8):
        out = out + pltpu.roll(total[r : r + 1], LINE - r, 1)
    line[...] = out


def make_own_tile(key_more, tiles, at):
    rows = lax.broadcasted_iota(jnp.int32, (BLK, BLK), 0)
    cols = lax.broadcasted_iota(jnp.int32, (BLK, BLK), 1)
    gone = key_more[pl.ds(at, BLK), PAD_LANE : PAD_LANE + 1].astype(jnp.float32)
    tiles[DIAGS] = tiles[MID] + jnp.where(rows == cols, 0.0, gone)


def half_of(n):
    lanes = lax.broadcasted_iota(jnp.int32, (BLK, 2 * HEAD_DIM), 1)
    return (lanes < HEAD_DIM) if n == 0 else (lanes >= HEAD_DIM)


def build_pairs(n, q, k, query_more, key_more, qx, kx):
    here = half_of(n)
    lanes = lax.broadcasted_iota(jnp.int32, (BLK, 2 * HEAD_DIM), 1)
    mark = jnp.where(lanes % HEAD_DIM == PAD_LANE, 1.0, 0.0).astype(jnp.bfloat16)

    def fill_q(i, _):
        rows = pl.ds(pl.multiple_of(i * BLK, BLK), BLK)
        more = query_more[rows, :]
        qx[0, rows, :] = jnp.where(here, q[rows, :], more)
        qx[1, rows, :] = jnp.where(here, q[rows, :], more + mark)
        return 0

    def fill_k(i, _):
        rows = pl.ds(pl.multiple_of(i * BLK, BLK), BLK)
        kx[rows, :] = jnp.where(here, k[rows, :], key_more[rows, :])
        return 0

    lax.fori_loop(0, q.shape[0] // BLK, fill_q, 0)
    lax.fori_loop(0, k.shape[0] // BLK, fill_k, 0)


def pair_of(j, first, end, here):
    out = []
    for m in range(2):
        block = first + 2 * j + m
        there = block < end
        block = jnp.minimum(block, end - 1)
        same = (there & (block == here)).astype(jnp.int32)
        away = block - here + MID
        tile = jnp.where(there, jnp.where(block == here, DIAGS, away), DIAGS + 1)
        out.append((pl.ds(pl.multiple_of(block * BLK, BLK), BLK), same, away, tile))
    return out


def forward_kernel(local, halo, n, *refs):
    if local:
        pos, pos_out, rng, own, other, query_more, key_more, diag, *refs = refs
        before, refs = refs[:n], refs[n:]
        outs, refs = (refs[:2], refs[2:]) if n else ((), refs)
        mixed_t, lse, q, k, v, qx, kx, vt, tiles, *joined = refs
        fill_rows(pos, own, other, own.shape[0] // 48, (q, k, v))
    else:
        rng, q, k, v, query_more, key_more, diag, *refs = refs
        before, refs = refs[:n], refs[n:]
        joined, refs = refs[:n], refs[n:]
        mixed_t, lse, qx, kx, vt, tiles = refs
    make_tiles(diag, tiles)
    build_pairs(n, q, k, query_more, key_more, qx, kx)
    cols = slice(n * HEAD_DIM, (n + 1) * HEAD_DIM)

    def turn(i, _):
        rows = pl.ds(pl.multiple_of(i * BLK, BLK), BLK)
        vt[:, rows] = v[rows, :].T[cols]
        return 0

    lax.fori_loop(0, v.shape[0] // BLK, turn, 0)

    def query_block(i, _):
        at = pl.multiple_of(i * BLK, BLK)
        rows = pl.ds(at, BLK)
        here = i + halo // BLK
        first, end = rng[0, i], rng[1, i]
        make_own_tile(key_more, tiles, pl.multiple_of(here * BLK, BLK))

        def key_blocks(j, carry):
            top, total, acc = carry
            both = pair_of(j, first, end, here)
            s = [
                dot(kx[span, :], qx[1 - same, rows, :], NT) + tiles[tile]
                for span, same, _, tile in both
            ]
            high = jnp.max(jnp.maximum(s[0], s[1]), axis=0, keepdims=True)
            high = jnp.maximum(top, high)
            p = [jnp.exp(part - high) for part in s]
            shrink = jnp.exp(top - high)
            total = total * shrink + jnp.sum(p[0] + p[1], axis=0, keepdims=True)
            acc = acc * shrink
            for part, (span, _, _, _) in zip(p, both):
                acc = acc + dot(vt[:, span], part.astype(jnp.bfloat16))
            return high, total, acc

        start = (
            jnp.full((1, BLK), -1e30, jnp.float32),
            jnp.zeros((1, BLK), jnp.float32),
            jnp.zeros((HEAD_DIM, BLK), jnp.float32),
        )
        top, total, acc = lax.fori_loop(0, (end - first + 1) // 2, key_blocks, start)
        mixed_t[:, rows] = acc / total
        lse[:, rows] = top + jnp.log(total)
        if n:
            whole = jnp.concatenate([before[0][:, rows], mixed_t[:, rows]], axis=0)
            joined[0][rows, :] = whole.T.astype(jnp.bfloat16)
        return 0

    lax.fori_loop(0, q.shape[0] // BLK, query_block, 0)
    if local and n:
        drain_rows(pos_out, joined[0], *outs, outs[0].shape[0] // 16, 0)


def backward_kernel(local, halo, n, *refs):
    if local:
        pos, pos_out, rng, own, other, query_more, key_more, diag, g_own, g_other, mixed_t, lse, *refs = refs
        before, refs = refs[: 3 * n], refs[3 * n :]
        outs, refs = refs[: 3 - n], refs[3 - n :]
        d_diag, q, k, v, g, qx, kx, vx, gx, kt, tiles, dk, dv, dtiles, *whole = refs
        fill_rows(pos, own, other, own.shape[0] // 48, (q, k, v))
        fill_rows(pos_out, g_own, g_other, g_own.shape[0] // 16, (g,))
        dq_out, dk_out, dv_out = whole if n else outs
    else:
        rng, q, k, v, query_more, key_more, diag, g, mixed_t, lse, *refs = refs
        before, refs = refs[: 3 * n], refs[3 * n :]
        dq_out, dk_out, dv_out, d_diag, qx, kx, vx, gx, kt, tiles, dk, dv, dtiles = refs
    make_tiles(diag, tiles)
    build_pairs(n, q, k, query_more, key_more, qx, kx)
    blank = jnp.zeros((BLK, 2 * HEAD_DIM), jnp.bfloat16)
    mine = half_of(n)
    cols = slice(n * HEAD_DIM, (n + 1) * HEAD_DIM)

    def store(out, slot, rows, part):
        part = part.astype(out.dtype)
        out[rows, :] = jnp.where(mine, part, before[slot][rows, :]) if n else part

    def turn(i, _):
        rows = pl.ds(pl.multiple_of(i * BLK, BLK), BLK)
        kt[:, rows] = k[rows, :].T[cols]
        vx[rows, :] = jnp.where(mine, v[rows, :], blank)
        dk[rows, :] = jnp.zeros((BLK, 2 * HEAD_DIM), jnp.float32)
        dv[rows, :] = jnp.zeros((BLK, 2 * HEAD_DIM), jnp.float32)
        return 0

    def spread_g(i, _):
        rows = pl.ds(pl.multiple_of(i * BLK, BLK), BLK)
        gx[rows, :] = jnp.where(mine, g[rows, :], blank)
        return 0

    lax.fori_loop(0, k.shape[0] // BLK, turn, 0)
    lax.fori_loop(0, q.shape[0] // BLK, spread_g, 0)
    for slot in range(DIAGS):
        dtiles[slot] = jnp.zeros((BLK, BLK), jnp.float32)

    def query_block(i, _):
        at = pl.multiple_of(i * BLK, BLK)
        rows = pl.ds(at, BLK)
        here = i + halo // BLK
        first, end = rng[0, i], rng[1, i]
        make_own_tile(key_more, tiles, pl.multiple_of(here * BLK, BLK))
        turned = g[rows, :].astype(jnp.float32).T[cols] * mixed_t[:, rows]
        delta = jnp.sum(turned, axis=0, keepdims=True)
        level = lse[:, rows]

        def key_blocks(j, acc):
            both = pair_of(j, first, end, here)
            s = [
                dot(kx[span, :], qx[1 - same, rows, :], NT) + tiles[tile]
                for span, same, _, tile in both
            ]
            dp = [dot(vx[span, :], gx[rows, :], NT) for span, _, _, _ in both]
            for m, (span, same, away, _) in enumerate(both):
                p = jnp.exp(s[m] - level)
                ds = (p * (dp[m] - delta)).astype(jnp.bfloat16)
                dtiles[away] += ds.astype(jnp.float32)
                dv[span, :] += dot(p.astype(jnp.bfloat16), gx[rows, :])
                dk[span, :] += dot(ds, qx[0, rows, :])
                acc = acc + dot(kt[:, span], ds)
            return acc

        zero = jnp.zeros((HEAD_DIM, BLK), jnp.float32)
        acc = lax.fori_loop(0, (end - first + 1) // 2, key_blocks, zero)
        empty = jnp.zeros((HEAD_DIM, BLK), jnp.float32)
        store(dq_out, 0, rows, jnp.concatenate([empty, acc] if n else [acc, empty], axis=0).T)
        return 0

    lax.fori_loop(0, q.shape[0] // BLK, query_block, 0)

    sum_tiles(dtiles, d_diag)

    def finish(i, _):
        rows = pl.ds(pl.multiple_of(i * BLK, BLK), BLK)
        store(dk_out, 1, rows, dk[rows, :])
        store(dv_out, 2, rows, dv[rows, :])
        return 0

    lax.fori_loop(0, k.shape[0] // BLK, finish, 0)
    if local and n:
        rows = own.shape[0] // 48
        for col, src in enumerate(whole):
            drain_rows(pos, src, *outs, rows, col * 2 * HEAD_DIM)


def specs(smem, vmem):
    return [pl.BlockSpec(memory_space=pltpu.SMEM)] * smem + [pl.BlockSpec(memory_space=pltpu.VMEM)] * vmem


def costs(length, times):
    return pl.CostEstimate(flops=length * times, bytes_accessed=1 << 16, transcendentals=0)


def attend_forward(local, halo, n, tables, tokens, extras, before):
    length, reach = extras[0].shape[0], extras[1].shape[0]
    both = 2 * HEAD_DIM
    shape = jax.ShapeDtypeStruct
    low = jnp.bfloat16
    outs, scratch, last = [], [], []
    if n:
        outs = [shape((length // 2, both), low)] * 2 if local else [shape((length, both), low)]
    outs = outs + [shape((HEAD_DIM, length), jnp.float32), shape((1, length), jnp.float32)]
    if local:
        scratch = [pltpu.VMEM((length, both), low)] + [pltpu.VMEM((reach, both), low)] * 2
        last = [pltpu.VMEM((length, both), low)] * n
    scratch = scratch + [
        pltpu.VMEM((2, length, both), low),
        pltpu.VMEM((reach, both), low),
        pltpu.VMEM((HEAD_DIM, reach), low),
        pltpu.VMEM((DIAGS + 2, BLK, BLK), jnp.float32),
    ]
    return pl.pallas_call(
        lambda *refs: forward_kernel(local, halo, n, *refs),
        out_shape=outs,
        in_specs=specs(len(tables), len(tokens) + len(extras) + len(before)),
        out_specs=specs(0, len(outs)),
        scratch_shapes=scratch + last,
        compiler_params=pltpu.CompilerParams(vmem_limit_bytes=56 << 20),
        cost_estimate=costs(length, FORWARD_COST),
    )(*tables, *tokens, *extras, *before)


def attend_backward(local, halo, n, tables, tokens, extras, grads, saved, before):
    length, reach = extras[0].shape[0], extras[1].shape[0]
    both = 2 * HEAD_DIM
    shape = jax.ShapeDtypeStruct
    low = jnp.bfloat16
    kind = low if local else jnp.float32
    d_diag = shape((1, LINE), jnp.float32)
    scratch, last = [], []
    if local and n:
        outs = [shape((length // 2, 3 * both), low)] * 2 + [d_diag]
    else:
        outs = [shape((length, both), kind)] + [shape((reach, both), kind)] * 2 + [d_diag]
    if local:
        scratch = [pltpu.VMEM((size, both), low) for size in (length, reach, reach, length)]
        last = [pltpu.VMEM((size, both), low) for size in (length, reach, reach)] * n
    scratch = scratch + [
        pltpu.VMEM((2, length, both), low),
        pltpu.VMEM((reach, both), low),
        pltpu.VMEM((reach, both), low),
        pltpu.VMEM((length, both), low),
        pltpu.VMEM((HEAD_DIM, reach), low),
        pltpu.VMEM((DIAGS + 2, BLK, BLK), jnp.float32),
        pltpu.VMEM((reach, both), jnp.float32),
        pltpu.VMEM((reach, both), jnp.float32),
        pltpu.VMEM((DIAGS, BLK, BLK), jnp.float32),
    ]
    operands = (*tokens, *extras, *grads, *saved, *before)
    return pl.pallas_call(
        lambda *refs: backward_kernel(local, halo, n, *refs),
        out_shape=outs,
        in_specs=specs(len(tables), len(operands)),
        out_specs=specs(0, len(outs)),
        scratch_shapes=scratch + last,
        compiler_params=pltpu.CompilerParams(vmem_limit_bytes=60 << 20),
        cost_estimate=costs(length, BACKWARD_COST),
    )(*tables, *operands)


def bucket_line(bucket_table):
    edge = jnp.full((2 * BLK,), -1, jnp.int32)
    wide = jnp.concatenate([edge, bucket_table, edge])[::-1]
    return wide[BLK - 1 : BLK - 1 + LINE]


def query_ranges(segments, halo):
    reach = segments.shape[0]
    first = halo + BLK * jnp.arange((reach - 2 * halo) // BLK, dtype=jnp.int32)
    last = first + BLK - 1
    cut = segments.reshape(-1, BLK)[halo // BLK : (reach - halo) // BLK]
    low = jnp.sum(segments[None, :] < cut[:, :1], axis=1)
    high = jnp.sum(segments[None, :] <= cut[:, -1:], axis=1)
    low = jnp.maximum(low, jnp.maximum(first - WINDOW + 1, 0))
    high = jnp.minimum(high, jnp.minimum(last + WINDOW, reach))
    return jnp.stack([low // BLK, (high + BLK - 1) // BLK]).astype(jnp.int32)


def barring_lanes(codes, halo):
    lanes = jnp.arange(2 * HEAD_DIM, dtype=jnp.int32) % HEAD_DIM
    segments = (codes >> 1)[:, None]
    key_more = jnp.where(lanes == segments, 1.0, 0.0)
    key_more = jnp.where((lanes == PAD_LANE) & ((codes & 1) == 0)[:, None], -FAR, key_more)
    mine = segments[halo : codes.shape[0] - halo]
    query_more = jnp.where((lanes < PAD_LANE) & (lanes != mine), -FAR, 0.0)
    return query_more.astype(jnp.bfloat16), key_more.astype(jnp.bfloat16)


def swap(value, axis):
    return lax.ppermute(value, axis, SWAP)


def pick(value, index, axis=0):
    return lax.dynamic_index_in_dim(value, index, axis, keepdims=False)


def both(mine, theirs, bit, axis, joined=False):
    put = jnp.concatenate if joined else jnp.stack
    return jnp.where(bit == 0, put([mine, theirs], axis), put([theirs, mine], axis))


def matmul(left, right, dims=NN):
    return lax.dot_general(left, right, dims, preferred_element_type=F32)


TN = (((0,), (0,)), ((), ()))


def fence(*values):
    return lax.optimization_barrier(values)


def cut_kernel(order, wide, src, out):
    for m in range(8):
        for j, o in enumerate(order):
            first = (o * 8 + m) * wide
            out[m, :, j * wide : (j + 1) * wide] = src[:, first : first + wide]


def cut_columns(matrix, order, wide):
    rows = matrix.shape[0]
    return pl.pallas_call(
        lambda src, out: cut_kernel(order, wide, src, out),
        out_shape=jax.ShapeDtypeStruct((8, rows, len(order) * wide), matrix.dtype),
        in_specs=specs(0, 1),
        out_specs=specs(0, 1)[0],
        compiler_params=pltpu.CompilerParams(vmem_limit_bytes=32 << 20),
        cost_estimate=pl.CostEstimate(flops=0, bytes_accessed=4 * matrix.size, transcendentals=0),
    )(matrix)


def join_kernel(order, wide, src, out):
    for m in range(8):
        for j, o in enumerate(order):
            first = (o * 8 + m) * wide
            part = src[m, :, j * wide : (j + 1) * wide]
            out[:, first : first + wide] = part.astype(jnp.float32)


def join_columns(chunks, order, wide):
    rows = chunks.shape[1]
    return pl.pallas_call(
        lambda src, out: join_kernel(order, wide, src, out),
        out_shape=jax.ShapeDtypeStruct((rows, len(order) * 8 * wide), F32),
        in_specs=specs(0, 1),
        out_specs=specs(0, 1)[0],
        compiler_params=pltpu.CompilerParams(vmem_limit_bytes=32 << 20),
        cost_estimate=pl.CostEstimate(flops=0, bytes_accessed=6 * chunks.size, transcendentals=0),
    )(chunks)


def distance(k, i):
    mask = 0
    for step in range(3):
        if i >> step & 1:
            mask |= 4 >> (k + step) % 3
    return mask


def join_kernel_rows(counts, *refs):
    total = sum(counts)
    sources, outs, sems = refs[:total], refs[total : total + len(counts)], refs[-1]
    copies = []
    for out, count in zip(outs, counts):
        at = 0
        for src in sources[len(copies) : len(copies) + count]:
            rows = src.shape[0]
            copies.append(pltpu.make_async_copy(src, out.at[pl.ds(at, rows)], sems.at[len(copies)]))
            at += rows
    for copy in copies:
        copy.start()
    for copy in copies:
        copy.wait()


def join_rows(*lists):
    counts = [len(pieces) for pieces in lists]
    pieces = [piece for listed in lists for piece in listed]
    shapes = [
        jax.ShapeDtypeStruct((sum(p.shape[0] for p in listed),) + listed[0].shape[1:], listed[0].dtype)
        for listed in lists
    ]
    outs = pl.pallas_call(
        lambda *refs: join_kernel_rows(counts, *refs),
        out_shape=shapes,
        in_specs=[pl.BlockSpec(memory_space=pl.ANY)] * len(pieces),
        out_specs=specs(0, len(lists)),
        scratch_shapes=[pltpu.SemaphoreType.DMA((len(pieces),))],
        compiler_params=pltpu.CompilerParams(vmem_limit_bytes=32 << 20),
        cost_estimate=pl.CostEstimate(
            flops=0, bytes_accessed=4 * sum(p.size for p in pieces), transcendentals=0
        ),
    )(*pieces)
    return list(outs)


def gather_send(parts, step):
    return [swap(parts[k], CUBE[(k + step) % 3]) for k in range(3)]


def gather_join(parts, wires):
    return join_rows(*([a, b] for a, b in zip(parts, wires)))


def gather_step(parts, step):
    return gather_join(parts, gather_send(parts, step))


def reduce_send(parts):
    half = parts[0].shape[0] // 2
    step = half.bit_length() - 1
    return [swap(parts[k][half:], CUBE[(k + step) % 3]) for k in range(3)]


def reduce_add(parts, wires):
    half = parts[0].shape[0] // 2
    return [(a[:half].astype(F32) + b.astype(F32)).astype(LOW) for a, b in zip(parts, wires)]


def reduce_step(parts, step):
    return reduce_add(parts, reduce_send(parts))


def thirds(rows):
    third = rows.shape[0] // 3
    return [rows[k * third : (k + 1) * third][None] for k in range(3)]


def gathered_rows(parts):
    return join_rows([part.reshape(-1, part.shape[-1]) for part in parts])[0]


def to_parts(rows):
    return list(rows.reshape(3, 8, -1, rows.shape[-1]))


def own_rows(parts):
    return jnp.concatenate([part[0] for part in parts], axis=0).astype(F32)


def exchange(chunks):
    return lax.all_to_all(chunks, CUBE, 0, 0)


def move_kernel(gather, rows, table, src, out):
    for n in range(src.shape[0] // rows):
        fixed = pl.ds(n * rows, rows)
        moved = pl.ds(pl.multiple_of(table[n], rows), rows)
        if gather:
            out[fixed, :] = src[moved, :]
        else:
            out[moved, :] = src[fixed, :]


def move_rows(table, src, gather):
    rows = src.shape[0] // table.shape[0]
    return pl.pallas_call(
        lambda *refs: move_kernel(gather, rows, *refs),
        out_shape=jax.ShapeDtypeStruct(src.shape, src.dtype),
        in_specs=specs(1, 1),
        out_specs=specs(0, 1)[0],
        compiler_params=pltpu.CompilerParams(vmem_limit_bytes=32 << 20),
        cost_estimate=pl.CostEstimate(flops=0, bytes_accessed=4 * src.size, transcendentals=0),
    )(table, src)


def tell_all(line):
    count = lax.axis_size(AXES)
    return lax.all_to_all(jnp.broadcast_to(line, (count,) + line.shape), AXES, 0, 0)


def sum_line(line):
    count = lax.axis_size(AXES)
    return jnp.sum(lax.all_to_all(line.reshape(count, -1), AXES, 0, 0), axis=0)


def wire_halves(shard):
    if lax.axis_size("b") == 1:
        return swap(shard, "h")
    return lax.all_gather(shard, ("b", "h"), axis=0)


def wire_halves_twice(shard):
    if lax.axis_size("b") == 1:
        return swap(shard[:4], "h"), swap(shard[4:], "h")
    return (wire_halves(shard),)


def light_distance(part, i):
    return (i & 1) * 4 | (i >> 1 & 1) * (2, 1)[part] | (i >> 2 & 1) * (1, 2)[part]


def light_send(parts):
    half = parts[0].shape[0] // 2
    axes = {4: ("r", "q"), 2: ("q", "r"), 1: ("p", "p")}[half]
    return [swap(part[half:], axis) for part, axis in zip(parts, axes)]


def by_rows_kernel(src, out):
    count = src.shape[0] // 48
    for part in range(2):
        for i in range(8):
            mask = light_distance(part, i)
            for j in range(3):
                row = 3 * part + j
                k = row // 2
                place = [distance(k, e) for e in range(8)].index(mask)
                first = ((k * 8 + place) * 2 + row % 2) * count
                at = ((part * 8 + i) * 3 + j) * count
                out[at : at + count, :] = src[first : first + count, :]


def by_rows_of_light(rows):
    return pl.pallas_call(
        by_rows_kernel,
        out_shape=jax.ShapeDtypeStruct(rows.shape, rows.dtype),
        in_specs=specs(0, 1),
        out_specs=specs(0, 1)[0],
        compiler_params=pltpu.CompilerParams(vmem_limit_bytes=32 << 20),
        cost_estimate=pl.CostEstimate(flops=0, bytes_accessed=1 << 16, transcendentals=0),
    )(rows)


def by_light_kernel(table, src, out):
    rows, wide = src.shape[0] // 8, src.shape[1] // 2
    for part in range(2):
        for i in range(8):
            at = pl.ds(pl.multiple_of((table[0] ^ light_distance(part, i)) * rows, rows), rows)
            to = (part * 8 + i) * wide
            out[:, to : to + wide] = src[at, part * wide : (part + 1) * wide]


def by_light_distance(chunks, at):
    tall, wide = chunks.shape
    return pl.pallas_call(
        by_light_kernel,
        out_shape=jax.ShapeDtypeStruct((tall // 8, wide * 8), chunks.dtype),
        in_specs=specs(1, 1),
        out_specs=specs(0, 1)[0],
        compiler_params=pltpu.CompilerParams(vmem_limit_bytes=32 << 20),
        cost_estimate=pl.CostEstimate(flops=0, bytes_accessed=1 << 16, transcendentals=0),
    )(at["cube"][None].astype(jnp.int32), chunks)


def gather_halves(shard):
    return lax.all_gather(shard, ("b", "h"), axis=0)


def scatter_halves(parts):
    return lax.psum_scatter(parts, ("b", "h"), scatter_dimension=0, tiled=False)


def weave_halves(halves, core, at):
    if lax.axis_size("b") > 1:
        return both(halves, core, at["c"], 2)
    count = halves.shape[1]
    halves, core = (v.reshape((-1,) + v.shape[2:]) for v in (halves, core))
    return weave([(halves, None, 0), (core, None, 1)], at, count, True)


def join_halves(shard, wire, at):
    return both(shard, wire, at["h"], 0) if lax.axis_size("b") == 1 else wire


def send_halves(parts, at):
    if lax.axis_size("b") == 1:
        return swap(pick(parts, 1 - at["h"]), "h")
    return lax.psum_scatter(parts.astype(F32), ("b", "h"), scatter_dimension=0, tiled=False)


def add_halves(parts, wire, at):
    if lax.axis_size("b") == 1:
        return pick(parts, at["h"]).astype(F32) + wire.astype(F32)
    return wire


def add_cores(grad, wire, at, axis):
    return (pick(grad, at["c"], axis).astype(F32) + wire.astype(F32)).astype(LOW)


def send_cores(grad, at, axis):
    return swap(pick(grad, 1 - at["c"], axis), "c")


def fetch_out_wide(shard):
    whole = lax.all_gather(shard, AXES, axis=0, tiled=True)
    whole = whole.reshape(2, 8, 2, HEAD_DIM, -1).transpose(1, 0, 2, 3, 4)
    return whole.reshape(-1, whole.shape[-1])


def grad_out_wide(grad):
    grad = grad.reshape(8, 2, 2, HEAD_DIM, -1).transpose(1, 0, 2, 3, 4)
    return lax.psum_scatter(grad.reshape(-1, grad.shape[-1]), AXES, scatter_dimension=0, tiled=True)


def gelu_tanh(value):
    return (
        0.5
        * value
        * (1.0 + jnp.tanh(0.7978845608028654 * (value + 0.044715 * value * value * value)))
    )


def normalize(hidden):
    scale = lax.rsqrt(jnp.mean(hidden * hidden, axis=-1, keepdims=True) + EPS)
    return (hidden * scale, scale)


def norm_back(grad_unit, unit, scale):
    return scale * (grad_unit - unit * jnp.mean(grad_unit * unit, axis=-1, keepdims=True))


def piece_tables(rows, at):
    both_rows = 2 * rows
    third = both_rows // 3
    side, k, i, half = np.meshgrid(range(2), range(3), range(8), range(2), indexing="ij")
    mask = np.vectorize(distance)(k, i)
    row = k * third + half * (third // 2)
    other, row = row // rows, row % rows
    side, other, row, mask = (jnp.asarray(v.reshape(-1), jnp.int32) for v in (side, other, row, mask))
    spread_at = (16 * (at["h"] ^ other) + 2 * (at["cube"] ^ mask) + (at["c"] ^ side)) * rows + row
    side, place, other = np.meshgrid(range(2), range(8), range(2), indexing="ij")
    side, place, other = (jnp.asarray(v.reshape(-1), jnp.int32) for v in (side, place, other))
    chunk_at = (16 * (at["h"] ^ other) + 2 * place + (at["c"] ^ side)) * rows
    k, i = np.meshgrid(range(3), range(8), indexing="ij")
    mask = jnp.asarray(np.vectorize(distance)(k, i).reshape(-1), jnp.int32)
    cube_at = (at["cube"] ^ mask) * both_rows + jnp.asarray(k.reshape(-1) * third, jnp.int32)
    return spread_at, chunk_at, cube_at


def weave_kernel(kinds, by_half, turn, *refs):
    place, sources, out, sems = refs[0], refs[1:-2], refs[-2], refs[-1]
    copies = []
    for src, (half_off, core_off) in zip(sources, kinds):
        core = place[1] ^ core_off
        count = out.shape[1]
        for part in range(src.shape[0] // count):
            half = part
            if by_half and half_off is not None:
                half = place[0] ^ part
            rows_part = src.at[part * count : (part + 1) * count]
            for j in range(2 if turn else 1):
                dst, src_part = out.at[half, :, core], rows_part
                if turn:
                    first = pl.multiple_of((j ^ place[1]) * turn, turn)
                    dst = out.at[half, :, core, :, pl.ds(first, turn)]
                    src_part = rows_part.at[:, :, j * turn : (j + 1) * turn]
                copies.append(pltpu.make_async_copy(src_part, dst, sems.at[len(copies)]))
    for copy in copies:
        copy.start()
    for copy in copies:
        copy.wait()


def weave(pieces, at, count, by_half, turn=0):
    rows, wide = pieces[0][0].shape[1:]
    place = jnp.stack([at["h"], at["c"]]).astype(jnp.int32)
    kinds = [piece[1:] for piece in pieces]
    arrays = [piece[0] for piece in pieces]
    return pl.pallas_call(
        lambda *refs: weave_kernel(kinds, by_half, turn, *refs),
        out_shape=jax.ShapeDtypeStruct((2 if by_half else 1, count, 2, rows, wide), arrays[0].dtype),
        in_specs=specs(1, 0) + [pl.BlockSpec(memory_space=pl.ANY)] * len(arrays),
        out_specs=specs(0, 1)[0],
        scratch_shapes=[pltpu.SemaphoreType.DMA((4 * len(arrays),))],
        compiler_params=pltpu.CompilerParams(vmem_limit_bytes=32 << 20),
        cost_estimate=pl.CostEstimate(flops=0, bytes_accessed=1 << 16, transcendentals=0),
    )(place, *arrays)


def small_line(segment_ids, padding_mask, attention_norm_gain, feed_gain, position_bias):
    codes = (segment_ids * 2 + padding_mask).astype(LOW)
    fields = [codes[0], codes[1], attention_norm_gain, feed_gain, position_bias]
    return jnp.concatenate([jnp.pad(field, (0, 128 - field.shape[0])) for field in fields])


def prepare_kernel(rows, place, lines, buckets, gains, query_more, key_more, diag, rng):
    count = lines.shape[0]
    fields = [lines[:, 128 * i : 128 * (i + 1)].astype(jnp.float32) for i in range(5)]
    codes = jnp.where(place[0] == 0, fields[0], fields[1])
    turned = codes.T
    lanes = lax.broadcasted_iota(jnp.int32, (rows, 2 * HEAD_DIM), 1) % HEAD_DIM
    for dev in range(count):
        code = turned[:rows, dev : dev + 1].astype(jnp.int32)
        segment = code >> 1
        key = jnp.where(lanes == segment, 1.0, 0.0)
        key = jnp.where((lanes == PAD_LANE) & ((code & 1) == 0), -FAR, key)
        query = jnp.where((lanes < PAD_LANE) & (lanes != segment), -FAR, 0.0)
        key_more[dev * rows : (dev + 1) * rows, :] = key.astype(key_more.dtype)
        query_more[dev * rows : (dev + 1) * rows, :] = query.astype(query_more.dtype)
        wide = gains.shape[1] // count
        for i in range(2):
            gains[i : i + 1, dev * wide : (dev + 1) * wide] = fields[2 + i][dev : dev + 1, :wide]
    heads = lax.broadcasted_iota(jnp.int32, fields[4].shape, 1)
    line = buckets[...]
    hot = lax.broadcasted_iota(jnp.int32, (BUCKETS, line.shape[1]), 0) == line
    for n in range(2):
        bias = jnp.sum(jnp.where(heads == 2 * place[1] + n, fields[4], 0.0), axis=1, keepdims=True)
        chosen = jnp.sum(jnp.where(hot, bias, 0.0), axis=0, keepdims=True)
        diag[n : n + 1, :] = jnp.where(line < 0, -FAR, chosen)
    real = lax.broadcasted_iota(jnp.int32, codes.shape, 1) < rows
    segments = codes.astype(jnp.int32) >> 1
    total = count * rows
    starts = [jnp.sum(jnp.where(real & (segments < s), 1.0, 0.0)).astype(jnp.int32) for s in range(1, PAD_LANE)]
    for i in range(total // BLK):
        first, last = i * BLK, i * BLK + BLK - 1
        low, high = jnp.int32(max(first - WINDOW + 1, 0)), jnp.int32(min(last + WINDOW, total))
        for start in starts:
            low = jnp.where(start <= first, jnp.maximum(low, start), low)
            high = jnp.where(start > last, jnp.minimum(high, start), high)
        rng[0, i] = low // BLK
        rng[1, i] = (high + BLK - 1) // BLK


def prepare(lines, buckets, near, lane, rows):
    count = lines.shape[0]
    place = jnp.stack([near, lane]).astype(jnp.int32)
    shape = jax.ShapeDtypeStruct
    total = count * rows
    gains, query_more, key_more, diag, rng = pl.pallas_call(
        lambda *refs: prepare_kernel(rows, *refs),
        out_shape=[
            shape((2, count * HEAD_DIM), F32),
            shape((total, 2 * HEAD_DIM), LOW),
            shape((total, 2 * HEAD_DIM), LOW),
            shape((2, LINE), F32),
            shape((2, total // BLK), jnp.int32),
        ],
        in_specs=specs(1, 2),
        out_specs=specs(0, 4) + specs(1, 0),
        compiler_params=pltpu.CompilerParams(vmem_limit_bytes=32 << 20),
        cost_estimate=pl.CostEstimate(flops=0, bytes_accessed=1 << 16, transcendentals=0),
    )(place, lines, buckets[None])
    return gains, (query_more, key_more), diag, rng


def prepare_wide(lines, buckets, near, lane, rows, halo, at):
    count = lines.shape[0]
    shard = 32 * HEAD_DIM // count
    gain_attn = lines[:, 256 : 256 + shard].reshape(-1).astype(F32)
    gain_feed = lines[:, 384 : 384 + shard].reshape(-1).astype(F32)
    bias_full = lines[:, 512 : 512 + BUCKETS * 32 // count].reshape(BUCKETS, -1).astype(F32)
    codes = pick(jnp.stack([lines[:, :rows], lines[:, 128 : 128 + rows]]).astype(jnp.int32), near)
    rim = jnp.full((halo,), -2, jnp.int32)
    codes = jnp.concatenate([rim, codes.reshape(-1), rim])
    length = 32 * rows
    codes = lax.dynamic_slice_in_dim(codes, at["b"] * length, length + 2 * halo)
    bias_here = pick(bias_full.reshape(BUCKETS, -1, 2), lane, 1)
    hot = buckets[None] == jnp.arange(BUCKETS, dtype=jnp.int32)[:, None]
    diag = jnp.sum(jnp.where(hot[:, None], bias_here[:, :, None], 0.0), axis=0)
    diag = jnp.where(buckets < 0, -FAR, diag)
    return gain_attn, gain_feed, barring_lanes(codes, halo), diag, query_ranges(codes >> 1, halo)


def in_order(pieces, table):
    count = table.shape[0]
    cut = pieces.reshape(count, -1, pieces.shape[-1])
    return jnp.take(cut, jnp.argsort(table), axis=0).reshape(pieces.shape)


def as_pieces(rows, table):
    count = table.shape[0]
    cut = rows.reshape(count, -1, rows.shape[-1])
    return jnp.take(cut, table // cut.shape[1], axis=0).reshape(rows.shape)


def with_sides(rows, halo):
    count = lax.axis_size("b")
    before = lax.ppermute(rows[-halo:], "b", [(i, i + 1) for i in range(count - 1)])
    after_it = lax.ppermute(rows[:halo], "b", [(i + 1, i) for i in range(count - 1)])
    return jnp.concatenate([before, rows, after_it], axis=0)


def add_sides(rows, halo):
    count = lax.axis_size("b")
    after_it = lax.ppermute(rows[:halo], "b", [(i + 1, i) for i in range(count - 1)])
    before = lax.ppermute(rows[-halo:], "b", [(i, i + 1) for i in range(count - 1)])
    mine = rows[halo:-halo]
    return mine.at[-halo:].add(after_it).at[:halo].add(before)


def local(
    layer_input,
    output_cotangent,
    segment_ids,
    padding_mask,
    bucket_table,
    attention_norm_gain,
    stacked_query_key_value,
    attention_out,
    position_bias,
    feed_gain,
    feed_in,
    feed_out,
):
    at = {name: lax.axis_index(name) for name in AXES}
    at["cube"] = 4 * at["p"] + 2 * at["q"] + at["r"]
    blocks = lax.axis_size("b")
    halves = 2 * blocks
    one_block = blocks == 1
    _, rows, width = layer_input.shape
    shard_rows = stacked_query_key_value.shape[0]
    hidden_shard = feed_out.shape[0]
    hidden_here = hidden_shard * halves * 2
    halo = 0 if one_block else WINDOW
    length = 32 * rows
    near = at["h"]
    far = 1 - near
    span = 2 * HEAD_DIM
    side = 3 * span
    lane = 8 * at["c"] + at["cube"]
    expand_order = tuple(range(2 * halves))
    project_order = (0, 2, 4, 1, 3, 5)

    lines = tell_all(small_line(segment_ids, padding_mask, attention_norm_gain, feed_gain, position_bias))
    x_near = pick(layer_input, near)
    x_far = swap(pick(layer_input, far), "h")
    cut = cut_columns(stacked_query_key_value, project_order, span)
    cut_in = cut_columns(feed_in, expand_order, 2 * hidden_shard)
    masked = output_cotangent * padding_mask[..., None].astype(LOW)
    x_far, lines, cut, cut_in, masked, attention_out, feed_out = fence(
        x_far, lines, cut, cut_in, masked, attention_out, feed_out
    )

    cut = exchange(cut)
    x_here = jnp.concatenate([x_near, x_far], axis=0)
    x_parts = gather_step(thirds(x_here), 0)
    buckets = bucket_line(bucket_table)
    spread_at, chunk_at, cube_at = piece_tables(rows, at)
    out_wire = swap(attention_out, "h") if one_block else ()
    x_parts, cut, buckets, spread_at, chunk_at, cube_at, masked, out_wire = fence(
        x_parts, cut, buckets, spread_at, chunk_at, cube_at, masked, out_wire
    )
    project_wire = wire_halves(cut)
    x_parts = gather_step(x_parts, 1)
    x_parts, project_wire, masked, feed_out = fence(x_parts, project_wire, masked, feed_out)
    x_parts = gather_step(x_parts, 2)
    res_far = swap(pick(masked, far), "h")
    if one_block:
        gains_both, barring, diag, rng = prepare(lines, buckets, near, lane, rows)
        gain_attn, gain_feed = gains_both[0], gains_both[1]
        project_pair = join_rows([cut, project_wire])[0]
    else:
        gain_attn, gain_feed, barring, diag, rng = prepare_wide(lines, buckets, near, lane, rows, halo, at)
        project_pair = project_wire.reshape(-1, shard_rows, 2 * side)
    if one_block:
        out_halves = both(attention_out, out_wire, at["h"], 0)
        out_halves = jnp.broadcast_to(out_halves, (8,) + out_halves.shape)
    else:
        out_halves = ()
    x_parts, gain_attn, gain_feed, barring, diag, rng, cut_in, project_pair, out_halves, res_far = fence(
        x_parts, gain_attn, gain_feed, barring, diag, rng, cut_in, project_pair, out_halves, res_far
    )

    project_core = swap(project_pair, "c")
    cut_in = exchange(cut_in)
    gathered = gathered_rows(x_parts)
    gathered, project_core = fence(gathered, project_core)
    gathered_unit, gathered_scale = normalize(gathered.astype(F32))
    normed_one = (gathered_unit * gain_attn).astype(LOW)
    if one_block:
        pieces = [(project_pair, 0, 0), (project_core, 0, 1)]
        project = weave(pieces, at, 8, True, side).reshape(width, -1)
    else:
        shape = (-1, 8, shard_rows, 2 * side)
        project = both(project_pair.reshape(shape), project_core.reshape(shape), at["c"], 2).reshape(width, -1)
        project = jnp.where(
            at["c"] == 0, project, jnp.concatenate([project[:, side:], project[:, :side]], axis=1)
        )
    projected = matmul(normed_one, project).astype(LOW)
    projected, cut_in, masked, out_halves = fence(projected, cut_in, masked, out_halves)
    out_chunks = exchange(out_halves) if one_block else ()
    own, other = projected[:, :side], swap(projected[:, side:], "c")
    res = jnp.concatenate([pick(masked, near), res_far], axis=0)
    res_parts = thirds(res)
    res_wires = gather_send(res_parts, 0)
    own, other = fence(own, other)

    expand_halves = gather_halves(cut_in)
    if one_block:
        tables = (spread_at, chunk_at, rng)
        tokens = (own, other)
    else:
        tables = (rng,)
        ordered = in_order(jnp.concatenate([own, other], axis=0), spread_at)
        sides = with_sides(ordered[:, span:], halo)
        tokens = (ordered[:, :span], sides[:, :span], sides[:, span:])
    extras = [(*barring, diag[n : n + 1]) for n in range(2)]
    first = attend_forward(one_block, halo, 0, tables, tokens, extras[0], ())
    *mixed, mixed_t, level = attend_forward(one_block, halo, 1, tables, tokens, extras[1], first[:1])
    saved = (first, (mixed_t, level))
    if not one_block:
        mixed = jnp.split(as_pieces(mixed[0], chunk_at), 2, axis=0)
    mixed, mixed_other, out_chunks, feed_out, res_wires, expand_halves = fence(
        *mixed, out_chunks, feed_out, res_wires, expand_halves
    )
    down_halves = gather_halves(feed_out)
    mixed_wire = swap(mixed_other, "c")
    out_wire = swap(out_chunks, "c") if one_block else ()
    res_parts = gather_join(res_parts, res_wires)
    mixed, mixed_wire, res_parts, out_wire = fence(mixed, mixed_wire, res_parts, out_wire)
    mixed = both(mixed, mixed_wire, at["c"], 1, joined=True)
    mixed = exchange(mixed.reshape(8, 2 * rows, 2 * span))
    expand_core = swap(expand_halves, "c")
    if one_block:
        pieces = [(out_chunks.reshape(16, HEAD_DIM, width), 0, 0), (out_wire.reshape(16, HEAD_DIM, width), 0, 1)]
        out_full = weave(pieces, at, 16, False).reshape(-1, width)
    else:
        out_full = fetch_out_wide(attention_out)
    mixed, out_full, expand_core = fence(mixed, out_full, expand_core)
    mixed_chunks = mixed.reshape(16 * rows, 2 * span)
    res_wires = gather_send(res_parts, 1)
    mixed = mixed.transpose(1, 0, 2).reshape(2 * rows, -1)
    tokens_here = x_here.astype(F32)
    hidden_one = tokens_here + matmul(mixed, out_full)

    unit_two, scale_two = normalize(hidden_one)
    normed_two = (unit_two * gain_feed).astype(LOW)
    normed_two, mixed = fence(normed_two, mixed)
    parts = gather_step(thirds(normed_two), 0)
    expand = weave_halves(expand_halves, expand_core, at).reshape(width, -1)
    parts, expand, res_wires, down_halves = fence(parts, expand, res_wires, down_halves)
    res_parts = gather_join(res_parts, res_wires)
    down_core = swap(down_halves, "c")
    parts = gather_step(parts, 1)
    (parts,) = fence(parts)
    parts = gather_step(parts, 2)
    res_wires = gather_send(res_parts, 2)
    down = weave_halves(down_halves[:, None], down_core[:, None], at).reshape(hidden_here, width)
    parts, down = fence(parts, down)
    fed = gathered_rows(parts)
    gate_up = matmul(fed, expand)
    gate = gate_up[:, :hidden_here]
    upward = gate_up[:, hidden_here:]
    activated, gelu_pull = jax.vjp(gelu_tanh, gate)
    inner = (activated * upward).astype(LOW)

    inner, res_wires = fence(inner, res_wires)
    res_all = gathered_rows(gather_join(res_parts, res_wires))
    grad_res = res.astype(F32)
    grad_inner = matmul(res_all, down, NT)
    grad_gate = gelu_pull(grad_inner * upward)[0]
    grad_gate_up = jnp.concatenate([grad_gate, grad_inner * activated], axis=1).astype(LOW)
    grad_fed = matmul(grad_gate_up, expand, NT).astype(LOW)
    grad_fed, inner, res_all, fed = fence(grad_fed, inner, res_all, fed)
    parts = reduce_step(to_parts(grad_fed), 2)
    grad_down = matmul(inner, res_all, TN).astype(LOW).reshape(halves, 2, hidden_shard, width)
    parts, inner, grad_down = fence(parts, inner, grad_down)
    parts = reduce_step(parts, 1)
    down_wire = send_cores(grad_down, at, 1)
    final = matmul(by_rows_of_light(inner), down).astype(LOW)
    parts, final, down_wire = fence(parts, final, down_wire)
    parts = reduce_step(parts, 0)
    grad_down = add_cores(grad_down, down_wire, at, 1)
    parts, grad_down = fence(parts, grad_down)
    grad_normed_two = own_rows(parts)
    grad_hidden = grad_res + norm_back(grad_normed_two * gain_feed, unit_two, scale_two)

    grad_hidden_low = grad_hidden.astype(LOW)
    grad_mixed = matmul(grad_hidden_low, out_full, NT).astype(LOW)
    grad_mixed = grad_mixed.reshape(2 * rows, 8, 2 * span).transpose(1, 0, 2)
    grad_mixed, fed, grad_down = fence(grad_mixed, fed, grad_down)
    grad_down = scatter_halves(grad_down)
    grad_mixed = exchange(grad_mixed)
    grad_expand = matmul(fed, grad_gate_up, TN).astype(LOW).reshape(halves, 8, 2, shard_rows, -1)
    if one_block:
        mixed = by_light_distance(mixed_chunks, at)
    grad_mixed, final, mixed, grad_expand = fence(grad_mixed, final, mixed, grad_expand)
    final_parts = list(final.reshape(2, 8, rows, width))
    grad_mixed = grad_mixed.reshape(16 * rows, 2 * span)
    g_halves = grad_mixed[:, :span], grad_mixed[:, span:]
    g_own = jnp.where(at["c"] == 0, *g_halves)
    g_other = swap(jnp.where(at["c"] == 0, *g_halves[::-1]), "c")
    expand_wire = send_cores(grad_expand, at, 2)
    grad_out = matmul(mixed, grad_hidden_low, TN)
    if one_block:
        grad_out = grad_out.astype(LOW).reshape(2, 8, 2, HEAD_DIM, width)
        out_wire = send_cores(grad_out, at, 2)
    else:
        out_wire = ()
    g_own, g_other, expand_wire, out_wire = fence(g_own, g_other, expand_wire, out_wire)
    grad_expand = add_cores(grad_expand, expand_wire, at, 2)
    if one_block:
        grads = (g_own, g_other)
    else:
        grads = (in_order(jnp.concatenate([g_own, g_other], axis=0), chunk_at),)
    final_wires = light_send(final_parts)
    grad_expand = scatter_halves(grad_expand)
    *half_grads, d_diag_first = attend_backward(one_block, halo, 0, tables, tokens, extras[0], grads, saved[0], ())
    half_grads, final_wires, out_wire, grad_out = fence(half_grads, final_wires, out_wire, grad_out)
    final_parts = reduce_add(final_parts, final_wires)
    final_wires = light_send(final_parts)
    if one_block:
        out_parts = list(add_cores(grad_out, out_wire, at, 2))
        out_wires = light_send(out_parts)
    else:
        out_parts = out_wires = ()
    *d_all, d_diag = attend_backward(
        one_block, halo, 1, tables, tokens, extras[1], grads, saved[1], tuple(half_grads)
    )
    if one_block:
        d_own, d_other = d_all
    else:
        dq, dk, dv = d_all
        d_all = jnp.concatenate([dq, add_sides(dk, halo), add_sides(dv, halo)], axis=1)
        d_own, d_other = jnp.split(as_pieces(d_all.astype(LOW), spread_at), 2, axis=0)
    d_own, d_other, final_wires, out_wires, grad_expand = fence(d_own, d_other, final_wires, out_wires, grad_expand)
    d_other = swap(d_other, "c")
    final_parts = reduce_add(final_parts, final_wires)
    final_wires = light_send(final_parts)
    if one_block:
        out_parts = reduce_add(out_parts, out_wires)
        out_wires = light_send(out_parts)
    (d_other,) = fence(d_other)
    grad_projected = jnp.concatenate([d_own, d_other], axis=1)
    grad_normed_one = matmul(grad_projected, project, NT).astype(LOW)
    grad_normed_one, grad_projected, final_wires, out_wires, final_parts, out_parts = fence(
        grad_normed_one, grad_projected, final_wires, out_wires, final_parts, out_parts
    )

    def turn(got):
        return jnp.concatenate([got[..., side:], got[..., :side]], axis=-1)

    parts = reduce_step(to_parts(grad_normed_one), 2)
    grad_expand = exchange(grad_expand)
    grad_project = matmul(normed_one, grad_projected, TN).astype(LOW).reshape(halves, 8, 2, shard_rows, -1)
    project_wire = send_cores(grad_project, at, 2)
    grad_project = add_cores(grad_project, turn(project_wire), at, 2)
    moved = grad_normed_one.astype(F32) * gathered_scale * gathered.astype(F32)
    grad_gain_rows = jnp.sum(moved, axis=0)
    grad_feed_gain = jnp.sum(grad_normed_two * unit_two, axis=0)
    sums = jnp.concatenate([d_diag_first, d_diag], axis=0)
    hot = buckets == jnp.arange(BUCKETS, dtype=jnp.int32)[:, None]
    sums = jnp.sum(jnp.where(hot[:, None], sums, 0.0), axis=2)
    lanes = (jnp.arange(16, dtype=jnp.int32) == lane).astype(F32)
    grad_position_bias = (sums[:, None, :] * lanes[:, None]).reshape(-1)
    count = lax.axis_size(AXES)
    gains = attention_norm_gain.shape[0]
    small = [grad_feed_gain, grad_gain_rows, grad_position_bias]
    small = jnp.concatenate([line.reshape(count, -1) for line in small], axis=1)
    final_near, final_far = [part[0].astype(F32) for part in reduce_add(final_parts, final_wires)]
    final_near = (hidden_one[:rows] + final_near).astype(LOW)
    final_far = (hidden_one[rows:] + final_far).astype(LOW)
    if one_block:
        out_parts = reduce_add(out_parts, out_wires)
    parts, small, final_far, grad_project, out_parts = fence(parts, small, final_far, grad_project, out_parts)
    grad_project = scatter_halves(grad_project)
    small = sum_line(small)
    parts = reduce_step(parts, 1)
    final_far = swap(final_far, "h")
    if one_block:
        out_wires = light_send(out_parts)
    parts, small, out_wires = fence(parts, small, out_wires)
    parts = reduce_step(parts, 0)
    if one_block:
        grad_out = scatter_halves(jnp.concatenate(reduce_add(out_parts, out_wires), axis=0))
    parts, grad_project = fence(parts, grad_project)
    grad_part = own_rows(parts)
    unit_one, scale_one = normalize(tokens_here)
    token_grad = grad_hidden + norm_back(grad_part * gain_attn, unit_one, scale_one)
    token_grad = token_grad.astype(LOW)
    input_grad = both(token_grad[:rows], swap(token_grad[rows:], "h"), near, 0)
    grad_project = exchange(grad_project)
    layer_output = both(final_near, final_far, near, 0)
    grad_expand = join_columns(grad_expand, expand_order, 2 * hidden_shard)
    grad_feed_gain = small[:gains]
    grad_attention_gain = small[gains : 2 * gains]
    grad_position_bias = small[2 * gains :]
    grad_out = grad_out.astype(F32) if one_block else grad_out_wide(grad_out)
    grad_down = grad_down.astype(F32)
    grad_project = jnp.where(at["c"] == 0, grad_project, turn(grad_project))
    grad_project = join_columns(grad_project, project_order, span)
    return (
        layer_output,
        input_grad,
        grad_attention_gain,
        grad_project,
        grad_out,
        grad_position_bias,
        grad_feed_gain,
        grad_expand,
        grad_down,
    )


def solution(mesh):
    wide = Mesh(mesh.devices.reshape(-1, 2, 2, 2, 2, 2), AXES)
    lead, tokens, rows = P(AXES), P(None, AXES), P(AXES, None)
    return jax.shard_map(
        local,
        mesh=wide,
        in_specs=(tokens, tokens, tokens, tokens, P(), lead, rows, rows, lead, lead, rows, rows),
        out_specs=(tokens, tokens, lead, rows, rows, lead, lead, rows, rows),
        check_vma=False,
    )
```

time: 1120 us -> 825 us (0.74)
  waiting for transfers between devices: 404 us -> 270 us
  starting transfers between devices: 214 us -> 125 us
  local copies, waits for them, and re-layouts: 146 us -> 85.2 us
  other arithmetic: 129 us -> 85.9 us
  Pallas kernels: 119 us -> 135 us
  between operations: 3.99 us -> 16.2 us
    ppermute x154 -> x75, waiting for transfers between devices: 349 us -> 221 us  [swap(): return lax.ppermute(value, axis, SWAP)]
    ppermute x154 -> x75, starting transfers between devices: 172 us -> 89.7 us  [swap(): return lax.ppermute(value, axis, SWAP)]
    select_n x29 -> x4, other arithmetic: 42.9 us -> 6.93 us  [both(): jnp.where(bit == 0, put([mine, theirs], axis), put([theirs, mine], axis))]
    convert_element_type x8 -> x0, local copies, waits for them, and re-layouts: 34.3 us -> none  [the longest x3 22.3 us: local(): grad_expand.transpose(1, 2, 3, 0, 4, 5).reshape(shard_rows, -1).astype(F32)]
    all_to_all x3 -> x1, waiting for transfers between devices: 55 us -> 22.1 us  [sum_line(): return jnp.sum(lax.all_to_all(line.reshape(count, -1), AXES, 0, 0), axis=0)]
    convert_element_type x56 -> x35, other arithmetic: 30.5 us -> 57 us  [the longest x27 35.8 us: reduce_add(): (a[:half].astype(F32) + b.astype(F32)).astype(LOW)]
    concatenate x65 -> x4, other arithmetic: 24.1 us -> 3.11 us  [the longest x1 1.46 us: local(): grad_projected = jnp.concatenate([d_own, d_other], axis=1)]
    reshape x13 -> x3, local copies, waits for them, and re-layouts: 20.4 us -> 1.07 us  [the longest x1 0.93 us: local(): grad_mixed = grad_mixed.reshape(2 * rows, 8, 2 * span).transpose(1, 0, 2)]
  transfers between devices with their start and end apart: 164 -> 90, of which waited for: 61 -> 40; matrix products, arithmetic and copies ran while one was open for 25% -> 22% of each run, Pallas kernels for 11% -> 16%
where the time goes in v2:
time: 825 us; the launch traced here: 816 us
  waiting for transfers between devices  270 us (33%)
  Pallas kernels  135 us (16%)
  starting transfers between devices  125 us (15%)
  matrix products  98.9 us (12%)
  other arithmetic  85.9 us (10%)
  local copies, waits for them, and re-layouts  85.2 us (10%)
  between operations  16.2 us (2%)
    ppermute x75, waiting for transfers between devices, swap(): return lax.ppermute(value, axis, SWAP)  221 us
    dot_general x12, matrix products, matmul(): return lax.dot_general(left, right, dims, preferred_element_type=F32)  98.9 us
    ppermute x75, starting transfers between devices, swap(): return lax.ppermute(value, axis, SWAP)  89.7 us
    pallas_call x2, Pallas kernels, attend_backward(): pl.pallas_call(lambda *refs: backward_kernel(local, halo, n, *refs), out_...  59 us
    pallas_call x2, Pallas kernels, attend_forward(): pl.pallas_call(lambda *refs: forward_kernel(local, halo, n, *refs), out_s...  46.5 us
    unnamed x235, local copies, waits for them, and re-layouts  40.4 us
    convert_element_type x27, other arithmetic, reduce_add(): (a[:half].astype(F32) + b.astype(F32)).astype(LOW)  35.8 us
    all_to_all x7, starting transfers between devices, exchange(): return lax.all_to_all(chunks, CUBE, 0, 0)  27.8 us
  transfers between devices with their start and end apart: 90, of which 40 were waited for; matrix products, arithmetic and copies ran while one was open for 22% of the time, Pallas kernels for 16%

profile of v2, /device:TPU:0, one launch (start us, length us, event | category | flops | bytes accessed | tf_op | source)
XLA Modules:
  0.0 815.9 jit_solution(2963875795247214487)
XLA Ops:
  9.2 4.0 collective-permute-start
  19.1 3.8 all-to-all-start
  27.6 6.3 all-to-all-done
  34.1 3.6 all-to-all-start.1
  47.5 12.3 %collective-permute-done.1.refs_1_ = bf16[1,64,2048]{2,1,0:T(8,128)(2,1)S(1)} collective-permute-done((bf16[1,64,2048]{2,1,0:T(8,128)(2,1)S(1)}, bf16[1,64,2048]{2,1,0:T(8,128)(2,1)S(1)}, u32[]{:S(2)}, u32[]{:S(2)}) %collective-permute-start.1) | collective-permute-done | bytes 262176 | tf_op jit(solution)/shard_map/ppermute | solution.py:384
  71.3 6.0 collective-permute-done.5.refs_1_
  78.3 13.7 %collective-permute-done.7.refs_5_ = bf16[2,64,2048]{2,1,0:T(8,128)(2,1)S(1)} collective-permute-done((bf16[2,64,2048]{2,1,0:T(8,128)(2,1)S(1)}, bf16[2,64,2048]{2,1,0:T(8,128)(2,1)S(1)}, u32[]{:S(2)}, u32[]{:S(2)}) %collective-permute-start.7) | collective-permute-done | bytes 524320 | tf_op jit(solution)/shard_map/ppermute | solution.py:384
  95.7 3.6 collective-permute-done.8.refs_1_
  103.3 2.9 shard_map.265
  110.3 3.0 collective-permute-start.12
  113.5 19.6 %collective-permute-done.10.refs_3_ = bf16[4,64,2048]{2,1,0:T(8,128)(2,1)} collective-permute-done((bf16[4,64,2048]{2,1,0:T(8,128)(2,1)}, bf16[4,64,2048]{2,1,0:T(8,128)(2,1)}, u32[]{:S(2)}, u32[]{:S(2)}) %collective-permute-start.10) | collective-permute-done | bytes 1048608 | tf_op jit(solution)/shard_map/ppermute | solution.py:384
  140.5 4.3 all-to-all-start.2
  153.5 6.6 convolution_convert_fusion.5
  160.1 2.9 all-to-all-done.2
  163.1 4.9 all-to-all-start.3
  168.7 3.0 fusion.56
  178.5 22.5 %shard_map.269 = (f32[64,3072]{1,0:T(8,128)}, f32[1,3072]{1,0:T(1,128)}) custom-call(s32[96]{0:T(128)} %multiply_add_fusion.2.refs_0_, s32[32]{0:T(128)} %add_multiply_fusion.1.refs_1_, s32[2,12]{1,0:T(2,128)} %copy-done.36, bf16[1536,384]{1,0:T(8,128)(2,1)} %get-tuple-element.248.refs_3_, bf16[1536,384]{1,0:T(8,128)(2,1)} %copy-done.41, ...), custom_call_target="tpu_custom_call" | custom-call | flops 3072 | bytes 65536 | tf_op jit(solution)/shard_map/pallas_call | solution.py:306
  201.0 23.9 %shard_map.270 = (bf16[1536,128]{1,0:T(8,128)(2,1)}, bf16[1536,128]{1,0:T(8,128)(2,1)}, f32[64,3072]{1,0:T(8,128)}, f32[1,3072]{1,0:T(1,128)}) custom-call(s32[96]{0:T(128)} %multiply_add_fusion.2.refs_0_, s32[32]{0:T(128)} %add_multiply_fusion.1.refs_1_, s32[2,12]{1,0:T(2,128)} %copy-done.36, bf16[1536,384]{1,0:T(8,128)(2,1)} %get-tuple-element.248.refs_3_, ...), custom_call_target="tpu_custom_call" | custom-call | flops 3072 | bytes 65536 | tf_op jit(solution)/shard_map/pallas_call | solution.py:306
  226.4 22.5 %collective-permute-done.15.refs_1_ = bf16[1,64,2048]{2,1,0:T(8,128)(2,1)S(1)} collective-permute-done((bf16[1,64,2048]{2,1,0:T(8,128)(2,1)S(1)}, bf16[1,64,2048]{2,1,0:T(8,128)(2,1)S(1)}, u32[]{:S(2)}, u32[]{:S(2)}) %collective-permute-start.15) | collective-permute-done | bytes 262176 | tf_op jit(solution)/shard_map/ppermute | solution.py:384
  254.4 7.1 collective-permute-done.18
  263.9 4.4 all-to-all-start.4
  269.0 4.1 shard_map.272
  273.1 3.3 copy-done.3
  276.4 3.9 all-to-all-done.4
  280.4 5.6 multiply_reduce_fusion
  291.1 9.7 %collective-permute-done.21.refs_1_ = bf16[1,64,2048]{2,1,0:T(8,128)(2,1)S(1)} collective-permute-done((bf16[1,64,2048]{2,1,0:T(8,128)(2,1)S(1)}, bf16[1,64,2048]{2,1,0:T(8,128)(2,1)S(1)}, u32[]{:S(2)}, u32[]{:S(2)}) %collective-permute-start.21) | collective-permute-done | bytes 262176 | tf_op jit(solution)/shard_map/ppermute | solution.py:384
  307.7 3.0 all-gather.7.cloned.1.call-done
  310.8 7.8 collective-permute-done.26.refs_5_
  320.3 10.9 %collective-permute-done.27.refs_1_ = bf16[2,64,2048]{2,1,0:T(8,128)(2,1)S(1)} collective-permute-done((bf16[2,64,2048]{2,1,0:T(8,128)(2,1)S(1)}, bf16[2,64,2048]{2,1,0:T(8,128)(2,1)S(1)}, u32[]{:S(2)}, u32[]{:S(2)}) %collective-permute-start.27) | collective-permute-done | bytes 524320 | tf_op jit(solution)/shard_map/ppermute | solution.py:384
  335.4 2.9 shard_map.279
  342.8 15.9 %collective-permute-done.30.refs_1_ = bf16[4,64,2048]{2,1,0:T(8,128)(2,1)S(1)} collective-permute-done((bf16[4,64,2048]{2,1,0:T(8,128)(2,1)S(1)}, bf16[4,64,2048]{2,1,0:T(8,128)(2,1)S(1)}, u32[]{:S(2)}, u32[]{:S(2)}) %collective-permute-start.30) | collective-permute-done | bytes 1048608 | tf_op jit(solution)/shard_map/ppermute | solution.py:384
  363.1 10.3 %fusion.63 = f32[1536,1280]{1,0:T(8,128)} fusion(bf16[1536,2048]{1,0:T(8,128)(2,1)S(1)} %shard_map.278, bf16[2048,1280]{1,0:T(8,128)(2,1)S(1)} %bitcast.190), kind=kOutput, calls=%fused_computation.185 | convolution fusion | flops 8053063680 | bytes 19398656 | tf_op jit(solution)/shard_map/dot_general | solution.py:397
  373.4 4.7 multiply_convert_fusion.1.src
  380.7 13.6 %fusion.9 = (bf16[1536,640]{1,0:T(8,128)(2,1)S(1)}, bf16[1536,640]{1,0:T(8,128)(2,1)}) fusion(f32[1536,1280]{1,0:T(8,128)} %fusion.63, bf16[1536,2048]{1,0:T(8,128)(2,1)S(1)} %shard_map.281, bf16[640,2048]{1,0:T(8,128)(2,1)S(1)} %bitcast.194), kind=kOutput, calls=%fused_computation.24 | convolution fusion | flops 4054056960 | bytes 20709376 | tf_op jit(solution)/shard_map/dot_general | solution.py:397
  394.3 10.5 %convolution_convert_fusion.3 = bf16[1536,2048]{1,0:T(8,128)(2,1)S(1)} fusion(bf16[2048,1280]{1,0:T(8,128)(2,1)S(1)} %bitcast.191, bf16[1536,640]{1,0:T(8,128)(2,1)} %get-tuple-element.398, bf16[1536,640]{1,0:T(8,128)(2,1)S(1)} %get-tuple-element.397), kind=kOutput, calls=%fused_computation.12 | convolution fusion | flops 8064073728 | bytes 15466496 | tf_op jit(solution)/shard_map/dot_general | solution.py:397
  412.3 7.1 convolution_convert_fusion.7
  419.3 9.5 %collective-permute-done.39 = bf16[4,64,2048]{2,1,0:T(8,128)(2,1)} collective-permute-done((bf16[4,64,2048]{2,1,0:T(8,128)(2,1)}, bf16[4,64,2048]{2,1,0:T(8,128)(2,1)}, u32[]{:S(2)}, u32[]{:S(2)}) %collective-permute-start.39) | collective-permute-done | bytes 1048608 | tf_op jit(solution)/shard_map/ppermute | solution.py:384
  433.9 7.3 convolution_convert_fusion.2
  445.0 5.5 collective-permute-done.41
  450.6 6.8 collective-permute-done.40
  471.7 6.9 convolution_convert_fusion.8
  479.5 3.5 all-to-all-start.5
  483.2 13.4 %convolution_convert_fusion.1 = bf16[2048,1280]{1,0:T(8,128)(2,1)} fusion(bf16[1536,2048]{1,0:T(8,128)(2,1)} %copy-done.4, bf16[1536,640]{1,0:T(8,128)(2,1)} %get-tuple-element.398, bf16[1536,640]{1,0:T(8,128)(2,1)} %copy-done.111), kind=kOutput, calls=%fused_computation.10 | convolution fusion | flops 8063549440 | bytes 15466496 | tf_op jit(solution)/shard_map/dot_general | solution.py:397
  499.6 3.6 copy-done.37
  506.2 8.6 %collective-permute-done.47.refs_9_ = bf16[1536,128]{1,0:T(8,128)(2,1)S(1)} collective-permute-done((bf16[1536,128]{1,0:T(8,128)(2,1)S(1)}, bf16[1536,128]{1,0:T(8,128)(2,1)S(1)}, u32[]{:S(2)}, u32[]{:S(2)}) %collective-permute-start.47) | collective-permute-done | bytes 393248 | tf_op jit(solution)/shard_map/ppermute | solution.py:384
  517.1 5.4 fusion.54
  526.9 28.7 %shard_map.284 = (bf16[3072,128]{1,0:T(8,128)(2,1)}, bf16[3072,128]{1,0:T(8,128)(2,1)}, bf16[3072,128]{1,0:T(8,128)(2,1)}, f32[1,2560]{1,0:T(1,128)}) custom-call(s32[96]{0:T(128)} %multiply_add_fusion.2.refs_0_, s32[32]{0:T(128)} %add_multiply_fusion.1.refs_1_, s32[2,12]{1,0:T(2,128)} %copy-done.36, bf16[1536,384]{1,0:T(8,128)(2,1)} %get-tuple-element.248.refs_3_, ...), custom_call_target="tpu_custom_call" | custom-call | flops 3072 | bytes 65536 | tf_op jit(solution)/shard_map/pallas_call | solution.py:344
  555.5 3.8 collective-permute-done.50
  560.8 5.4 fusion.4
  578.1 30.3 %shard_map.285 = (bf16[1536,384]{1,0:T(8,128)(2,1)}, bf16[1536,384]{1,0:T(8,128)(2,1)}, f32[1,2560]{1,0:T(1,128)}) custom-call(s32[96]{0:T(128)} %multiply_add_fusion.2.refs_0_, s32[32]{0:T(128)} %add_multiply_fusion.1.refs_1_, s32[2,12]{1,0:T(2,128)} %copy-done.36, bf16[1536,384]{1,0:T(8,128)(2,1)} %get-tuple-element.248.refs_3_, ...), custom_call_target="tpu_custom_call" | custom-call | flops 3072 | bytes 65536 | tf_op jit(solution)/shard_map/pallas_call | solution.py:344
  622.2 3.6 all-to-all-start.8
  625.9 7.4 convolution_convert_fusion
  634.7 8.2 %collective-permute-done.57 = bf16[1,96,2048]{2,1,0:T(8,128)(2,1)} collective-permute-done((bf16[1,96,2048]{2,1,0:T(8,128)(2,1)}, bf16[1,96,2048]{2,1,0:T(8,128)(2,1)}, u32[]{:S(2)}, u32[]{:S(2)}) %collective-permute-start.57) | collective-permute-done | bytes 393248 | tf_op jit(solution)/shard_map/ppermute | solution.py:384
  642.9 4.9 fusion.3
  650.3 7.9 convolution_convert_fusion.6
  668.9 16.5 %collective-permute-done.63 = bf16[4,64,2048]{2,1,0:T(8,128)(2,1)} collective-permute-done((bf16[4,64,2048]{2,1,0:T(8,128)(2,1)}, bf16[4,64,2048]{2,1,0:T(8,128)(2,1)}, u32[]{:S(2)}, u32[]{:S(2)}) %collective-permute-start.63) | collective-permute-done | bytes 1048608 | tf_op jit(solution)/shard_map/ppermute | solution.py:384
  685.4 2.9 fusion.16
  699.0 6.5 collective-permute-start.65
  720.6 22.1 %all-to-all-done.6 = f32[32,1,160]{2,1,0:T(1,128)S(1)} async-done(((f32[32,1,160]{2,1,0:T(1,128)}), f32[32,1,160]{2,1,0:T(1,128)S(1)}, u32[]{:S(2)}, u32[]{:S(2)}) %all-to-all-start.6) | async-done | bytes 20512 | tf_op jit(solution)/shard_map/all_to_all | solution.py:568
  742.8 3.1 collective-permute-start.70
  751.9 10.7 %collective-permute-done.70 = bf16[1,64,2048]{2,1,0:T(8,128)(2,1)S(1)} collective-permute-done((bf16[1,64,2048]{2,1,0:T(8,128)(2,1)}, bf16[1,64,2048]{2,1,0:T(8,128)(2,1)S(1)}, u32[]{:S(2)}, u32[]{:S(2)}) %collective-permute-start.70) | collective-permute-done | bytes 262176 | tf_op jit(solution)/shard_map/ppermute | solution.py:384
  775.5 3.5 all-to-all-start.7
  784.6 9.9 %reduce-scatter.9.cloned.1.call-done = bf16[1,64,2048]{2,1,0:T(8,128)(2,1)} async-done(((bf16[2,64,2048]{2,1,0:T(8,128)(2,1)}), bf16[1,64,2048]{2,1,0:T(8,128)(2,1)}) %reduce-scatter.9.cloned.1.call-update) | async-done | bytes 262160 | tf_op jit(solution)/shard_map/reduce_scatter | solution.py:644
  796.3 9.6 %collective-permute-done.74 = bf16[96,2048]{1,0:T(8,128)(2,1)S(1)} collective-permute-done((bf16[96,2048]{1,0:T(8,128)(2,1)S(1)}, bf16[96,2048]{1,0:T(8,128)(2,1)S(1)}, u32[]{:S(2)}, u32[]{:S(2)}) %collective-permute-start.74) | collective-permute-done | bytes 393248 | tf_op jit(solution)/shard_map/ppermute | solution.py:384
  (536 shorter events, 249.9 us)
Async XLA Ops:
  9.2 24.9 %collective-permute-start = (bf16[96,2048]{1,0:T(8,128)(2,1)}, bf16[96,2048]{1,0:T(8,128)(2,1)S(1)}, u32[]{:S(2)}, u32[]{:S(2)}) collective-permute-start(bf16[96,2048]{1,0:T(8,128)(2,1)} %get-tuple-element.434), channel_id=1, source_target_pairs={{0,16},{16,0},{1,17},{17,1},{2,18},{18,2},{3,19},{19,3},{4,20},{20... | collective-permute-start | bytes 1179656 | tf_op jit(solution)/shard_map/ppermute | solution.py:384
  34.1 29.2 %all-to-all-start.1 = ((bf16[8,64,768]{2,1,0:T(8,128)(2,1)}), bf16[8,64,768]{2,1,0:T(8,128)(2,1)S(1)}, u32[]{:S(2)}, u32[]{:S(2)}) async-start(bf16[8,64,768]{2,1,0:T(8,128)(2,1)} %shard_map.260), calls=%async_computation.1 | async-start | bytes 1572864 | tf_op jit(solution)/shard_map/all_to_all | solution.py:536
  38.7 21.1 %collective-permute-start.1 = (bf16[1,64,2048]{2,1,0:T(8,128)(2,1)S(1)}, bf16[1,64,2048]{2,1,0:T(8,128)(2,1)S(1)}, u32[]{:S(2)}, u32[]{:S(2)}) collective-permute-start(bf16[1,64,2048]{2,1,0:T(8,128)(2,1)S(1)} %constant_dynamic-slice_fusion.1.refs_0_), channel_id=1, source_target_pairs={{0,8},{8,0},{1,9},{9,1},{2,10},{10,2},{3,11},{11,3},{4,12},{12,4},... | collective-permute-start | bytes 786440 | tf_op jit(solution)/shard_map/ppermute | solution.py:384
  40.7 19.1 %collective-permute-start.2 = (bf16[1,64,2048]{2,1,0:T(8,128)(2,1)S(1)}, bf16[1,64,2048]{2,1,0:T(8,128)(2,1)S(1)}, u32[]{:S(2)}, u32[]{:S(2)}) collective-permute-start(bf16[1,64,2048]{2,1,0:T(8,128)(2,1)S(1)} %get-tuple-element.439.refs_2_), channel_id=1, source_target_pairs={{0,4},{4,0},{1,5},{5,1},{2,6},{6,2},{3,7},{7,3},{8,12},{12,8},{9,1... | collective-permute-start | bytes 786440 | tf_op jit(solution)/shard_map/ppermute | solution.py:384
  42.3 18.2 %collective-permute-start.3 = (bf16[1,64,2048]{2,1,0:T(8,128)(2,1)S(1)}, bf16[1,64,2048]{2,1,0:T(8,128)(2,1)S(1)}, u32[]{:S(2)}, u32[]{:S(2)}) collective-permute-start(bf16[1,64,2048]{2,1,0:T(8,128)(2,1)S(1)} %get-tuple-element.438.refs_4_), channel_id=1, source_target_pairs={{0,2},{2,0},{1,3},{3,1},{4,6},{6,4},{5,7},{7,5},{8,10},{10,8},{9,1... | collective-permute-start | bytes 786440 | tf_op jit(solution)/shard_map/ppermute | solution.py:384
  43.7 19.5 %collective-permute-start.4 = (bf16[64,2048]{1,0:T(8,128)(2,1)}, bf16[64,2048]{1,0:T(8,128)(2,1)}, u32[]{:S(2)}, u32[]{:S(2)}) collective-permute-start(bf16[64,2048]{1,0:T(8,128)(2,1)} %param.26), channel_id=1, source_target_pairs={{0,16},{16,0},{1,17},{17,1},{2,18},{18,2},{3,19},{19,3},{4,20},{20... | collective-permute-start | bytes 786440 | tf_op jit(solution)/shard_map/ppermute | solution.py:384
  63.3 36.1 %collective-permute-start.8 = (bf16[8,64,768]{2,1,0:T(8,128)(2,1)S(1)}, bf16[8,64,768]{2,1,0:T(8,128)(2,1)S(1)}, u32[]{:S(2)}, u32[]{:S(2)}) collective-permute-start(bf16[8,64,768]{2,1,0:T(8,128)(2,1)S(1)} %all-to-all-done.1.refs_0_), channel_id=1, source_target_pairs={{0,16},{16,0},{1,17},{17,1},{2,18},{18,2},{3,19},{19,3},{4,20},{20... | collective-permute-start | bytes 2359304 | tf_op jit(solution)/shard_map/ppermute | solution.py:384
  68.1 23.9 %collective-permute-start.7 = (bf16[2,64,2048]{2,1,0:T(8,128)(2,1)S(1)}, bf16[2,64,2048]{2,1,0:T(8,128)(2,1)S(1)}, u32[]{:S(2)}, u32[]{:S(2)}) collective-permute-start(bf16[2,64,2048]{2,1,0:T(8,128)(2,1)S(1)} %get-tuple-element.213.refs_4_), channel_id=1, source_target_pairs={{0,8},{8,0},{1,9},{9,1},{2,10},{10,2},{3,11},{11,3},{4,12},{12,4},... | collective-permute-start | bytes 1572872 | tf_op jit(solution)/shard_map/ppermute | solution.py:384
  100.2 32.8 %collective-permute-start.10 = (bf16[4,64,2048]{2,1,0:T(8,128)(2,1)}, bf16[4,64,2048]{2,1,0:T(8,128)(2,1)}, u32[]{:S(2)}, u32[]{:S(2)}) collective-permute-start(bf16[4,64,2048]{2,1,0:T(8,128)(2,1)} %get-tuple-element.221.refs_2_), channel_id=1, source_target_pairs={{0,8},{8,0},{1,9},{9,1},{2,10},{10,2},{3,11},{11,3},{4,12},{12,4},... | collective-permute-start | bytes 3145736 | tf_op jit(solution)/shard_map/ppermute | solution.py:384
  100.2 32.8 %collective-permute-start.11 = (bf16[4,64,2048]{2,1,0:T(8,128)(2,1)}, bf16[4,64,2048]{2,1,0:T(8,128)(2,1)}, u32[]{:S(2)}, u32[]{:S(2)}) collective-permute-start(bf16[4,64,2048]{2,1,0:T(8,128)(2,1)} %get-tuple-element.222.refs_4_), channel_id=1, source_target_pairs={{0,4},{4,0},{1,5},{5,1},{2,6},{6,2},{3,7},{7,3},{8,12},{12,8},{9,1... | collective-permute-start | bytes 3145736 | tf_op jit(solution)/shard_map/ppermute | solution.py:384
  101.7 31.4 %collective-permute-start.9 = (bf16[4,64,2048]{2,1,0:T(8,128)(2,1)S(1)}, bf16[4,64,2048]{2,1,0:T(8,128)(2,1)}, u32[]{:S(2)}, u32[]{:S(2)}) collective-permute-start(bf16[4,64,2048]{2,1,0:T(8,128)(2,1)S(1)} %get-tuple-element.220.refs_0_), channel_id=1, source_target_pairs={{0,2},{2,0},{1,3},{3,1},{4,6},{6,4},{5,7},{7,5},{8,10},{10,8},{9,1... | collective-permute-start | bytes 3145736 | tf_op jit(solution)/shard_map/ppermute | solution.py:384
  110.3 26.8 %collective-permute-start.12 = (bf16[96,2048]{1,0:T(8,128)(2,1)S(1)}, bf16[96,2048]{1,0:T(8,128)(2,1)S(1)}, u32[]{:S(2)}, u32[]{:S(2)}) collective-permute-start(bf16[96,2048]{1,0:T(8,128)(2,1)S(1)} %dynamic-slice_bitcast_fusion.5), channel_id=1, source_target_pairs={{0,16},{16,0},{1,17},{17,1},{2,18},{18,2},{3,19},{19,3},{4,20},{20... | collective-permute-start | bytes 1179656 | tf_op jit(solution)/shard_map/ppermute | solution.py:384
  140.5 22.6 %all-to-all-start.2 = ((bf16[8,64,1280]{2,1,0:T(8,128)(2,1)}), bf16[8,64,1280]{2,1,0:T(8,128)(2,1)}, u32[]{:S(2)}, u32[]{:S(2)}) async-start(bf16[8,64,1280]{2,1,0:T(8,128)(2,1)} %shard_map.261), calls=%async_computation.2 | async-start | bytes 2621440 | tf_op jit(solution)/shard_map/all_to_all | solution.py:536
  163.1 86.5 %all-to-all-start.3 = ((bf16[8,2,64,2048]{3,2,1,0:T(8,128)(2,1)}), bf16[8,2,64,2048]{3,2,1,0:T(8,128)(2,1)}, u32[]{:S(2)}, u32[]{:S(2)}) async-start(bf16[8,2,64,2048]{3,2,1,0:T(8,128)(2,1)} %broadcast_in_dim.73), calls=%async_computation.3 | async-start | bytes 8388608 | tf_op jit(solution)/shard_map/all_to_all | solution.py:536
  167.9 81.7 %all-gather.5.cloned.1.call-start = ((), (), s32[]{:S(2)}) async-start(), calls=%async_computation.17 | async-start | bytes 3932160 | tf_op jit(solution)/shard_map/all_gather | solution.py:640
  171.8 53.2 %collective-permute-start.16 = (bf16[1,64,2048]{2,1,0:T(8,128)(2,1)S(1)}, bf16[1,64,2048]{2,1,0:T(8,128)(2,1)S(1)}, u32[]{:S(2)}, u32[]{:S(2)}) collective-permute-start(bf16[1,64,2048]{2,1,0:T(8,128)(2,1)S(1)} %get-tuple-element.437.refs_2_), channel_id=1, source_target_pairs={{0,4},{4,0},{1,5},{5,1},{2,6},{6,2},{3,7},{7,3},{8,12},{12,8},{9,1... | collective-permute-start | bytes 786440 | tf_op jit(solution)/shard_map/ppermute | solution.py:384
  173.8 51.8 %collective-permute-start.17 = (bf16[1,64,2048]{2,1,0:T(8,128)(2,1)S(1)}, bf16[1,64,2048]{2,1,0:T(8,128)(2,1)S(1)}, u32[]{:S(2)}, u32[]{:S(2)}) collective-permute-start(bf16[1,64,2048]{2,1,0:T(8,128)(2,1)S(1)} %get-tuple-element.436.refs_4_), channel_id=1, source_target_pairs={{0,2},{2,0},{1,3},{3,1},{4,6},{6,4},{5,7},{7,5},{8,10},{10,8},{9,1... | collective-permute-start | bytes 786440 | tf_op jit(solution)/shard_map/ppermute | solution.py:384
  175.6 73.3 %collective-permute-start.15 = (bf16[1,64,2048]{2,1,0:T(8,128)(2,1)S(1)}, bf16[1,64,2048]{2,1,0:T(8,128)(2,1)S(1)}, u32[]{:S(2)}, u32[]{:S(2)}) collective-permute-start(bf16[1,64,2048]{2,1,0:T(8,128)(2,1)S(1)} %constant_dynamic-slice_fusion.refs_0_), channel_id=1, source_target_pairs={{0,8},{8,0},{1,9},{9,1},{2,10},{10,2},{3,11},{11,3},{4,12},{12,4},... | collective-permute-start | bytes 786440 | tf_op jit(solution)/shard_map/ppermute | solution.py:384
  249.6 26.8 %collective-permute-start.20 = (bf16[2,8,64,1280]{3,2,1,0:T(8,128)(2,1)}, bf16[2,8,64,1280]{3,2,1,0:T(8,128)(2,1)S(1)}, u32[]{:S(2)}, u32[]{:S(2)}) collective-permute-start(bf16[2,8,64,1280]{3,2,1,0:T(8,128)(2,1)} %bitcast.196), channel_id=1, source_target_pairs={{0,1},{1,0},{2,3},{3,2},{4,5},{5,4},{6,7},{7,6},{8,9},{9,8},{10,11... | collective-permute-start | bytes 7864328 | tf_op jit(solution)/shard_map/ppermute | solution.py:384
  263.9 16.4 %all-to-all-start.4 = ((bf16[8,192,256]{2,1,0:T(8,128)(2,1)}), bf16[8,192,256]{2,1,0:T(8,128)(2,1)S(1)}, u32[]{:S(2)}, u32[]{:S(2)}) async-start(bf16[8,192,256]{2,1,0:T(8,128)(2,1)} %maximum_select_fusion), calls=%async_computation.4 | async-start | bytes 1572864 | tf_op jit(solution)/shard_map/all_to_all | solution.py:536
  268.3 42.5 %all-gather.7.cloned.1.call-start = ((), (), s32[]{:S(2)}) async-start(), calls=%async_computation.18 | async-start | bytes 1966080 | tf_op jit(solution)/shard_map/all_gather | solution.py:640
  287.8 23.0 %collective-permute-start.24 = (bf16[2,64,2048]{2,1,0:T(8,128)(2,1)}, bf16[2,64,2048]{2,1,0:T(8,128)(2,1)}, u32[]{:S(2)}, u32[]{:S(2)}) collective-permute-start(bf16[2,64,2048]{2,1,0:T(8,128)(2,1)} %get-tuple-element.282.refs_0_), channel_id=1, source_target_pairs={{0,4},{4,0},{1,5},{5,1},{2,6},{6,2},{3,7},{7,3},{8,12},{12,8},{9,1... | collective-permute-start | bytes 1572872 | tf_op jit(solution)/shard_map/ppermute | solution.py:384
  288.4 22.4 %collective-permute-start.25 = (bf16[2,64,2048]{2,1,0:T(8,128)(2,1)}, bf16[2,64,2048]{2,1,0:T(8,128)(2,1)}, u32[]{:S(2)}, u32[]{:S(2)}) collective-permute-start(bf16[2,64,2048]{2,1,0:T(8,128)(2,1)} %get-tuple-element.283.refs_2_), channel_id=1, source_target_pairs={{0,2},{2,0},{1,3},{3,1},{4,6},{6,4},{5,7},{7,5},{8,10},{10,8},{9,1... | collective-permute-start | bytes 1572872 | tf_op jit(solution)/shard_map/ppermute | solution.py:384
  289.5 29.2 %collective-permute-start.26 = (bf16[2,64,2048]{2,1,0:T(8,128)(2,1)}, bf16[2,64,2048]{2,1,0:T(8,128)(2,1)}, u32[]{:S(2)}, u32[]{:S(2)}) collective-permute-start(bf16[2,64,2048]{2,1,0:T(8,128)(2,1)} %get-tuple-element.284.refs_4_), channel_id=1, source_target_pairs={{0,8},{8,0},{1,9},{9,1},{2,10},{10,2},{3,11},{11,3},{4,12},{12,4},... | collective-permute-start | bytes 1572872 | tf_op jit(solution)/shard_map/ppermute | solution.py:384
  290.5 16.7 %collective-permute-start.22 = (bf16[1,64,2048]{2,1,0:T(8,128)(2,1)S(1)}, bf16[1,64,2048]{2,1,0:T(8,128)(2,1)S(1)}, u32[]{:S(2)}, u32[]{:S(2)}) collective-permute-start(bf16[1,64,2048]{2,1,0:T(8,128)(2,1)S(1)} %get-tuple-element.432.refs_2_), channel_id=1, source_target_pairs={{0,4},{4,0},{1,5},{5,1},{2,6},{6,2},{3,7},{7,3},{8,12},{12,8},{9,1... | collective-permute-start | bytes 786440 | tf_op jit(solution)/shard_map/ppermute | solution.py:384
  320.3 19.3 %collective-permute-start.33 = (bf16[2,160,2048]{2,1,0:T(8,128)(2,1)}, bf16[2,160,2048]{2,1,0:T(8,128)(2,1)S(1)}, u32[]{:S(2)}, u32[]{:S(2)}) collective-permute-start(bf16[2,160,2048]{2,1,0:T(8,128)(2,1)} %bitcast.207), channel_id=1, source_target_pairs={{0,1},{1,0},{2,3},{3,2},{4,5},{5,4},{6,7},{7,6},{8,9},{9,8},{10,11... | collective-permute-start | bytes 3932168 | tf_op jit(solution)/shard_map/ppermute | solution.py:384
  332.6 26.2 %collective-permute-start.30 = (bf16[4,64,2048]{2,1,0:T(8,128)(2,1)S(1)}, bf16[4,64,2048]{2,1,0:T(8,128)(2,1)S(1)}, u32[]{:S(2)}, u32[]{:S(2)}) collective-permute-start(bf16[4,64,2048]{2,1,0:T(8,128)(2,1)S(1)} %get-tuple-element.289.refs_0_), channel_id=1, source_target_pairs={{0,2},{2,0},{1,3},{3,1},{4,6},{6,4},{5,7},{7,5},{8,10},{10,8},{9,1... | collective-permute-start | bytes 3145736 | tf_op jit(solution)/shard_map/ppermute | solution.py:384
  333.8 26.7 %collective-permute-start.31 = (bf16[4,64,2048]{2,1,0:T(8,128)(2,1)S(1)}, bf16[4,64,2048]{2,1,0:T(8,128)(2,1)S(1)}, u32[]{:S(2)}, u32[]{:S(2)}) collective-permute-start(bf16[4,64,2048]{2,1,0:T(8,128)(2,1)S(1)} %get-tuple-element.290.refs_2_), channel_id=1, source_target_pairs={{0,8},{8,0},{1,9},{9,1},{2,10},{10,2},{3,11},{11,3},{4,12},{12,4},... | collective-permute-start | bytes 3145736 | tf_op jit(solution)/shard_map/ppermute | solution.py:384
  334.1 26.4 %collective-permute-start.32 = (bf16[4,64,2048]{2,1,0:T(8,128)(2,1)S(1)}, bf16[4,64,2048]{2,1,0:T(8,128)(2,1)S(1)}, u32[]{:S(2)}, u32[]{:S(2)}) collective-permute-start(bf16[4,64,2048]{2,1,0:T(8,128)(2,1)S(1)} %get-tuple-element.291.refs_4_), channel_id=1, source_target_pairs={{0,4},{4,0},{1,5},{5,1},{2,6},{6,2},{3,7},{7,3},{8,12},{12,8},{9,1... | collective-permute-start | bytes 3145736 | tf_op jit(solution)/shard_map/ppermute | solution.py:384
  338.3 39.8 %collective-permute-start.34 = (bf16[4,64,2048]{2,1,0:T(8,128)(2,1)S(1)}, bf16[4,64,2048]{2,1,0:T(8,128)(2,1)S(1)}, u32[]{:S(2)}, u32[]{:S(2)}) collective-permute-start(bf16[4,64,2048]{2,1,0:T(8,128)(2,1)S(1)} %get-tuple-element.303.refs_0_), channel_id=1, source_target_pairs={{0,2},{2,0},{1,3},{3,1},{4,6},{6,4},{5,7},{7,5},{8,10},{10,8},{9,1... | collective-permute-start | bytes 3145736 | tf_op jit(solution)/shard_map/ppermute | solution.py:384
  339.6 38.8 %collective-permute-start.35 = (bf16[4,64,2048]{2,1,0:T(8,128)(2,1)S(1)}, bf16[4,64,2048]{2,1,0:T(8,128)(2,1)S(1)}, u32[]{:S(2)}, u32[]{:S(2)}) collective-permute-start(bf16[4,64,2048]{2,1,0:T(8,128)(2,1)S(1)} %get-tuple-element.304.refs_2_), channel_id=1, source_target_pairs={{0,8},{8,0},{1,9},{9,1},{2,10},{10,2},{3,11},{11,3},{4,12},{12,4},... | collective-permute-start | bytes 3145736 | tf_op jit(solution)/shard_map/ppermute | solution.py:384
  358.7 20.0 %collective-permute-start.36 = (bf16[4,64,2048]{2,1,0:T(8,128)(2,1)}, bf16[4,64,2048]{2,1,0:T(8,128)(2,1)S(1)}, u32[]{:S(2)}, u32[]{:S(2)}) collective-permute-start(bf16[4,64,2048]{2,1,0:T(8,128)(2,1)} %get-tuple-element.305.refs_4_), channel_id=1, source_target_pairs={{0,4},{4,0},{1,5},{5,1},{2,6},{6,2},{3,7},{7,3},{8,12},{12,8},{9,1... | collective-permute-start | bytes 3145736 | tf_op jit(solution)/shard_map/ppermute | solution.py:384
  407.6 21.3 %collective-permute-start.39 = (bf16[4,64,2048]{2,1,0:T(8,128)(2,1)}, bf16[4,64,2048]{2,1,0:T(8,128)(2,1)}, u32[]{:S(2)}, u32[]{:S(2)}) collective-permute-start(bf16[4,64,2048]{2,1,0:T(8,128)(2,1)} %bitcast.47), channel_id=1, source_target_pairs={{0,4},{4,0},{1,5},{5,1},{2,6},{6,2},{3,7},{7,3},{8,12},{12,8},{9,1... | collective-permute-start | bytes 3145736 | tf_op jit(solution)/shard_map/ppermute | solution.py:384
  409.1 21.9 %collective-permute-start.38 = (bf16[4,64,2048]{2,1,0:T(8,128)(2,1)}, bf16[4,64,2048]{2,1,0:T(8,128)(2,1)S(1)}, u32[]{:S(2)}, u32[]{:S(2)}) collective-permute-start(bf16[4,64,2048]{2,1,0:T(8,128)(2,1)} %bitcast.241), channel_id=1, source_target_pairs={{0,8},{8,0},{1,9},{9,1},{2,10},{10,2},{3,11},{11,3},{4,12},{12,4},... | collective-permute-start | bytes 3145736 | tf_op jit(solution)/shard_map/ppermute | solution.py:384
  410.8 20.6 %collective-permute-start.37 = (bf16[4,64,2048]{2,1,0:T(8,128)(2,1)}, bf16[4,64,2048]{2,1,0:T(8,128)(2,1)S(1)}, u32[]{:S(2)}, u32[]{:S(2)}) collective-permute-start(bf16[4,64,2048]{2,1,0:T(8,128)(2,1)} %bitcast.240), channel_id=1, source_target_pairs={{0,2},{2,0},{1,3},{3,1},{4,6},{6,4},{5,7},{7,5},{8,10},{10,8},{9,1... | collective-permute-start | bytes 3145736 | tf_op jit(solution)/shard_map/ppermute | solution.py:384
  479.5 17.1 %all-to-all-start.5 = ((bf16[8,192,256]{2,1,0:T(8,128)(2,1)}), bf16[8,192,256]{2,1,0:T(8,128)(2,1)S(1)}, u32[]{:S(2)}, u32[]{:S(2)}) async-start(bf16[8,192,256]{2,1,0:T(8,128)(2,1)} %bitcast.182), calls=%async_computation.5 | async-start | bytes 1572864 | tf_op jit(solution)/shard_map/all_to_all | solution.py:536
  483.1 127.0 %reduce-scatter.5.cloned.1.call-start = ((), (), s32[]{:S(2)}) async-start(), calls=%async_computation.13 | async-start | bytes 3932160 | tf_op jit(solution)/shard_map/reduce_scatter | solution.py:644
  517.1 191.4 %reduce-scatter.11.cloned.1.call-start = ((), (), s32[]{:S(2)}) async-start(), calls=%async_computation.16 | async-start | bytes 1966080 | tf_op jit(solution)/shard_map/reduce_scatter | solution.py:644
  522.5 36.9 %collective-permute-start.50 = (bf16[4,96,2048]{2,1,0:T(8,128)(2,1)}, bf16[4,96,2048]{2,1,0:T(8,128)(2,1)}, u32[]{:S(2)}, u32[]{:S(2)}) collective-permute-start(bf16[4,96,2048]{2,1,0:T(8,128)(2,1)} %bitcast.62), channel_id=1, source_target_pairs={{0,2},{2,0},{1,3},{3,1},{4,6},{6,4},{5,7},{7,5},{8,10},{10,8},{9,1... | collective-permute-start | bytes 4718600 | tf_op jit(solution)/shard_map/ppermute | solution.py:384
  524.4 36.5 %collective-permute-start.51 = (bf16[4,96,2048]{2,1,0:T(8,128)(2,1)}, bf16[4,96,2048]{2,1,0:T(8,128)(2,1)}, u32[]{:S(2)}, u32[]{:S(2)}) collective-permute-start(bf16[4,96,2048]{2,1,0:T(8,128)(2,1)} %bitcast.63), channel_id=1, source_target_pairs={{0,4},{4,0},{1,5},{5,1},{2,6},{6,2},{3,7},{7,3},{8,12},{12,8},{9,1... | collective-permute-start | bytes 4718600 | tf_op jit(solution)/shard_map/ppermute | solution.py:384
  567.7 42.4 %collective-permute-start.54 = (bf16[4,64,2048]{2,1,0:T(8,128)(2,1)}, bf16[4,64,2048]{2,1,0:T(8,128)(2,1)S(1)}, u32[]{:S(2)}, u32[]{:S(2)}) collective-permute-start(bf16[4,64,2048]{2,1,0:T(8,128)(2,1)} %get-tuple-element.418), channel_id=1, source_target_pairs={{0,2},{2,0},{1,3},{3,1},{4,6},{6,4},{5,7},{7,5},{8,10},{10,8},{9,1... | collective-permute-start | bytes 3145736 | tf_op jit(solution)/shard_map/ppermute | solution.py:384
  568.0 42.1 %collective-permute-start.55 = (bf16[4,64,2048]{2,1,0:T(8,128)(2,1)}, bf16[4,64,2048]{2,1,0:T(8,128)(2,1)}, u32[]{:S(2)}, u32[]{:S(2)}) collective-permute-start(bf16[4,64,2048]{2,1,0:T(8,128)(2,1)} %get-tuple-element.417), channel_id=1, source_target_pairs={{0,4},{4,0},{1,5},{5,1},{2,6},{6,2},{3,7},{7,3},{8,12},{12,8},{9,1... | collective-permute-start | bytes 3145736 | tf_op jit(solution)/shard_map/ppermute | solution.py:384
  572.8 37.4 %collective-permute-start.53 = (bf16[2,96,2048]{2,1,0:T(8,128)(2,1)}, bf16[2,96,2048]{2,1,0:T(8,128)(2,1)}, u32[]{:S(2)}, u32[]{:S(2)}) collective-permute-start(bf16[2,96,2048]{2,1,0:T(8,128)(2,1)} %slice.467), channel_id=1, source_target_pairs={{0,2},{2,0},{1,3},{3,1},{4,6},{6,4},{5,7},{7,5},{8,10},{10,8},{9,1... | collective-permute-start | bytes 2359304 | tf_op jit(solution)/shard_map/ppermute | solution.py:384
  577.4 32.7 %collective-permute-start.52 = (bf16[2,96,2048]{2,1,0:T(8,128)(2,1)S(1)}, bf16[2,96,2048]{2,1,0:T(8,128)(2,1)S(1)}, u32[]{:S(2)}, u32[]{:S(2)}) collective-permute-start(bf16[2,96,2048]{2,1,0:T(8,128)(2,1)S(1)} %slice.466), channel_id=1, source_target_pairs={{0,4},{4,0},{1,5},{5,1},{2,6},{6,2},{3,7},{7,3},{8,12},{12,8},{9,1... | collective-permute-start | bytes 2359304 | tf_op jit(solution)/shard_map/ppermute | solution.py:384
  613.8 29.1 %collective-permute-start.59 = (bf16[2,64,2048]{2,1,0:T(8,128)(2,1)}, bf16[2,64,2048]{2,1,0:T(8,128)(2,1)}, u32[]{:S(2)}, u32[]{:S(2)}) collective-permute-start(bf16[2,64,2048]{2,1,0:T(8,128)(2,1)} %slice.475), channel_id=1, source_target_pairs={{0,4},{4,0},{1,5},{5,1},{2,6},{6,2},{3,7},{7,3},{8,12},{12,8},{9,1... | collective-permute-start | bytes 1572872 | tf_op jit(solution)/shard_map/ppermute | solution.py:384
  616.1 26.8 %collective-permute-start.60 = (bf16[2,64,2048]{2,1,0:T(8,128)(2,1)}, bf16[2,64,2048]{2,1,0:T(8,128)(2,1)}, u32[]{:S(2)}, u32[]{:S(2)}) collective-permute-start(bf16[2,64,2048]{2,1,0:T(8,128)(2,1)} %slice.477), channel_id=1, source_target_pairs={{0,2},{2,0},{1,3},{3,1},{4,6},{6,4},{5,7},{7,5},{8,10},{10,8},{9,1... | collective-permute-start | bytes 1572872 | tf_op jit(solution)/shard_map/ppermute | solution.py:384
  618.9 15.9 %collective-permute-start.58 = (bf16[1,96,2048]{2,1,0:T(8,128)(2,1)}, bf16[1,96,2048]{2,1,0:T(8,128)(2,1)}, u32[]{:S(2)}, u32[]{:S(2)}) collective-permute-start(bf16[1,96,2048]{2,1,0:T(8,128)(2,1)} %slice.473), channel_id=1, source_target_pairs={{0,8},{8,0},{1,9},{9,1},{2,10},{10,2},{3,11},{11,3},{4,12},{12,4},... | collective-permute-start | bytes 1179656 | tf_op jit(solution)/shard_map/ppermute | solution.py:384
  621.6 21.3 %collective-permute-start.57 = (bf16[1,96,2048]{2,1,0:T(8,128)(2,1)}, bf16[1,96,2048]{2,1,0:T(8,128)(2,1)}, u32[]{:S(2)}, u32[]{:S(2)}) collective-permute-start(bf16[1,96,2048]{2,1,0:T(8,128)(2,1)} %slice.471), channel_id=1, source_target_pairs={{0,8},{8,0},{1,9},{9,1},{2,10},{10,2},{3,11},{11,3},{4,12},{12,4},... | collective-permute-start | bytes 1179656 | tf_op jit(solution)/shard_map/ppermute | solution.py:384
  622.2 83.4 %all-to-all-start.8 = ((bf16[8,64,1280]{2,1,0:T(8,128)(2,1)}), bf16[8,64,1280]{2,1,0:T(8,128)(2,1)S(1)}, u32[]{:S(2)}, u32[]{:S(2)}) async-start(bf16[8,64,1280]{2,1,0:T(8,128)(2,1)} %bitcast.239), calls=%async_computation.11 | async-start | bytes 2621440 | tf_op jit(solution)/shard_map/all_to_all | solution.py:536
  625.8 149.7 %reduce-scatter.7.cloned.1.call-start = ((), (), s32[]{:S(2)}) async-start(), calls=%async_computation.14 | async-start | bytes 2359296 | tf_op jit(solution)/shard_map/reduce_scatter | solution.py:644
  659.5 34.1 %collective-permute-start.64 = (bf16[2,8,64,768]{3,2,1,0:T(8,128)(2,1)}, bf16[2,8,64,768]{3,2,1,0:T(8,128)(2,1)}, u32[]{:S(2)}, u32[]{:S(2)}) collective-permute-start(bf16[2,8,64,768]{3,2,1,0:T(8,128)(2,1)} %dynamic-slice_bitcast_fusion.2), channel_id=1, source_target_pairs={{0,1},{1,0},{2,3},{3,2},{4,5},{5,4},{6,7},{7,6},{8,9},{9,8},{10,11... | collective-permute-start | bytes 4718600 | tf_op jit(solution)/shard_map/ppermute | solution.py:384
  659.5 25.9 %collective-permute-start.63 = (bf16[4,64,2048]{2,1,0:T(8,128)(2,1)}, bf16[4,64,2048]{2,1,0:T(8,128)(2,1)}, u32[]{:S(2)}, u32[]{:S(2)}) collective-permute-start(bf16[4,64,2048]{2,1,0:T(8,128)(2,1)} %bitcast.80), channel_id=1, source_target_pairs={{0,4},{4,0},{1,5},{5,1},{2,6},{6,2},{3,7},{7,3},{8,12},{12,8},{9,1... | collective-permute-start | bytes 3145736 | tf_op jit(solution)/shard_map/ppermute | solution.py:384
  661.0 27.3 %collective-permute-start.62 = (bf16[4,64,2048]{2,1,0:T(8,128)(2,1)}, bf16[4,64,2048]{2,1,0:T(8,128)(2,1)}, u32[]{:S(2)}, u32[]{:S(2)}) collective-permute-start(bf16[4,64,2048]{2,1,0:T(8,128)(2,1)} %bitcast.78), channel_id=1, source_target_pairs={{0,8},{8,0},{1,9},{9,1},{2,10},{10,2},{3,11},{11,3},{4,12},{12,4},... | collective-permute-start | bytes 3145736 | tf_op jit(solution)/shard_map/ppermute | solution.py:384
  661.0 30.0 %collective-permute-start.61 = (bf16[4,64,2048]{2,1,0:T(8,128)(2,1)}, bf16[4,64,2048]{2,1,0:T(8,128)(2,1)}, u32[]{:S(2)}, u32[]{:S(2)}) collective-permute-start(bf16[4,64,2048]{2,1,0:T(8,128)(2,1)} %bitcast.76), channel_id=1, source_target_pairs={{0,2},{2,0},{1,3},{3,1},{4,6},{6,4},{5,7},{7,5},{8,10},{10,8},{9,1... | collective-permute-start | bytes 3145736 | tf_op jit(solution)/shard_map/ppermute | solution.py:384
  698.4 49.7 %collective-permute-start.68 = (bf16[2,64,2048]{2,1,0:T(8,128)(2,1)}, bf16[2,64,2048]{2,1,0:T(8,128)(2,1)}, u32[]{:S(2)}, u32[]{:S(2)}) collective-permute-start(bf16[2,64,2048]{2,1,0:T(8,128)(2,1)} %slice.438), channel_id=1, source_target_pairs={{0,8},{8,0},{1,9},{9,1},{2,10},{10,2},{3,11},{11,3},{4,12},{12,4},... | collective-permute-start | bytes 1572872 | tf_op jit(solution)/shard_map/ppermute | solution.py:384
  699.0 43.8 %collective-permute-start.65 = (bf16[96,2048]{1,0:T(8,128)(2,1)}, bf16[96,2048]{1,0:T(8,128)(2,1)}, u32[]{:S(2)}, u32[]{:S(2)}) collective-permute-start(bf16[96,2048]{1,0:T(8,128)(2,1)} %get-tuple-element.375), channel_id=1, source_target_pairs={{0,16},{16,0},{1,17},{17,1},{2,18},{18,2},{3,19},{19,3},{4,20},{20... | collective-permute-start | bytes 1179656 | tf_op jit(solution)/shard_map/ppermute | solution.py:384
  705.6 37.1 %all-to-all-start.6 = ((f32[32,1,160]{2,1,0:T(1,128)}), f32[32,1,160]{2,1,0:T(1,128)S(1)}, u32[]{:S(2)}, u32[]{:S(2)}) async-start(f32[32,1,160]{2,1,0:T(1,128)} %all_to_all.40), calls=%async_computation.7 | async-start | bytes 65536 | tf_op jit(solution)/shard_map/all_to_all | solution.py:568
  708.2 86.4 %reduce-scatter.9.cloned.1.call-start = ((), (), s32[]{:S(2)}) async-start(), calls=%async_computation.15 | async-start | bytes 786432 | tf_op jit(solution)/shard_map/reduce_scatter | solution.py:644
  713.6 35.7 %collective-permute-start.67 = (bf16[2,64,2048]{2,1,0:T(8,128)(2,1)}, bf16[2,64,2048]{2,1,0:T(8,128)(2,1)}, u32[]{:S(2)}, u32[]{:S(2)}) collective-permute-start(bf16[2,64,2048]{2,1,0:T(8,128)(2,1)} %slice.436), channel_id=1, source_target_pairs={{0,2},{2,0},{1,3},{3,1},{4,6},{6,4},{5,7},{7,5},{8,10},{10,8},{9,1... | collective-permute-start | bytes 1572872 | tf_op jit(solution)/shard_map/ppermute | solution.py:384
  716.1 34.6 %collective-permute-start.66 = (bf16[2,64,2048]{2,1,0:T(8,128)(2,1)}, bf16[2,64,2048]{2,1,0:T(8,128)(2,1)}, u32[]{:S(2)}, u32[]{:S(2)}) collective-permute-start(bf16[2,64,2048]{2,1,0:T(8,128)(2,1)} %slice.434), channel_id=1, source_target_pairs={{0,4},{4,0},{1,5},{5,1},{2,6},{6,2},{3,7},{7,3},{8,12},{12,8},{9,1... | collective-permute-start | bytes 1572872 | tf_op jit(solution)/shard_map/ppermute | solution.py:384
  718.4 33.5 %collective-permute-start.69 = (bf16[1,64,2048]{2,1,0:T(8,128)(2,1)}, bf16[1,64,2048]{2,1,0:T(8,128)(2,1)}, u32[]{:S(2)}, u32[]{:S(2)}) collective-permute-start(bf16[1,64,2048]{2,1,0:T(8,128)(2,1)} %slice.439), channel_id=1, source_target_pairs={{0,8},{8,0},{1,9},{9,1},{2,10},{10,2},{3,11},{11,3},{4,12},{12,4},... | collective-permute-start | bytes 786440 | tf_op jit(solution)/shard_map/ppermute | solution.py:384
  742.8 19.8 %collective-permute-start.70 = (bf16[1,64,2048]{2,1,0:T(8,128)(2,1)}, bf16[1,64,2048]{2,1,0:T(8,128)(2,1)S(1)}, u32[]{:S(2)}, u32[]{:S(2)}) collective-permute-start(bf16[1,64,2048]{2,1,0:T(8,128)(2,1)} %slice.440), channel_id=1, source_target_pairs={{0,8},{8,0},{1,9},{9,1},{2,10},{10,2},{3,11},{11,3},{4,12},{12,4},... | collective-permute-start | bytes 786440 | tf_op jit(solution)/shard_map/ppermute | solution.py:384
  775.5 31.4 %all-to-all-start.7 = ((bf16[8,64,768]{2,1,0:T(8,128)(2,1)}), bf16[8,64,768]{2,1,0:T(8,128)(2,1)S(1)}, u32[]{:S(2)}, u32[]{:S(2)}) async-start(bf16[8,64,768]{2,1,0:T(8,128)(2,1)} %bitcast.242), calls=%async_computation.9 | async-start | bytes 1572864 | tf_op jit(solution)/shard_map/all_to_all | solution.py:536
  782.1 23.8 %collective-permute-start.74 = (bf16[96,2048]{1,0:T(8,128)(2,1)S(1)}, bf16[96,2048]{1,0:T(8,128)(2,1)S(1)}, u32[]{:S(2)}, u32[]{:S(2)}) collective-permute-start(bf16[96,2048]{1,0:T(8,128)(2,1)S(1)} %get-tuple-element.428), channel_id=1, source_target_pairs={{0,16},{16,0},{1,17},{17,1},{2,18},{18,2},{3,19},{19,3},{4,20},{20... | collective-permute-start | bytes 1179656 | tf_op jit(solution)/shard_map/ppermute | solution.py:384
  (140 other events, 1311.2 us)
Sparse Core Ops, SparseCore 0:
  170.3 68.2 all-gather.4
  270.7 40.0 all-gather.6
  517.2 69.8 reduce-scatter.4
  589.9 37.2 reduce-scatter.10
  705.7 52.9 reduce-scatter.6
  768.6 25.9 reduce-scatter.8

commit v3 on v2

--- a/solution.py
+++ b/solution.py
@@ -563,11 +563,6 @@
     return lax.all_to_all(jnp.broadcast_to(line, (count,) + line.shape), AXES, 0, 0)
 
 
-def sum_line(line):
-    count = lax.axis_size(AXES)
-    return jnp.sum(lax.all_to_all(line.reshape(count, -1), AXES, 0, 0), axis=0)
-
-
 def wire_halves(shard):
     if lax.axis_size("b") == 1:
         return swap(shard, "h")
@@ -578,6 +573,54 @@
     if lax.axis_size("b") == 1:
         return swap(shard[:4], "h"), swap(shard[4:], "h")
     return (wire_halves(shard),)
+
+
+def turned_kernel(left, right, out):
+    def block(i, _):
+        cols = pl.ds(pl.multiple_of(i * BLK, BLK), BLK)
+        out[cols, :] = dot(left[:, cols].T, right[...]).astype(out.dtype)
+        return 0
+
+    lax.fori_loop(0, left.shape[1] // BLK, block, 0)
+
+
+def turned_matmul(left, right):
+    return pl.pallas_call(
+        turned_kernel,
+        out_shape=jax.ShapeDtypeStruct((left.shape[1], right.shape[1]), LOW),
+        in_specs=specs(0, 2),
+        out_specs=specs(0, 1)[0],
+        compiler_params=pltpu.CompilerParams(vmem_limit_bytes=40 << 20),
+        cost_estimate=pl.CostEstimate(flops=0, bytes_accessed=1 << 16, transcendentals=0),
+    )(left, right)
+
+
+def scaled_kernel(left, right, scale, out):
+    step = 64
+    out[...] = jnp.zeros_like(out)
+
+    def block(i, _):
+        rows = pl.ds(pl.multiple_of(i * step, step), step)
+        part = left[rows, :].astype(jnp.float32) * scale[rows, :] * right[rows, :].astype(jnp.float32)
+        total = part[0:8]
+        for j in range(1, step // 8):
+            total = total + part[8 * j : 8 * j + 8]
+        out[...] += total
+        return 0
+
+    lax.fori_loop(0, left.shape[0] // step, block, 0)
+
+
+def scaled_sum(left, right, scale):
+    eight = pl.pallas_call(
+        scaled_kernel,
+        out_shape=jax.ShapeDtypeStruct((8, left.shape[1]), F32),
+        in_specs=specs(0, 3),
+        out_specs=specs(0, 1)[0],
+        compiler_params=pltpu.CompilerParams(vmem_limit_bytes=40 << 20),
+        cost_estimate=pl.CostEstimate(flops=0, bytes_accessed=1 << 16, transcendentals=0),
+    )(left, right, scale)
+    return jnp.sum(eight, axis=0)
 
 
 def light_distance(part, i):
@@ -985,14 +1028,11 @@
     saved = (first, (mixed_t, level))
     if not one_block:
         mixed = jnp.split(as_pieces(mixed[0], chunk_at), 2, axis=0)
-    mixed, mixed_other, out_chunks, feed_out, res_wires, expand_halves = fence(
-        *mixed, out_chunks, feed_out, res_wires, expand_halves
-    )
+    mixed, mixed_other, out_chunks, feed_out, expand_halves = fence(*mixed, out_chunks, feed_out, expand_halves)
     down_halves = gather_halves(feed_out)
     mixed_wire = swap(mixed_other, "c")
+    mixed, mixed_wire, out_chunks, expand_halves = fence(mixed, mixed_wire, out_chunks, expand_halves)
     out_wire = swap(out_chunks, "c") if one_block else ()
-    res_parts = gather_join(res_parts, res_wires)
-    mixed, mixed_wire, res_parts, out_wire = fence(mixed, mixed_wire, res_parts, out_wire)
     mixed = both(mixed, mixed_wire, at["c"], 1, joined=True)
     mixed = exchange(mixed.reshape(8, 2 * rows, 2 * span))
     expand_core = swap(expand_halves, "c")
@@ -1001,7 +1041,8 @@
         out_full = weave(pieces, at, 16, False).reshape(-1, width)
     else:
         out_full = fetch_out_wide(attention_out)
-    mixed, out_full, expand_core = fence(mixed, out_full, expand_core)
+    mixed, out_full, expand_core, res_wires = fence(mixed, out_full, expand_core, res_wires)
+    res_parts = gather_join(res_parts, res_wires)
     mixed_chunks = mixed.reshape(16 * rows, 2 * span)
     res_wires = gather_send(res_parts, 1)
     mixed = mixed.transpose(1, 0, 2).reshape(2 * rows, -1)
@@ -1013,12 +1054,12 @@
     normed_two, mixed = fence(normed_two, mixed)
     parts = gather_step(thirds(normed_two), 0)
     expand = weave_halves(expand_halves, expand_core, at).reshape(width, -1)
-    parts, expand, res_wires, down_halves = fence(parts, expand, res_wires, down_halves)
-    res_parts = gather_join(res_parts, res_wires)
+    parts, expand, down_halves = fence(parts, expand, down_halves)
     down_core = swap(down_halves, "c")
     parts = gather_step(parts, 1)
-    (parts,) = fence(parts)
+    parts, res_wires = fence(parts, res_wires)
     parts = gather_step(parts, 2)
+    res_parts = gather_join(res_parts, res_wires)
     res_wires = gather_send(res_parts, 2)
     down = weave_halves(down_halves[:, None], down_core[:, None], at).reshape(hidden_here, width)
     parts, down = fence(parts, down)
@@ -1100,16 +1141,16 @@
         d_own, d_other = jnp.split(as_pieces(d_all.astype(LOW), spread_at), 2, axis=0)
     d_own, d_other, final_wires, out_wires, grad_expand = fence(d_own, d_other, final_wires, out_wires, grad_expand)
     d_other = swap(d_other, "c")
-    final_parts = reduce_add(final_parts, final_wires)
-    final_wires = light_send(final_parts)
+    final_parts = jnp.stack(reduce_add(final_parts, final_wires))
+    final_wires = swap(final_parts[:, 1], "p")
     if one_block:
         out_parts = reduce_add(out_parts, out_wires)
         out_wires = light_send(out_parts)
     (d_other,) = fence(d_other)
     grad_projected = jnp.concatenate([d_own, d_other], axis=1)
     grad_normed_one = matmul(grad_projected, project, NT).astype(LOW)
-    grad_normed_one, grad_projected, final_wires, out_wires, final_parts, out_parts = fence(
-        grad_normed_one, grad_projected, final_wires, out_wires, final_parts, out_parts
+    grad_normed_one, grad_projected, final_wires, out_wires, final_parts, out_parts, grad_down = fence(
+        grad_normed_one, grad_projected, final_wires, out_wires, final_parts, out_parts, grad_down
     )
 
     def turn(got):
@@ -1117,11 +1158,8 @@
 
     parts = reduce_step(to_parts(grad_normed_one), 2)
     grad_expand = exchange(grad_expand)
-    grad_project = matmul(normed_one, grad_projected, TN).astype(LOW).reshape(halves, 8, 2, shard_rows, -1)
-    project_wire = send_cores(grad_project, at, 2)
-    grad_project = add_cores(grad_project, turn(project_wire), at, 2)
-    moved = grad_normed_one.astype(F32) * gathered_scale * gathered.astype(F32)
-    grad_gain_rows = jnp.sum(moved, axis=0)
+    grad_project = turned_matmul(normed_one, grad_projected).reshape(halves, 8, 2, shard_rows, -1)
+    grad_gain_rows = scaled_sum(grad_normed_one, gathered, gathered_scale)
     grad_feed_gain = jnp.sum(grad_normed_two * unit_two, axis=0)
     sums = jnp.concatenate([d_diag_first, d_diag], axis=0)
     hot = buckets == jnp.arange(BUCKETS, dtype=jnp.int32)[:, None]
@@ -1132,35 +1170,41 @@
     gains = attention_norm_gain.shape[0]
     small = [grad_feed_gain, grad_gain_rows, grad_position_bias]
     small = jnp.concatenate([line.reshape(count, -1) for line in small], axis=1)
-    final_near, final_far = [part[0].astype(F32) for part in reduce_add(final_parts, final_wires)]
+    final_near, final_far = (final_parts[:, 0].astype(F32) + final_wires.astype(F32)).astype(LOW).astype(F32)
     final_near = (hidden_one[:rows] + final_near).astype(LOW)
     final_far = (hidden_one[rows:] + final_far).astype(LOW)
-    if one_block:
-        out_parts = reduce_add(out_parts, out_wires)
-    parts, small, final_far, grad_project, out_parts = fence(parts, small, final_far, grad_project, out_parts)
-    grad_project = scatter_halves(grad_project)
-    small = sum_line(small)
+    final_far = swap(final_far, "h")
+    if one_block:
+        out_parts = jnp.stack(reduce_add(out_parts, out_wires))
+    parts, small, final_far, grad_project, out_parts, grad_expand = fence(
+        parts, small, final_far, grad_project, out_parts, grad_expand
+    )
+    project_wire = send_cores(grad_project, at, 2)
     parts = reduce_step(parts, 1)
-    final_far = swap(final_far, "h")
-    if one_block:
-        out_wires = light_send(out_parts)
-    parts, small, out_wires = fence(parts, small, out_wires)
+    grad_project = scatter_halves(add_cores(grad_project, turn(project_wire), at, 2))
+    (parts,) = fence(parts)
+    if one_block:
+        out_wires = swap(out_parts[:, 1], "p")
     parts = reduce_step(parts, 0)
-    if one_block:
-        grad_out = scatter_halves(jnp.concatenate(reduce_add(out_parts, out_wires), axis=0))
-    parts, grad_project = fence(parts, grad_project)
+    parts, out_wires, grad_project, small = fence(parts, out_wires, grad_project, small)
+    grad_project = exchange(grad_project)
+    if one_block:
+        out_halves = (out_parts[:, 0].astype(F32) + out_wires.astype(F32)).astype(LOW)
+        out_wires = send_halves(out_halves, at)
     grad_part = own_rows(parts)
     unit_one, scale_one = normalize(tokens_here)
     token_grad = grad_hidden + norm_back(grad_part * gain_attn, unit_one, scale_one)
     token_grad = token_grad.astype(LOW)
-    input_grad = both(token_grad[:rows], swap(token_grad[rows:], "h"), near, 0)
-    grad_project = exchange(grad_project)
+    token_wire = swap(token_grad[rows:], "h")
+    grad_project, small = fence(grad_project, small)
+    small = jnp.sum(lax.all_to_all(small, AXES, 0, 0), axis=0)
+    input_grad = both(token_grad[:rows], token_wire, near, 0)
     layer_output = both(final_near, final_far, near, 0)
     grad_expand = join_columns(grad_expand, expand_order, 2 * hidden_shard)
     grad_feed_gain = small[:gains]
     grad_attention_gain = small[gains : 2 * gains]
     grad_position_bias = small[2 * gains :]
-    grad_out = grad_out.astype(F32) if one_block else grad_out_wide(grad_out)
+    grad_out = add_halves(out_halves, out_wires, at) if one_block else grad_out_wide(grad_out)
     grad_down = grad_down.astype(F32)
     grad_project = jnp.where(at["c"] == 0, grad_project, turn(grad_project))
     grad_project = join_columns(grad_project, project_order, span)

time: 825 us -> 810 us (0.982)
  waiting for transfers between devices: 270 us -> 245 us
  Pallas kernels: 135 us -> 158 us
  starting transfers between devices: 125 us -> 116 us
    all_gather x2, waiting for transfers between devices: 3.05 us -> 23.9 us  [gather_halves(): return lax.all_gather(shard, ('b', 'h'), axis=0)]
    ppermute x75 -> x74, waiting for transfers between devices: 221 us -> 203 us  [swap(): return lax.ppermute(value, axis, SWAP)]
    all_to_all x1, waiting for transfers between devices: 22.1 us -> 5.72 us  [local(): small = jnp.sum(lax.all_to_all(small, AXES, 0, 0), axis=0)]
    another operation x0 -> x6, other arithmetic: none -> 11.3 us  [the longest x3 6.24 us: local(): out_parts = jnp.stack(reduce_add(out_parts, out_wires))]
    pallas_call x0 -> x2, Pallas kernels: none -> 10.7 us  [the longest x1 6.88 us: turned_matmul(): pl.pallas_call(turned_kernel, out_shape=jax.ShapeDtypeStruct((left.shape[...]
    reduce_scatter x4 -> x3, waiting for transfers between devices: 9.97 us -> 0.02 us  [scatter_halves(): return lax.psum_scatter(parts, ('b', 'h'), scatter_dimension=0, tiled=False)]
    ppermute x75 -> x74, starting transfers between devices: 89.7 us -> 80.5 us  [swap(): return lax.ppermute(value, axis, SWAP)]
    convert_element_type x27 -> x21, other arithmetic: 35.8 us -> 27 us  [reduce_add(): (a[:half].astype(F32) + b.astype(F32)).astype(LOW)]
  transfers between devices with their start and end apart: 90 -> 88, of which waited for: 40 -> 39; matrix products, arithmetic and copies ran while one was open for 22% -> 21% of each run, Pallas kernels for 16% -> 19%
where the time goes in v3:
time: 810 us; the launch traced here: 802 us
  waiting for transfers between devices  245 us (30%)
  Pallas kernels  158 us (20%)
  starting transfers between devices  116 us (14%)
  matrix products  93.1 us (11%)
  local copies, waits for them, and re-layouts  87.9 us (11%)
  other arithmetic  86.1 us (11%)
  between operations  15.8 us (2%)
    ppermute x74, waiting for transfers between devices, swap(): return lax.ppermute(value, axis, SWAP)  203 us
    dot_general x11, matrix products, matmul(): return lax.dot_general(left, right, dims, preferred_element_type=F32)  93.1 us
    ppermute x74, starting transfers between devices, swap(): return lax.ppermute(value, axis, SWAP)  80.5 us
    pallas_call x2, Pallas kernels, attend_backward(): pl.pallas_call(lambda *refs: backward_kernel(local, halo, n, *refs), out_...  66.5 us
    pallas_call x2, Pallas kernels, attend_forward(): pl.pallas_call(lambda *refs: forward_kernel(local, halo, n, *refs), out_s...  53.1 us
    unnamed x237, local copies, waits for them, and re-layouts  47 us
    all_to_all x7, starting transfers between devices, exchange(): return lax.all_to_all(chunks, CUBE, 0, 0)  28.6 us
    convert_element_type x21, other arithmetic, reduce_add(): (a[:half].astype(F32) + b.astype(F32)).astype(LOW)  27 us
  transfers between devices with their start and end apart: 88, of which 39 were waited for; matrix products, arithmetic and copies ran while one was open for 21% of the time, Pallas kernels for 19%

profile of v3, /device:TPU:0, one launch (start us, length us, event | category | flops | bytes accessed | tf_op | source)
XLA Modules:
  0.0 801.7 jit_solution(3741623739693960742)
XLA Ops:
  9.3 4.0 collective-permute-start
  19.2 3.8 all-to-all-start
  26.5 7.5 all-to-all-done
  34.2 3.6 all-to-all-start.1
  47.6 12.2 %collective-permute-done.1.refs_1_ = bf16[1,64,2048]{2,1,0:T(8,128)(2,1)S(1)} collective-permute-done((bf16[1,64,2048]{2,1,0:T(8,128)(2,1)S(1)}, bf16[1,64,2048]{2,1,0:T(8,128)(2,1)S(1)}, u32[]{:S(2)}, u32[]{:S(2)}) %collective-permute-start.1) | collective-permute-done | bytes 262176 | tf_op jit(solution)/shard_map/ppermute | solution.py:384
  71.4 6.0 collective-permute-done.5.refs_1_
  78.4 13.7 %collective-permute-done.7.refs_5_ = bf16[2,64,2048]{2,1,0:T(8,128)(2,1)S(1)} collective-permute-done((bf16[2,64,2048]{2,1,0:T(8,128)(2,1)S(1)}, bf16[2,64,2048]{2,1,0:T(8,128)(2,1)S(1)}, u32[]{:S(2)}, u32[]{:S(2)}) %collective-permute-start.7) | collective-permute-done | bytes 524320 | tf_op jit(solution)/shard_map/ppermute | solution.py:384
  95.8 3.6 collective-permute-done.8.refs_1_
  103.3 2.9 shard_map.265
  109.4 3.0 collective-permute-start.12
  112.5 20.6 %collective-permute-done.10.refs_3_ = bf16[4,64,2048]{2,1,0:T(8,128)(2,1)} collective-permute-done((bf16[4,64,2048]{2,1,0:T(8,128)(2,1)}, bf16[4,64,2048]{2,1,0:T(8,128)(2,1)}, u32[]{:S(2)}, u32[]{:S(2)}) %collective-permute-start.10) | collective-permute-done | bytes 1048608 | tf_op jit(solution)/shard_map/ppermute | solution.py:384
  140.5 4.7 all-to-all-start.2
  156.4 7.1 convolution_convert_fusion.5
  166.2 5.1 all-to-all-start.3
  177.2 25.6 %shard_map.269 = (f32[64,3072]{1,0:T(8,128)}, f32[1,3072]{1,0:T(1,128)}) custom-call(s32[96]{0:T(128)} %multiply_add_fusion.2.refs_0_, s32[32]{0:T(128)} %add_multiply_fusion.1.refs_1_, s32[2,12]{1,0:T(2,128)} %copy-done.38, bf16[1536,384]{1,0:T(8,128)(2,1)} %get-tuple-element.249.refs_3_, bf16[1536,384]{1,0:T(8,128)(2,1)} %copy-done.43, ...), custom_call_target="tpu_custom_call" | custom-call | flops 3072 | bytes 65536 | tf_op jit(solution)/shard_map/pallas_call | solution.py:306
  202.8 27.4 %shard_map.270 = (bf16[1536,128]{1,0:T(8,128)(2,1)}, bf16[1536,128]{1,0:T(8,128)(2,1)}, f32[64,3072]{1,0:T(8,128)}, f32[1,3072]{1,0:T(1,128)}) custom-call(s32[96]{0:T(128)} %multiply_add_fusion.2.refs_0_, s32[32]{0:T(128)} %add_multiply_fusion.1.refs_1_, s32[2,12]{1,0:T(2,128)} %copy-done.38, bf16[1536,384]{1,0:T(8,128)(2,1)} %get-tuple-element.249.refs_3_, ...), custom_call_target="tpu_custom_call" | custom-call | flops 3072 | bytes 65536 | tf_op jit(solution)/shard_map/pallas_call | solution.py:306
  230.3 12.3 %all-gather.5.cloned.1.call-done = bf16[16,64,1280]{2,1,0:T(8,128)(2,1)} async-done(((bf16[8,64,1280]{2,1,0:T(8,128)(2,1)}), bf16[16,64,1280]{2,1,0:T(8,128)(2,1)}) %all-gather.5.cloned.1.call-update) | async-done | bytes 2621456 | tf_op jit(solution)/shard_map/all_gather | solution.py:683
  242.6 4.7 all-to-all-done.3
  252.0 3.8 all-to-all-start.4
  266.0 4.1 shard_map.271
  270.1 3.3 copy-done.7
  273.5 5.5 multiply_reduce_fusion
  286.1 5.7 collective-permute-done.21.refs_1_
  291.9 11.5 %all-gather.7.cloned.1.call-done = bf16[320,2048]{1,0:T(8,128)(2,1)} async-done(((bf16[160,2048]{1,0:T(8,128)(2,1)}), bf16[320,2048]{1,0:T(8,128)(2,1)}) %all-gather.7.cloned.1.call-update) | async-done | bytes 1310736 | tf_op jit(solution)/shard_map/all_gather | solution.py:683
  309.0 9.3 %collective-permute-done.24.refs_1_ = bf16[2,64,2048]{2,1,0:T(8,128)(2,1)S(1)} collective-permute-done((bf16[2,64,2048]{2,1,0:T(8,128)(2,1)S(1)}, bf16[2,64,2048]{2,1,0:T(8,128)(2,1)S(1)}, u32[]{:S(2)}, u32[]{:S(2)}) %collective-permute-start.24) | collective-permute-done | bytes 524320 | tf_op jit(solution)/shard_map/ppermute | solution.py:384
  319.8 3.5 collective-permute-done.26.refs_5_
  323.6 4.8 collective-permute-done.27.refs_1_
  329.6 2.9 collective-permute-done.29.refs_5_
  339.9 18.8 %collective-permute-done.30.refs_1_ = bf16[4,64,2048]{2,1,0:T(8,128)(2,1)S(1)} collective-permute-done((bf16[4,64,2048]{2,1,0:T(8,128)(2,1)S(1)}, bf16[4,64,2048]{2,1,0:T(8,128)(2,1)S(1)}, u32[]{:S(2)}, u32[]{:S(2)}) %collective-permute-start.30) | collective-permute-done | bytes 1048608 | tf_op jit(solution)/shard_map/ppermute | solution.py:384
  362.7 10.3 %fusion.69 = f32[1536,1280]{1,0:T(8,128)} fusion(bf16[1536,2048]{1,0:T(8,128)(2,1)S(1)} %shard_map.278, bf16[2048,1280]{1,0:T(8,128)(2,1)S(1)} %bitcast.216), kind=kOutput, calls=%fused_computation.193 | convolution fusion | flops 8053063680 | bytes 19398656 | tf_op jit(solution)/shard_map/dot_general | solution.py:397
  373.0 4.7 multiply_convert_fusion.1.src
  382.9 13.6 %fusion.8 = (bf16[1536,640]{1,0:T(8,128)(2,1)S(1)}, bf16[1536,640]{1,0:T(8,128)(2,1)}) fusion(f32[1536,1280]{1,0:T(8,128)} %fusion.69, bf16[1536,2048]{1,0:T(8,128)(2,1)S(1)} %shard_map.281, bf16[640,2048]{1,0:T(8,128)(2,1)S(1)} %bitcast.220), kind=kOutput, calls=%fused_computation.22 | convolution fusion | flops 4054056960 | bytes 20709376 | tf_op jit(solution)/shard_map/dot_general | solution.py:397
  396.5 10.4 %convolution_convert_fusion.3 = bf16[1536,2048]{1,0:T(8,128)(2,1)S(1)} fusion(bf16[2048,1280]{1,0:T(8,128)(2,1)S(1)} %bitcast.217, bf16[1536,640]{1,0:T(8,128)(2,1)} %get-tuple-element.400, bf16[1536,640]{1,0:T(8,128)(2,1)S(1)} %get-tuple-element.399), kind=kOutput, calls=%fused_computation.10 | convolution fusion | flops 8064073728 | bytes 15466496 | tf_op jit(solution)/shard_map/dot_general | solution.py:397
  413.3 7.1 convolution_convert_fusion.6
  420.4 12.2 %collective-permute-done.39 = bf16[4,64,2048]{2,1,0:T(8,128)(2,1)} collective-permute-done((bf16[4,64,2048]{2,1,0:T(8,128)(2,1)}, bf16[4,64,2048]{2,1,0:T(8,128)(2,1)}, u32[]{:S(2)}, u32[]{:S(2)}) %collective-permute-start.39) | collective-permute-done | bytes 1048608 | tf_op jit(solution)/shard_map/ppermute | solution.py:384
  437.5 7.4 convolution_convert_fusion.2
  447.6 7.8 collective-permute-done.41
  455.5 4.7 collective-permute-done.40
  475.5 6.9 convolution_convert_fusion.7
  483.3 3.5 all-to-all-start.5
  486.9 13.4 %convolution_convert_fusion.1 = bf16[2048,1280]{1,0:T(8,128)(2,1)} fusion(bf16[1536,2048]{1,0:T(8,128)(2,1)} %copy-done.8, bf16[1536,640]{1,0:T(8,128)(2,1)} %get-tuple-element.400, bf16[1536,640]{1,0:T(8,128)(2,1)} %copy-done.108), kind=kOutput, calls=%fused_computation.8 | convolution fusion | flops 8063549440 | bytes 15466496 | tf_op jit(solution)/shard_map/dot_general | solution.py:397
  503.4 4.8 copy-done.57
  509.8 5.0 collective-permute-done.47.refs_9_
  517.2 5.4 fusion.60
  526.1 32.4 %shard_map.284 = (bf16[3072,128]{1,0:T(8,128)(2,1)}, bf16[3072,128]{1,0:T(8,128)(2,1)}, bf16[3072,128]{1,0:T(8,128)(2,1)}, f32[1,2560]{1,0:T(1,128)}) custom-call(s32[96]{0:T(128)} %multiply_add_fusion.2.refs_0_, s32[32]{0:T(128)} %add_multiply_fusion.1.refs_1_, s32[2,12]{1,0:T(2,128)} %copy-done.38, bf16[1536,384]{1,0:T(8,128)(2,1)} %get-tuple-element.249.refs_3_, ...), custom_call_target="tpu_custom_call" | custom-call | flops 3072 | bytes 65536 | tf_op jit(solution)/shard_map/pallas_call | solution.py:344
  560.9 5.5 fusion.3
  579.7 34.2 %shard_map.285 = (bf16[1536,384]{1,0:T(8,128)(2,1)}, bf16[1536,384]{1,0:T(8,128)(2,1)}, f32[1,2560]{1,0:T(1,128)}) custom-call(s32[96]{0:T(128)} %multiply_add_fusion.2.refs_0_, s32[32]{0:T(128)} %add_multiply_fusion.1.refs_1_, s32[2,12]{1,0:T(2,128)} %copy-done.38, bf16[1536,384]{1,0:T(8,128)(2,1)} %get-tuple-element.249.refs_3_, ...), custom_call_target="tpu_custom_call" | custom-call | flops 3072 | bytes 65536 | tf_op jit(solution)/shard_map/pallas_call | solution.py:344
  615.0 3.2 fusion.18
  627.0 4.3 all-to-all-start.6
  634.1 9.0 %convolution_convert_fusion.left = bf16[1536,2048]{1,0:T(8,128)(2,1)} fusion(bf16[2048,768]{1,0:T(8,128)(2,1)S(1)} %bitcast.219, bf16[1536,384]{1,0:T(8,128)(2,1)} %collective-permute-done.56, bf16[1536,384]{1,0:T(8,128)(2,1)} %get-tuple-element.359), kind=kOutput, calls=%fused_computation.7 | convolution fusion | flops 4839702528 | bytes 11796480 | tf_op jit(solution)/shard_map/dot_general | solution.py:397
  643.1 3.0 pad_maximum_fusion.3.right
  649.5 3.2 fusion.59
  661.5 6.9 shard_map.287
  671.2 3.8 shard_map.286
  682.7 7.3 collective-permute-done.61
  705.8 9.2 %collective-permute-done.66 = bf16[2,64,2048]{2,1,0:T(8,128)(2,1)} collective-permute-done((bf16[2,64,2048]{2,1,0:T(8,128)(2,1)}, bf16[2,64,2048]{2,1,0:T(8,128)(2,1)}, u32[]{:S(2)}, u32[]{:S(2)}) %collective-permute-start.66) | collective-permute-done | bytes 524320 | tf_op jit(solution)/shard_map/ppermute | solution.py:384
  722.7 3.1 shard_map.289
  728.9 5.4 collective-permute-done.68
  735.2 16.5 %collective-permute-done.67 = bf16[1,64,2048]{2,1,0:T(8,128)(2,1)S(1)} collective-permute-done((bf16[1,64,2048]{2,1,0:T(8,128)(2,1)S(1)}, bf16[1,64,2048]{2,1,0:T(8,128)(2,1)S(1)}, u32[]{:S(2)}, u32[]{:S(2)}) %collective-permute-start.67) | collective-permute-done | bytes 262176 | tf_op jit(solution)/shard_map/ppermute | solution.py:384
  754.1 3.5 all-to-all-start.7
  760.9 3.0 collective-permute-start.72
  763.9 3.1 collective-permute-done.73
  768.7 13.5 %collective-permute-done.72 = bf16[96,2048]{1,0:T(8,128)(2,1)S(1)} collective-permute-done((bf16[96,2048]{1,0:T(8,128)(2,1)S(1)}, bf16[96,2048]{1,0:T(8,128)(2,1)S(1)}, u32[]{:S(2)}, u32[]{:S(2)}) %collective-permute-start.72) | collective-permute-done | bytes 393248 | tf_op jit(solution)/shard_map/ppermute | solution.py:384
  788.1 5.7 all-to-all-done.8
  (538 shorter events, 251.8 us)
Async XLA Ops:
  9.3 24.9 %collective-permute-start = (bf16[96,2048]{1,0:T(8,128)(2,1)}, bf16[96,2048]{1,0:T(8,128)(2,1)S(1)}, u32[]{:S(2)}, u32[]{:S(2)}) collective-permute-start(bf16[96,2048]{1,0:T(8,128)(2,1)} %get-tuple-element.436), channel_id=1, source_target_pairs={{0,16},{16,0},{1,17},{17,1},{2,18},{18,2},{3,19},{19,3},{4,20},{20... | collective-permute-start | bytes 1179656 | tf_op jit(solution)/shard_map/ppermute | solution.py:384
  19.2 14.8 %all-to-all-start = ((bf16[32,2,320]{2,1,0:T(2,128)(2,1)}), bf16[32,2,320]{2,1,0:T(2,128)(2,1)S(1)}, u32[]{:S(2)}, u32[]{:S(2)}) async-start(bf16[32,2,320]{2,1,0:T(2,128)(2,1)} %reshape.307), calls=%async_computation | async-start | bytes 98304 | tf_op jit(solution)/shard_map/all_to_all | solution.py:563
  34.2 29.2 %all-to-all-start.1 = ((bf16[8,64,768]{2,1,0:T(8,128)(2,1)}), bf16[8,64,768]{2,1,0:T(8,128)(2,1)S(1)}, u32[]{:S(2)}, u32[]{:S(2)}) async-start(bf16[8,64,768]{2,1,0:T(8,128)(2,1)} %shard_map.260), calls=%async_computation.1 | async-start | bytes 1572864 | tf_op jit(solution)/shard_map/all_to_all | solution.py:536
  38.7 21.1 %collective-permute-start.1 = (bf16[1,64,2048]{2,1,0:T(8,128)(2,1)S(1)}, bf16[1,64,2048]{2,1,0:T(8,128)(2,1)S(1)}, u32[]{:S(2)}, u32[]{:S(2)}) collective-permute-start(bf16[1,64,2048]{2,1,0:T(8,128)(2,1)S(1)} %constant_dynamic-slice_fusion.1.refs_0_), channel_id=1, source_target_pairs={{0,8},{8,0},{1,9},{9,1},{2,10},{10,2},{3,11},{11,3},{4,12},{12,4},... | collective-permute-start | bytes 786440 | tf_op jit(solution)/shard_map/ppermute | solution.py:384
  40.8 19.1 %collective-permute-start.2 = (bf16[1,64,2048]{2,1,0:T(8,128)(2,1)S(1)}, bf16[1,64,2048]{2,1,0:T(8,128)(2,1)S(1)}, u32[]{:S(2)}, u32[]{:S(2)}) collective-permute-start(bf16[1,64,2048]{2,1,0:T(8,128)(2,1)S(1)} %get-tuple-element.441.refs_2_), channel_id=1, source_target_pairs={{0,4},{4,0},{1,5},{5,1},{2,6},{6,2},{3,7},{7,3},{8,12},{12,8},{9,1... | collective-permute-start | bytes 786440 | tf_op jit(solution)/shard_map/ppermute | solution.py:384
  42.3 18.2 %collective-permute-start.3 = (bf16[1,64,2048]{2,1,0:T(8,128)(2,1)S(1)}, bf16[1,64,2048]{2,1,0:T(8,128)(2,1)S(1)}, u32[]{:S(2)}, u32[]{:S(2)}) collective-permute-start(bf16[1,64,2048]{2,1,0:T(8,128)(2,1)S(1)} %get-tuple-element.440.refs_4_), channel_id=1, source_target_pairs={{0,2},{2,0},{1,3},{3,1},{4,6},{6,4},{5,7},{7,5},{8,10},{10,8},{9,1... | collective-permute-start | bytes 786440 | tf_op jit(solution)/shard_map/ppermute | solution.py:384
  43.8 19.5 %collective-permute-start.4 = (bf16[64,2048]{1,0:T(8,128)(2,1)}, bf16[64,2048]{1,0:T(8,128)(2,1)}, u32[]{:S(2)}, u32[]{:S(2)}) collective-permute-start(bf16[64,2048]{1,0:T(8,128)(2,1)} %param.26), channel_id=1, source_target_pairs={{0,16},{16,0},{1,17},{17,1},{2,18},{18,2},{3,19},{19,3},{4,20},{20... | collective-permute-start | bytes 786440 | tf_op jit(solution)/shard_map/ppermute | solution.py:384
  63.3 36.1 %collective-permute-start.8 = (bf16[8,64,768]{2,1,0:T(8,128)(2,1)S(1)}, bf16[8,64,768]{2,1,0:T(8,128)(2,1)S(1)}, u32[]{:S(2)}, u32[]{:S(2)}) collective-permute-start(bf16[8,64,768]{2,1,0:T(8,128)(2,1)S(1)} %all-to-all-done.1.refs_0_), channel_id=1, source_target_pairs={{0,16},{16,0},{1,17},{17,1},{2,18},{18,2},{3,19},{19,3},{4,20},{20... | collective-permute-start | bytes 2359304 | tf_op jit(solution)/shard_map/ppermute | solution.py:384
  68.1 23.9 %collective-permute-start.7 = (bf16[2,64,2048]{2,1,0:T(8,128)(2,1)S(1)}, bf16[2,64,2048]{2,1,0:T(8,128)(2,1)S(1)}, u32[]{:S(2)}, u32[]{:S(2)}) collective-permute-start(bf16[2,64,2048]{2,1,0:T(8,128)(2,1)S(1)} %get-tuple-element.214.refs_4_), channel_id=1, source_target_pairs={{0,8},{8,0},{1,9},{9,1},{2,10},{10,2},{3,11},{11,3},{4,12},{12,4},... | collective-permute-start | bytes 1572872 | tf_op jit(solution)/shard_map/ppermute | solution.py:384
  100.3 32.8 %collective-permute-start.10 = (bf16[4,64,2048]{2,1,0:T(8,128)(2,1)}, bf16[4,64,2048]{2,1,0:T(8,128)(2,1)}, u32[]{:S(2)}, u32[]{:S(2)}) collective-permute-start(bf16[4,64,2048]{2,1,0:T(8,128)(2,1)} %get-tuple-element.222.refs_2_), channel_id=1, source_target_pairs={{0,8},{8,0},{1,9},{9,1},{2,10},{10,2},{3,11},{11,3},{4,12},{12,4},... | collective-permute-start | bytes 3145736 | tf_op jit(solution)/shard_map/ppermute | solution.py:384
  100.3 32.8 %collective-permute-start.11 = (bf16[4,64,2048]{2,1,0:T(8,128)(2,1)}, bf16[4,64,2048]{2,1,0:T(8,128)(2,1)}, u32[]{:S(2)}, u32[]{:S(2)}) collective-permute-start(bf16[4,64,2048]{2,1,0:T(8,128)(2,1)} %get-tuple-element.223.refs_4_), channel_id=1, source_target_pairs={{0,4},{4,0},{1,5},{5,1},{2,6},{6,2},{3,7},{7,3},{8,12},{12,8},{9,1... | collective-permute-start | bytes 3145736 | tf_op jit(solution)/shard_map/ppermute | solution.py:384
  101.8 31.4 %collective-permute-start.9 = (bf16[4,64,2048]{2,1,0:T(8,128)(2,1)S(1)}, bf16[4,64,2048]{2,1,0:T(8,128)(2,1)}, u32[]{:S(2)}, u32[]{:S(2)}) collective-permute-start(bf16[4,64,2048]{2,1,0:T(8,128)(2,1)S(1)} %get-tuple-element.221.refs_0_), channel_id=1, source_target_pairs={{0,2},{2,0},{1,3},{3,1},{4,6},{6,4},{5,7},{7,5},{8,10},{10,8},{9,1... | collective-permute-start | bytes 3145736 | tf_op jit(solution)/shard_map/ppermute | solution.py:384
  109.4 27.7 %collective-permute-start.12 = (bf16[96,2048]{1,0:T(8,128)(2,1)S(1)}, bf16[96,2048]{1,0:T(8,128)(2,1)S(1)}, u32[]{:S(2)}, u32[]{:S(2)}) collective-permute-start(bf16[96,2048]{1,0:T(8,128)(2,1)S(1)} %dynamic-slice_bitcast_fusion.5), channel_id=1, source_target_pairs={{0,16},{16,0},{1,17},{17,1},{2,18},{18,2},{3,19},{19,3},{4,20},{20... | collective-permute-start | bytes 1179656 | tf_op jit(solution)/shard_map/ppermute | solution.py:384
  140.5 25.7 %all-to-all-start.2 = ((bf16[8,64,1280]{2,1,0:T(8,128)(2,1)}), bf16[8,64,1280]{2,1,0:T(8,128)(2,1)}, u32[]{:S(2)}, u32[]{:S(2)}) async-start(bf16[8,64,1280]{2,1,0:T(8,128)(2,1)} %shard_map.261), calls=%async_computation.2 | async-start | bytes 2621440 | tf_op jit(solution)/shard_map/all_to_all | solution.py:536
  166.2 81.0 %all-to-all-start.3 = ((bf16[8,2,64,2048]{3,2,1,0:T(8,128)(2,1)}), bf16[8,2,64,2048]{3,2,1,0:T(8,128)(2,1)}, u32[]{:S(2)}, u32[]{:S(2)}) async-start(bf16[8,2,64,2048]{3,2,1,0:T(8,128)(2,1)} %broadcast_in_dim.73), calls=%async_computation.3 | async-start | bytes 8388608 | tf_op jit(solution)/shard_map/all_to_all | solution.py:536
  171.3 71.3 %all-gather.5.cloned.1.call-start = ((), (), s32[]{:S(2)}) async-start(), calls=%async_computation.15 | async-start | bytes 3932160 | tf_op jit(solution)/shard_map/all_gather | solution.py:683
  249.2 16.8 %collective-permute-start.16 = (bf16[8,2,64,2048]{3,2,1,0:T(8,128)(2,1)}, bf16[8,2,64,2048]{3,2,1,0:T(8,128)(2,1)}, u32[]{:S(2)}, u32[]{:S(2)}) collective-permute-start(bf16[8,2,64,2048]{3,2,1,0:T(8,128)(2,1)} %all-to-all-done.3), channel_id=1, source_target_pairs={{0,1},{1,0},{2,3},{3,2},{4,5},{5,4},{6,7},{7,6},{8,9},{9,8},{10,11... | collective-permute-start | bytes 12582920 | tf_op jit(solution)/shard_map/ppermute | solution.py:384
  249.3 24.1 %collective-permute-start.17 = (bf16[2,8,64,1280]{3,2,1,0:T(8,128)(2,1)}, bf16[2,8,64,1280]{3,2,1,0:T(8,128)(2,1)S(1)}, u32[]{:S(2)}, u32[]{:S(2)}) collective-permute-start(bf16[2,8,64,1280]{3,2,1,0:T(8,128)(2,1)} %bitcast.222), channel_id=1, source_target_pairs={{0,1},{1,0},{2,3},{3,2},{4,5},{5,4},{6,7},{7,6},{8,9},{9,8},{10,11... | collective-permute-start | bytes 7864328 | tf_op jit(solution)/shard_map/ppermute | solution.py:384
  252.0 21.5 %all-to-all-start.4 = ((bf16[8,192,256]{2,1,0:T(8,128)(2,1)}), bf16[8,192,256]{2,1,0:T(8,128)(2,1)S(1)}, u32[]{:S(2)}, u32[]{:S(2)}) async-start(bf16[8,192,256]{2,1,0:T(8,128)(2,1)} %maximum_select_fusion), calls=%async_computation.4 | async-start | bytes 1572864 | tf_op jit(solution)/shard_map/all_to_all | solution.py:536
  255.8 47.7 %all-gather.7.cloned.1.call-start = ((), (), s32[]{:S(2)}) async-start(), calls=%async_computation.16 | async-start | bytes 1966080 | tf_op jit(solution)/shard_map/all_gather | solution.py:683
  303.5 14.8 %collective-permute-start.24 = (bf16[2,64,2048]{2,1,0:T(8,128)(2,1)S(1)}, bf16[2,64,2048]{2,1,0:T(8,128)(2,1)S(1)}, u32[]{:S(2)}, u32[]{:S(2)}) collective-permute-start(bf16[2,64,2048]{2,1,0:T(8,128)(2,1)S(1)} %get-tuple-element.279.refs_0_), channel_id=1, source_target_pairs={{0,4},{4,0},{1,5},{5,1},{2,6},{6,2},{3,7},{7,3},{8,12},{12,8},{9,1... | collective-permute-start | bytes 1572872 | tf_op jit(solution)/shard_map/ppermute | solution.py:384
  305.0 14.8 %collective-permute-start.25 = (bf16[2,64,2048]{2,1,0:T(8,128)(2,1)S(1)}, bf16[2,64,2048]{2,1,0:T(8,128)(2,1)S(1)}, u32[]{:S(2)}, u32[]{:S(2)}) collective-permute-start(bf16[2,64,2048]{2,1,0:T(8,128)(2,1)S(1)} %get-tuple-element.280.refs_2_), channel_id=1, source_target_pairs={{0,2},{2,0},{1,3},{3,1},{4,6},{6,4},{5,7},{7,5},{8,10},{10,8},{9,1... | collective-permute-start | bytes 1572872 | tf_op jit(solution)/shard_map/ppermute | solution.py:384
  307.8 20.6 %collective-permute-start.27 = (bf16[2,64,2048]{2,1,0:T(8,128)(2,1)S(1)}, bf16[2,64,2048]{2,1,0:T(8,128)(2,1)S(1)}, u32[]{:S(2)}, u32[]{:S(2)}) collective-permute-start(bf16[2,64,2048]{2,1,0:T(8,128)(2,1)S(1)} %get-tuple-element.288.refs_0_), channel_id=1, source_target_pairs={{0,4},{4,0},{1,5},{5,1},{2,6},{6,2},{3,7},{7,3},{8,12},{12,8},{9,1... | collective-permute-start | bytes 1572872 | tf_op jit(solution)/shard_map/ppermute | solution.py:384
  308.5 14.9 %collective-permute-start.26 = (bf16[2,64,2048]{2,1,0:T(8,128)(2,1)S(1)}, bf16[2,64,2048]{2,1,0:T(8,128)(2,1)S(1)}, u32[]{:S(2)}, u32[]{:S(2)}) collective-permute-start(bf16[2,64,2048]{2,1,0:T(8,128)(2,1)S(1)} %get-tuple-element.281.refs_4_), channel_id=1, source_target_pairs={{0,8},{8,0},{1,9},{9,1},{2,10},{10,2},{3,11},{11,3},{4,12},{12,4},... | collective-permute-start | bytes 1572872 | tf_op jit(solution)/shard_map/ppermute | solution.py:384
  308.5 21.1 %collective-permute-start.28 = (bf16[2,64,2048]{2,1,0:T(8,128)(2,1)S(1)}, bf16[2,64,2048]{2,1,0:T(8,128)(2,1)S(1)}, u32[]{:S(2)}, u32[]{:S(2)}) collective-permute-start(bf16[2,64,2048]{2,1,0:T(8,128)(2,1)S(1)} %get-tuple-element.289.refs_2_), channel_id=1, source_target_pairs={{0,2},{2,0},{1,3},{3,1},{4,6},{6,4},{5,7},{7,5},{8,10},{10,8},{9,1... | collective-permute-start | bytes 1572872 | tf_op jit(solution)/shard_map/ppermute | solution.py:384
  318.3 14.2 %collective-permute-start.29 = (bf16[2,64,2048]{2,1,0:T(8,128)(2,1)S(1)}, bf16[2,64,2048]{2,1,0:T(8,128)(2,1)S(1)}, u32[]{:S(2)}, u32[]{:S(2)}) collective-permute-start(bf16[2,64,2048]{2,1,0:T(8,128)(2,1)S(1)} %get-tuple-element.290.refs_4_), channel_id=1, source_target_pairs={{0,8},{8,0},{1,9},{9,1},{2,10},{10,2},{3,11},{11,3},{4,12},{12,4},... | collective-permute-start | bytes 1572872 | tf_op jit(solution)/shard_map/ppermute | solution.py:384
  319.8 16.8 %collective-permute-start.33 = (bf16[2,160,2048]{2,1,0:T(8,128)(2,1)}, bf16[2,160,2048]{2,1,0:T(8,128)(2,1)S(1)}, u32[]{:S(2)}, u32[]{:S(2)}) collective-permute-start(bf16[2,160,2048]{2,1,0:T(8,128)(2,1)} %bitcast.233), channel_id=1, source_target_pairs={{0,1},{1,0},{2,3},{3,2},{4,5},{5,4},{6,7},{7,6},{8,9},{9,8},{10,11... | collective-permute-start | bytes 3932168 | tf_op jit(solution)/shard_map/ppermute | solution.py:384
  332.5 26.1 %collective-permute-start.30 = (bf16[4,64,2048]{2,1,0:T(8,128)(2,1)S(1)}, bf16[4,64,2048]{2,1,0:T(8,128)(2,1)S(1)}, u32[]{:S(2)}, u32[]{:S(2)}) collective-permute-start(bf16[4,64,2048]{2,1,0:T(8,128)(2,1)S(1)} %get-tuple-element.291.refs_0_), channel_id=1, source_target_pairs={{0,2},{2,0},{1,3},{3,1},{4,6},{6,4},{5,7},{7,5},{8,10},{10,8},{9,1... | collective-permute-start | bytes 3145736 | tf_op jit(solution)/shard_map/ppermute | solution.py:384
  333.1 27.0 %collective-permute-start.31 = (bf16[4,64,2048]{2,1,0:T(8,128)(2,1)S(1)}, bf16[4,64,2048]{2,1,0:T(8,128)(2,1)S(1)}, u32[]{:S(2)}, u32[]{:S(2)}) collective-permute-start(bf16[4,64,2048]{2,1,0:T(8,128)(2,1)S(1)} %get-tuple-element.292.refs_2_), channel_id=1, source_target_pairs={{0,8},{8,0},{1,9},{9,1},{2,10},{10,2},{3,11},{11,3},{4,12},{12,4},... | collective-permute-start | bytes 3145736 | tf_op jit(solution)/shard_map/ppermute | solution.py:384
  333.4 26.7 %collective-permute-start.32 = (bf16[4,64,2048]{2,1,0:T(8,128)(2,1)S(1)}, bf16[4,64,2048]{2,1,0:T(8,128)(2,1)S(1)}, u32[]{:S(2)}, u32[]{:S(2)}) collective-permute-start(bf16[4,64,2048]{2,1,0:T(8,128)(2,1)S(1)} %get-tuple-element.293.refs_4_), channel_id=1, source_target_pairs={{0,4},{4,0},{1,5},{5,1},{2,6},{6,2},{3,7},{7,3},{8,12},{12,8},{9,1... | collective-permute-start | bytes 3145736 | tf_op jit(solution)/shard_map/ppermute | solution.py:384
  335.1 43.1 %collective-permute-start.34 = (bf16[4,64,2048]{2,1,0:T(8,128)(2,1)S(1)}, bf16[4,64,2048]{2,1,0:T(8,128)(2,1)}, u32[]{:S(2)}, u32[]{:S(2)}) collective-permute-start(bf16[4,64,2048]{2,1,0:T(8,128)(2,1)S(1)} %get-tuple-element.305.refs_0_), channel_id=1, source_target_pairs={{0,2},{2,0},{1,3},{3,1},{4,6},{6,4},{5,7},{7,5},{8,10},{10,8},{9,1... | collective-permute-start | bytes 3145736 | tf_op jit(solution)/shard_map/ppermute | solution.py:384
  336.7 42.2 %collective-permute-start.35 = (bf16[4,64,2048]{2,1,0:T(8,128)(2,1)S(1)}, bf16[4,64,2048]{2,1,0:T(8,128)(2,1)S(1)}, u32[]{:S(2)}, u32[]{:S(2)}) collective-permute-start(bf16[4,64,2048]{2,1,0:T(8,128)(2,1)S(1)} %get-tuple-element.306.refs_2_), channel_id=1, source_target_pairs={{0,8},{8,0},{1,9},{9,1},{2,10},{10,2},{3,11},{11,3},{4,12},{12,4},... | collective-permute-start | bytes 3145736 | tf_op jit(solution)/shard_map/ppermute | solution.py:384
  358.6 21.2 %collective-permute-start.36 = (bf16[4,64,2048]{2,1,0:T(8,128)(2,1)S(1)}, bf16[4,64,2048]{2,1,0:T(8,128)(2,1)S(1)}, u32[]{:S(2)}, u32[]{:S(2)}) collective-permute-start(bf16[4,64,2048]{2,1,0:T(8,128)(2,1)S(1)} %get-tuple-element.307.refs_4_), channel_id=1, source_target_pairs={{0,4},{4,0},{1,5},{5,1},{2,6},{6,2},{3,7},{7,3},{8,12},{12,8},{9,1... | collective-permute-start | bytes 3145736 | tf_op jit(solution)/shard_map/ppermute | solution.py:384
  409.7 22.8 %collective-permute-start.39 = (bf16[4,64,2048]{2,1,0:T(8,128)(2,1)}, bf16[4,64,2048]{2,1,0:T(8,128)(2,1)}, u32[]{:S(2)}, u32[]{:S(2)}) collective-permute-start(bf16[4,64,2048]{2,1,0:T(8,128)(2,1)} %bitcast.47), channel_id=1, source_target_pairs={{0,4},{4,0},{1,5},{5,1},{2,6},{6,2},{3,7},{7,3},{8,12},{12,8},{9,1... | collective-permute-start | bytes 3145736 | tf_op jit(solution)/shard_map/ppermute | solution.py:384
  411.4 22.8 %collective-permute-start.38 = (bf16[4,64,2048]{2,1,0:T(8,128)(2,1)}, bf16[4,64,2048]{2,1,0:T(8,128)(2,1)S(1)}, u32[]{:S(2)}, u32[]{:S(2)}) collective-permute-start(bf16[4,64,2048]{2,1,0:T(8,128)(2,1)} %bitcast.264), channel_id=1, source_target_pairs={{0,8},{8,0},{1,9},{9,1},{2,10},{10,2},{3,11},{11,3},{4,12},{12,4},... | collective-permute-start | bytes 3145736 | tf_op jit(solution)/shard_map/ppermute | solution.py:384
  412.3 22.3 %collective-permute-start.37 = (bf16[4,64,2048]{2,1,0:T(8,128)(2,1)}, bf16[4,64,2048]{2,1,0:T(8,128)(2,1)S(1)}, u32[]{:S(2)}, u32[]{:S(2)}) collective-permute-start(bf16[4,64,2048]{2,1,0:T(8,128)(2,1)} %bitcast.263), channel_id=1, source_target_pairs={{0,2},{2,0},{1,3},{3,1},{4,6},{6,4},{5,7},{7,5},{8,10},{10,8},{9,1... | collective-permute-start | bytes 3145736 | tf_op jit(solution)/shard_map/ppermute | solution.py:384
  445.8 14.7 %collective-permute-start.43 = (bf16[2,160,2048]{2,1,0:T(8,128)(2,1)S(1)}, bf16[2,160,2048]{2,1,0:T(8,128)(2,1)S(1)}, u32[]{:S(2)}, u32[]{:S(2)}) collective-permute-start(bf16[2,160,2048]{2,1,0:T(8,128)(2,1)S(1)} %dynamic-slice_bitcast_fusion.3), channel_id=1, source_target_pairs={{0,1},{1,0},{2,3},{3,2},{4,5},{5,4},{6,7},{7,6},{8,9},{9,8},{10,11... | collective-permute-start | bytes 3932168 | tf_op jit(solution)/shard_map/ppermute | solution.py:384
  445.9 14.4 %collective-permute-start.40 = (bf16[2,64,2048]{2,1,0:T(8,128)(2,1)S(1)}, bf16[2,64,2048]{2,1,0:T(8,128)(2,1)S(1)}, u32[]{:S(2)}, u32[]{:S(2)}) collective-permute-start(bf16[2,64,2048]{2,1,0:T(8,128)(2,1)S(1)} %slice.372), channel_id=1, source_target_pairs={{0,4},{4,0},{1,5},{5,1},{2,6},{6,2},{3,7},{7,3},{8,12},{12,8},{9,1... | collective-permute-start | bytes 1572872 | tf_op jit(solution)/shard_map/ppermute | solution.py:384
  483.3 17.0 %all-to-all-start.5 = ((bf16[8,192,256]{2,1,0:T(8,128)(2,1)}), bf16[8,192,256]{2,1,0:T(8,128)(2,1)S(1)}, u32[]{:S(2)}, u32[]{:S(2)}) async-start(bf16[8,192,256]{2,1,0:T(8,128)(2,1)} %bitcast.202), calls=%async_computation.5 | async-start | bytes 1572864 | tf_op jit(solution)/shard_map/all_to_all | solution.py:536
  486.8 128.1 %reduce-scatter.4.cloned.1.call-start = ((), (), s32[]{:S(2)}) async-start(), calls=%async_computation.12 | async-start | bytes 3932160 | tf_op jit(solution)/shard_map/reduce_scatter | solution.py:687
  517.2 129.0 %reduce-scatter.6.cloned.1.call-start = ((), (), s32[]{:S(2)}) async-start(), calls=%async_computation.13 | async-start | bytes 1966080 | tf_op jit(solution)/shard_map/reduce_scatter | solution.py:687
  522.6 36.9 %collective-permute-start.50 = (bf16[4,96,2048]{2,1,0:T(8,128)(2,1)}, bf16[4,96,2048]{2,1,0:T(8,128)(2,1)}, u32[]{:S(2)}, u32[]{:S(2)}) collective-permute-start(bf16[4,96,2048]{2,1,0:T(8,128)(2,1)} %bitcast.62), channel_id=1, source_target_pairs={{0,2},{2,0},{1,3},{3,1},{4,6},{6,4},{5,7},{7,5},{8,10},{10,8},{9,1... | collective-permute-start | bytes 4718600 | tf_op jit(solution)/shard_map/ppermute | solution.py:384
  524.5 36.5 %collective-permute-start.51 = (bf16[4,96,2048]{2,1,0:T(8,128)(2,1)}, bf16[4,96,2048]{2,1,0:T(8,128)(2,1)}, u32[]{:S(2)}, u32[]{:S(2)}) collective-permute-start(bf16[4,96,2048]{2,1,0:T(8,128)(2,1)} %bitcast.63), channel_id=1, source_target_pairs={{0,4},{4,0},{1,5},{5,1},{2,6},{6,2},{3,7},{7,3},{8,12},{12,8},{9,1... | collective-permute-start | bytes 4718600 | tf_op jit(solution)/shard_map/ppermute | solution.py:384
  569.1 45.8 %collective-permute-start.54 = (bf16[4,64,2048]{2,1,0:T(8,128)(2,1)}, bf16[4,64,2048]{2,1,0:T(8,128)(2,1)}, u32[]{:S(2)}, u32[]{:S(2)}) collective-permute-start(bf16[4,64,2048]{2,1,0:T(8,128)(2,1)} %get-tuple-element.420), channel_id=1, source_target_pairs={{0,2},{2,0},{1,3},{3,1},{4,6},{6,4},{5,7},{7,5},{8,10},{10,8},{9,1... | collective-permute-start | bytes 3145736 | tf_op jit(solution)/shard_map/ppermute | solution.py:384
  569.3 45.6 %collective-permute-start.55 = (bf16[4,64,2048]{2,1,0:T(8,128)(2,1)}, bf16[4,64,2048]{2,1,0:T(8,128)(2,1)}, u32[]{:S(2)}, u32[]{:S(2)}) collective-permute-start(bf16[4,64,2048]{2,1,0:T(8,128)(2,1)} %get-tuple-element.419), channel_id=1, source_target_pairs={{0,4},{4,0},{1,5},{5,1},{2,6},{6,2},{3,7},{7,3},{8,12},{12,8},{9,1... | collective-permute-start | bytes 3145736 | tf_op jit(solution)/shard_map/ppermute | solution.py:384
  574.1 40.8 %collective-permute-start.53 = (bf16[2,96,2048]{2,1,0:T(8,128)(2,1)}, bf16[2,96,2048]{2,1,0:T(8,128)(2,1)}, u32[]{:S(2)}, u32[]{:S(2)}) collective-permute-start(bf16[2,96,2048]{2,1,0:T(8,128)(2,1)} %slice.451), channel_id=1, source_target_pairs={{0,2},{2,0},{1,3},{3,1},{4,6},{6,4},{5,7},{7,5},{8,10},{10,8},{9,1... | collective-permute-start | bytes 2359304 | tf_op jit(solution)/shard_map/ppermute | solution.py:384
  577.7 37.2 %collective-permute-start.52 = (bf16[2,96,2048]{2,1,0:T(8,128)(2,1)S(1)}, bf16[2,96,2048]{2,1,0:T(8,128)(2,1)S(1)}, u32[]{:S(2)}, u32[]{:S(2)}) collective-permute-start(bf16[2,96,2048]{2,1,0:T(8,128)(2,1)S(1)} %slice.450), channel_id=1, source_target_pairs={{0,4},{4,0},{1,5},{5,1},{2,6},{6,2},{3,7},{7,3},{8,12},{12,8},{9,1... | collective-permute-start | bytes 2359304 | tf_op jit(solution)/shard_map/ppermute | solution.py:384
  615.0 19.2 %collective-permute-start.56 = (bf16[1536,384]{1,0:T(8,128)(2,1)}, bf16[1536,384]{1,0:T(8,128)(2,1)}, u32[]{:S(2)}, u32[]{:S(2)}) collective-permute-start(bf16[1536,384]{1,0:T(8,128)(2,1)} %get-tuple-element.360), channel_id=1, source_target_pairs={{0,1},{1,0},{2,3},{3,2},{4,5},{5,4},{6,7},{7,6},{8,9},{9,8},{10,11... | collective-permute-start | bytes 3538952 | tf_op jit(solution)/shard_map/ppermute | solution.py:384
  621.2 24.9 %collective-permute-start.58 = (bf16[2,64,2048]{2,1,0:T(8,128)(2,1)}, bf16[2,64,2048]{2,1,0:T(8,128)(2,1)}, u32[]{:S(2)}, u32[]{:S(2)}) collective-permute-start(bf16[2,64,2048]{2,1,0:T(8,128)(2,1)} %slice.459), channel_id=1, source_target_pairs={{0,4},{4,0},{1,5},{5,1},{2,6},{6,2},{3,7},{7,3},{8,12},{12,8},{9,1... | collective-permute-start | bytes 1572872 | tf_op jit(solution)/shard_map/ppermute | solution.py:384
  623.5 22.6 %collective-permute-start.59 = (bf16[2,64,2048]{2,1,0:T(8,128)(2,1)}, bf16[2,64,2048]{2,1,0:T(8,128)(2,1)}, u32[]{:S(2)}, u32[]{:S(2)}) collective-permute-start(bf16[2,64,2048]{2,1,0:T(8,128)(2,1)} %slice.461), channel_id=1, source_target_pairs={{0,2},{2,0},{1,3},{3,1},{4,6},{6,4},{5,7},{7,5},{8,10},{10,8},{9,1... | collective-permute-start | bytes 1572872 | tf_op jit(solution)/shard_map/ppermute | solution.py:384
  625.5 20.7 %collective-permute-start.57 = (bf16[2,96,2048]{2,1,0:T(8,128)(2,1)}, bf16[2,96,2048]{2,1,0:T(8,128)(2,1)}, u32[]{:S(2)}, u32[]{:S(2)}) collective-permute-start(bf16[2,96,2048]{2,1,0:T(8,128)(2,1)} %fusion.43), channel_id=1, source_target_pairs={{0,8},{8,0},{1,9},{9,1},{2,10},{10,2},{3,11},{11,3},{4,12},{12,4},... | collective-permute-start | bytes 2359304 | tf_op jit(solution)/shard_map/ppermute | solution.py:384
  627.0 68.2 %all-to-all-start.6 = ((bf16[8,64,1280]{2,1,0:T(8,128)(2,1)}), bf16[8,64,1280]{2,1,0:T(8,128)(2,1)}, u32[]{:S(2)}, u32[]{:S(2)}) async-start(bf16[8,64,1280]{2,1,0:T(8,128)(2,1)} %bitcast.70), calls=%async_computation.8 | async-start | bytes 2621440 | tf_op jit(solution)/shard_map/all_to_all | solution.py:536
  631.3 121.2 %reduce-scatter.8.cloned.1.call-start = ((), (), s32[]{:S(2)}) async-start(), calls=%async_computation.14 | async-start | bytes 2359296 | tf_op jit(solution)/shard_map/reduce_scatter | solution.py:687
  648.8 46.4 %collective-permute-start.63 = (bf16[96,2048]{1,0:T(8,128)(2,1)}, bf16[96,2048]{1,0:T(8,128)(2,1)}, u32[]{:S(2)}, u32[]{:S(2)}) collective-permute-start(bf16[96,2048]{1,0:T(8,128)(2,1)} %get-tuple-element.422), channel_id=1, source_target_pairs={{0,16},{16,0},{1,17},{17,1},{2,18},{18,2},{3,19},{19,3},{4,20},{20... | collective-permute-start | bytes 1179656 | tf_op jit(solution)/shard_map/ppermute | solution.py:384
  652.8 27.3 %collective-permute-start.62 = (bf16[4,64,2048]{2,1,0:T(8,128)(2,1)}, bf16[4,64,2048]{2,1,0:T(8,128)(2,1)}, u32[]{:S(2)}, u32[]{:S(2)}) collective-permute-start(bf16[4,64,2048]{2,1,0:T(8,128)(2,1)} %bitcast.85), channel_id=1, source_target_pairs={{0,4},{4,0},{1,5},{5,1},{2,6},{6,2},{3,7},{7,3},{8,12},{12,8},{9,1... | collective-permute-start | bytes 3145736 | tf_op jit(solution)/shard_map/ppermute | solution.py:384
  654.6 35.4 %collective-permute-start.61 = (bf16[4,64,2048]{2,1,0:T(8,128)(2,1)}, bf16[4,64,2048]{2,1,0:T(8,128)(2,1)}, u32[]{:S(2)}, u32[]{:S(2)}) collective-permute-start(bf16[4,64,2048]{2,1,0:T(8,128)(2,1)} %bitcast.83), channel_id=1, source_target_pairs={{0,8},{8,0},{1,9},{9,1},{2,10},{10,2},{3,11},{11,3},{4,12},{12,4},... | collective-permute-start | bytes 3145736 | tf_op jit(solution)/shard_map/ppermute | solution.py:384
  656.1 36.5 %collective-permute-start.60 = (bf16[4,64,2048]{2,1,0:T(8,128)(2,1)}, bf16[4,64,2048]{2,1,0:T(8,128)(2,1)}, u32[]{:S(2)}, u32[]{:S(2)}) collective-permute-start(bf16[4,64,2048]{2,1,0:T(8,128)(2,1)} %bitcast.81), channel_id=1, source_target_pairs={{0,2},{2,0},{1,3},{3,1},{4,6},{6,4},{5,7},{7,5},{8,10},{10,8},{9,1... | collective-permute-start | bytes 3145736 | tf_op jit(solution)/shard_map/ppermute | solution.py:384
  698.6 16.3 %collective-permute-start.66 = (bf16[2,64,2048]{2,1,0:T(8,128)(2,1)}, bf16[2,64,2048]{2,1,0:T(8,128)(2,1)}, u32[]{:S(2)}, u32[]{:S(2)}) collective-permute-start(bf16[2,64,2048]{2,1,0:T(8,128)(2,1)} %slice.422), channel_id=1, source_target_pairs={{0,8},{8,0},{1,9},{9,1},{2,10},{10,2},{3,11},{11,3},{4,12},{12,4},... | collective-permute-start | bytes 1572872 | tf_op jit(solution)/shard_map/ppermute | solution.py:384
  700.9 15.3 %collective-permute-start.65 = (bf16[2,64,2048]{2,1,0:T(8,128)(2,1)}, bf16[2,64,2048]{2,1,0:T(8,128)(2,1)}, u32[]{:S(2)}, u32[]{:S(2)}) collective-permute-start(bf16[2,64,2048]{2,1,0:T(8,128)(2,1)} %slice.420), channel_id=1, source_target_pairs={{0,2},{2,0},{1,3},{3,1},{4,6},{6,4},{5,7},{7,5},{8,10},{10,8},{9,1... | collective-permute-start | bytes 1572872 | tf_op jit(solution)/shard_map/ppermute | solution.py:384
  703.2 14.3 %collective-permute-start.64 = (bf16[2,64,2048]{2,1,0:T(8,128)(2,1)}, bf16[2,64,2048]{2,1,0:T(8,128)(2,1)}, u32[]{:S(2)}, u32[]{:S(2)}) collective-permute-start(bf16[2,64,2048]{2,1,0:T(8,128)(2,1)} %slice.418), channel_id=1, source_target_pairs={{0,4},{4,0},{1,5},{5,1},{2,6},{6,2},{3,7},{7,3},{8,12},{12,8},{9,1... | collective-permute-start | bytes 1572872 | tf_op jit(solution)/shard_map/ppermute | solution.py:384
  720.1 32.3 %collective-permute-start.70 = (bf16[2,64,2048]{2,1,0:T(8,128)(2,1)S(1)}, bf16[2,64,2048]{2,1,0:T(8,128)(2,1)S(1)}, u32[]{:S(2)}, u32[]{:S(2)}) collective-permute-start(bf16[2,64,2048]{2,1,0:T(8,128)(2,1)S(1)} %slice_bitcast_fusion.6), channel_id=1, source_target_pairs={{0,8},{8,0},{1,9},{9,1},{2,10},{10,2},{3,11},{11,3},{4,12},{12,4},... | collective-permute-start | bytes 1572872 | tf_op jit(solution)/shard_map/ppermute | solution.py:384
  728.1 23.6 %collective-permute-start.67 = (bf16[1,64,2048]{2,1,0:T(8,128)(2,1)S(1)}, bf16[1,64,2048]{2,1,0:T(8,128)(2,1)S(1)}, u32[]{:S(2)}, u32[]{:S(2)}) collective-permute-start(bf16[1,64,2048]{2,1,0:T(8,128)(2,1)S(1)} %slice.424), channel_id=1, source_target_pairs={{0,8},{8,0},{1,9},{9,1},{2,10},{10,2},{3,11},{11,3},{4,12},{12,4},... | collective-permute-start | bytes 786440 | tf_op jit(solution)/shard_map/ppermute | solution.py:384
  754.1 29.1 %all-to-all-start.7 = ((bf16[8,64,768]{2,1,0:T(8,128)(2,1)}), bf16[8,64,768]{2,1,0:T(8,128)(2,1)S(1)}, u32[]{:S(2)}, u32[]{:S(2)}) async-start(bf16[8,64,768]{2,1,0:T(8,128)(2,1)} %bitcast.265), calls=%async_computation.10 | async-start | bytes 1572864 | tf_op jit(solution)/shard_map/all_to_all | solution.py:536
  760.9 21.3 %collective-permute-start.72 = (bf16[96,2048]{1,0:T(8,128)(2,1)S(1)}, bf16[96,2048]{1,0:T(8,128)(2,1)S(1)}, u32[]{:S(2)}, u32[]{:S(2)}) collective-permute-start(bf16[96,2048]{1,0:T(8,128)(2,1)S(1)} %get-tuple-element.430), channel_id=1, source_target_pairs={{0,16},{16,0},{1,17},{17,1},{2,18},{18,2},{3,19},{19,3},{4,20},{20... | collective-permute-start | bytes 1179656 | tf_op jit(solution)/shard_map/ppermute | solution.py:384
  (139 other events, 1212.6 us)
Sparse Core Ops, SparseCore 0:
  173.7 68.8 all-gather.4
  266.1 37.2 all-gather.6
  517.3 66.7 reduce-scatter.3
  586.9 37.1 reduce-scatter.5
  705.9 41.1 reduce-scatter.7

commit v4 on v3

--- a/solution.py
+++ b/solution.py
@@ -1097,7 +1097,7 @@
     grad_mixed, fed, grad_down = fence(grad_mixed, fed, grad_down)
     grad_down = scatter_halves(grad_down)
     grad_mixed = exchange(grad_mixed)
-    grad_expand = matmul(fed, grad_gate_up, TN).astype(LOW).reshape(halves, 8, 2, shard_rows, -1)
+    grad_expand = turned_matmul(fed, grad_gate_up).reshape(halves, 8, 2, shard_rows, -1)
     if one_block:
         mixed = by_light_distance(mixed_chunks, at)
     grad_mixed, final, mixed, grad_expand = fence(grad_mixed, final, mixed, grad_expand)

time: 810 us -> 813 us (level)
  matrix products: 93.1 us -> 79.4 us
    dot_general x11 -> x10, matrix products: 93.1 us -> 79.4 us  [matmul(): return lax.dot_general(left, right, dims, preferred_element_type=F32)]
    pallas_call x1 -> x2, Pallas kernels: 6.88 us -> 19.9 us  [turned_matmul(): pl.pallas_call(turned_kernel, out_shape=jax.ShapeDtypeStruct((left.shape[...]
    unnamed x237 -> x235, local copies, waits for them, and re-layouts: 47 us -> 47.8 us
  transfers between devices with their start and end apart: 88 -> 88, of which waited for: 39 -> 40; matrix products, arithmetic and copies ran while one was open for 21% -> 20% of each run, Pallas kernels for 19% -> 20%
where the time goes in v4:
time: 813 us; the launch traced here: 804 us
  waiting for transfers between devices  251 us (31%)
  Pallas kernels  163 us (20%)
  starting transfers between devices  117 us (14%)
  other arithmetic  89.1 us (11%)
  local copies, waits for them, and re-layouts  88.7 us (11%)
  matrix products  79.4 us (10%)
  between operations  16 us (2%)
    ppermute x74, waiting for transfers between devices, swap(): return lax.ppermute(value, axis, SWAP)  205 us
    ppermute x74, starting transfers between devices, swap(): return lax.ppermute(value, axis, SWAP)  80.6 us
    dot_general x10, matrix products, matmul(): return lax.dot_general(left, right, dims, preferred_element_type=F32)  79.4 us
    pallas_call x2, Pallas kernels, attend_backward(): pl.pallas_call(lambda *refs: backward_kernel(local, halo, n, *refs), out_...  62.1 us
    pallas_call x2, Pallas kernels, attend_forward(): pl.pallas_call(lambda *refs: forward_kernel(local, halo, n, *refs), out_s...  49.1 us
    unnamed x235, local copies, waits for them, and re-layouts  47.8 us
    all_to_all x7, starting transfers between devices, exchange(): return lax.all_to_all(chunks, CUBE, 0, 0)  29.8 us
    all_gather x2, waiting for transfers between devices, gather_halves(): return lax.all_gather(shard, ('b', 'h'), axis=0)  27.8 us
  transfers between devices with their start and end apart: 88, of which 40 were waited for; matrix products, arithmetic and copies ran while one was open for 20% of the time, Pallas kernels for 20%

profile of v4, /device:TPU:0, one launch (start us, length us, event | category | flops | bytes accessed | tf_op | source)
XLA Modules:
  0.0 804.3 jit_solution(641820217466111708)
XLA Ops:
  9.3 4.0 collective-permute-start
  19.2 3.8 all-to-all-start
  26.6 7.5 all-to-all-done
  34.2 3.6 all-to-all-start.1
  47.6 12.2 %collective-permute-done.1.refs_1_ = bf16[1,64,2048]{2,1,0:T(8,128)(2,1)S(1)} collective-permute-done((bf16[1,64,2048]{2,1,0:T(8,128)(2,1)S(1)}, bf16[1,64,2048]{2,1,0:T(8,128)(2,1)S(1)}, u32[]{:S(2)}, u32[]{:S(2)}) %collective-permute-start.1) | collective-permute-done | bytes 262176 | tf_op jit(solution)/shard_map/ppermute | solution.py:384
  71.4 6.0 collective-permute-done.5.refs_1_
  78.4 13.7 %collective-permute-done.7.refs_5_ = bf16[2,64,2048]{2,1,0:T(8,128)(2,1)S(1)} collective-permute-done((bf16[2,64,2048]{2,1,0:T(8,128)(2,1)S(1)}, bf16[2,64,2048]{2,1,0:T(8,128)(2,1)S(1)}, u32[]{:S(2)}, u32[]{:S(2)}) %collective-permute-start.7) | collective-permute-done | bytes 524320 | tf_op jit(solution)/shard_map/ppermute | solution.py:384
  95.8 3.6 collective-permute-done.8.refs_1_
  103.3 2.9 shard_map.265
  109.4 3.0 collective-permute-start.12
  112.6 20.6 %collective-permute-done.10.refs_3_ = bf16[4,64,2048]{2,1,0:T(8,128)(2,1)} collective-permute-done((bf16[4,64,2048]{2,1,0:T(8,128)(2,1)}, bf16[4,64,2048]{2,1,0:T(8,128)(2,1)}, u32[]{:S(2)}, u32[]{:S(2)}) %collective-permute-start.10) | collective-permute-done | bytes 1048608 | tf_op jit(solution)/shard_map/ppermute | solution.py:384
  140.5 4.5 all-to-all-start.2
  156.1 7.2 convolution_convert_fusion.4
  166.0 5.1 all-to-all-start.3
  177.0 23.7 %shard_map.269 = (f32[64,3072]{1,0:T(8,128)}, f32[1,3072]{1,0:T(1,128)}) custom-call(s32[96]{0:T(128)} %multiply_add_fusion.2.refs_0_, s32[32]{0:T(128)} %add_multiply_fusion.1.refs_1_, s32[2,12]{1,0:T(2,128)} %copy-done.40, bf16[1536,384]{1,0:T(8,128)(2,1)} %get-tuple-element.249.refs_3_, bf16[1536,384]{1,0:T(8,128)(2,1)} %copy-done.45, ...), custom_call_target="tpu_custom_call" | custom-call | flops 3072 | bytes 65536 | tf_op jit(solution)/shard_map/pallas_call | solution.py:306
  200.6 25.4 %shard_map.270 = (bf16[1536,128]{1,0:T(8,128)(2,1)}, bf16[1536,128]{1,0:T(8,128)(2,1)}, f32[64,3072]{1,0:T(8,128)}, f32[1,3072]{1,0:T(1,128)}) custom-call(s32[96]{0:T(128)} %multiply_add_fusion.2.refs_0_, s32[32]{0:T(128)} %add_multiply_fusion.1.refs_1_, s32[2,12]{1,0:T(2,128)} %copy-done.40, bf16[1536,384]{1,0:T(8,128)(2,1)} %get-tuple-element.249.refs_3_, ...), custom_call_target="tpu_custom_call" | custom-call | flops 3072 | bytes 65536 | tf_op jit(solution)/shard_map/pallas_call | solution.py:306
  226.1 16.3 %all-gather.5.cloned.1.call-done = bf16[16,64,1280]{2,1,0:T(8,128)(2,1)} async-done(((bf16[8,64,1280]{2,1,0:T(8,128)(2,1)}), bf16[16,64,1280]{2,1,0:T(8,128)(2,1)}) %all-gather.5.cloned.1.call-update) | async-done | bytes 2621456 | tf_op jit(solution)/shard_map/all_gather | solution.py:683
  242.4 4.6 all-to-all-done.3
  251.7 3.8 all-to-all-start.4
  265.8 4.1 shard_map.271
  269.9 3.3 copy-done.10
  273.3 5.5 multiply_reduce_fusion
  285.9 5.6 collective-permute-done.21.refs_1_
  291.7 11.5 %all-gather.7.cloned.1.call-done = bf16[320,2048]{1,0:T(8,128)(2,1)} async-done(((bf16[160,2048]{1,0:T(8,128)(2,1)}), bf16[320,2048]{1,0:T(8,128)(2,1)}) %all-gather.7.cloned.1.call-update) | async-done | bytes 1310736 | tf_op jit(solution)/shard_map/all_gather | solution.py:683
  308.8 9.3 %collective-permute-done.24.refs_1_ = bf16[2,64,2048]{2,1,0:T(8,128)(2,1)S(1)} collective-permute-done((bf16[2,64,2048]{2,1,0:T(8,128)(2,1)S(1)}, bf16[2,64,2048]{2,1,0:T(8,128)(2,1)S(1)}, u32[]{:S(2)}, u32[]{:S(2)}) %collective-permute-start.24) | collective-permute-done | bytes 524320 | tf_op jit(solution)/shard_map/ppermute | solution.py:384
  319.6 3.5 collective-permute-done.26.refs_5_
  323.4 4.8 collective-permute-done.27.refs_1_
  329.3 2.9 collective-permute-done.29.refs_5_
  339.6 18.8 %collective-permute-done.30.refs_1_ = bf16[4,64,2048]{2,1,0:T(8,128)(2,1)S(1)} collective-permute-done((bf16[4,64,2048]{2,1,0:T(8,128)(2,1)S(1)}, bf16[4,64,2048]{2,1,0:T(8,128)(2,1)S(1)}, u32[]{:S(2)}, u32[]{:S(2)}) %collective-permute-start.30) | collective-permute-done | bytes 1048608 | tf_op jit(solution)/shard_map/ppermute | solution.py:384
  362.4 10.3 %fusion.67 = f32[1536,1280]{1,0:T(8,128)} fusion(bf16[1536,2048]{1,0:T(8,128)(2,1)S(1)} %shard_map.278.left, bf16[2048,1280]{1,0:T(8,128)(2,1)S(1)} %bitcast.217), kind=kOutput, calls=%fused_computation.190 | convolution fusion | flops 8053063680 | bytes 19398656 | tf_op jit(solution)/shard_map/dot_general | solution.py:397
  372.8 4.7 multiply_convert_fusion.1.src
  382.6 13.6 %fusion.8 = (bf16[1536,640]{1,0:T(8,128)(2,1)S(1)}, bf16[1536,640]{1,0:T(8,128)(2,1)}) fusion(f32[1536,1280]{1,0:T(8,128)} %fusion.67, bf16[1536,2048]{1,0:T(8,128)(2,1)S(1)} %shard_map.281, bf16[640,2048]{1,0:T(8,128)(2,1)S(1)} %bitcast.221), kind=kOutput, calls=%fused_computation.21 | convolution fusion | flops 4054056960 | bytes 20709376 | tf_op jit(solution)/shard_map/dot_general | solution.py:397
  396.2 10.4 %convolution_convert_fusion.2 = bf16[1536,2048]{1,0:T(8,128)(2,1)S(1)} fusion(bf16[2048,1280]{1,0:T(8,128)(2,1)S(1)} %bitcast.218, bf16[1536,640]{1,0:T(8,128)(2,1)} %get-tuple-element.400, bf16[1536,640]{1,0:T(8,128)(2,1)S(1)} %get-tuple-element.399), kind=kOutput, calls=%fused_computation.9 | convolution fusion | flops 8064073728 | bytes 15466496 | tf_op jit(solution)/shard_map/dot_general | solution.py:397
  412.8 7.1 convolution_convert_fusion.5
  419.9 12.5 %collective-permute-done.39 = bf16[4,64,2048]{2,1,0:T(8,128)(2,1)} collective-permute-done((bf16[4,64,2048]{2,1,0:T(8,128)(2,1)}, bf16[4,64,2048]{2,1,0:T(8,128)(2,1)}, u32[]{:S(2)}, u32[]{:S(2)}) %collective-permute-start.39) | collective-permute-done | bytes 1048608 | tf_op jit(solution)/shard_map/ppermute | solution.py:384
  437.3 7.1 convolution_convert_fusion.1
  447.0 7.8 collective-permute-done.41
  455.0 4.8 collective-permute-done.40
  474.9 6.8 convolution_convert_fusion.6
  482.8 4.2 all-to-all-start.5
  489.1 13.0 %shard_map.284 = bf16[2048,1280]{1,0:T(8,128)(2,1)S(1)} custom-call(bf16[1536,2048]{1,0:T(8,128)(2,1)} %copy-done.4, bf16[1536,1280]{1,0:T(8,128)(2,1)S(1)} %pad_maximum_fusion.right), custom_call_target="tpu_custom_call" | custom-call | bytes 65536 | tf_op jit(solution)/shard_map/pallas_call | solution.py:588
  507.6 4.8 copy-done.6
  515.2 3.9 collective-permute-done.47.refs_9_
  521.5 5.4 fusion.58
  530.3 30.1 %shard_map.285 = (bf16[3072,128]{1,0:T(8,128)(2,1)}, bf16[3072,128]{1,0:T(8,128)(2,1)}, bf16[3072,128]{1,0:T(8,128)(2,1)}, f32[1,2560]{1,0:T(1,128)}) custom-call(s32[96]{0:T(128)} %multiply_add_fusion.2.refs_0_, s32[32]{0:T(128)} %add_multiply_fusion.1.refs_1_, s32[2,12]{1,0:T(2,128)} %copy-done.40, bf16[1536,384]{1,0:T(8,128)(2,1)} %get-tuple-element.249.refs_3_, ...), custom_call_target="tpu_custom_call" | custom-call | flops 3072 | bytes 65536 | tf_op jit(solution)/shard_map/pallas_call | solution.py:344
  560.4 3.2 collective-permute-done.50
  565.1 5.5 fusion.3
  583.0 32.0 %shard_map.286 = (bf16[1536,384]{1,0:T(8,128)(2,1)}, bf16[1536,384]{1,0:T(8,128)(2,1)}, f32[1,2560]{1,0:T(1,128)}) custom-call(s32[96]{0:T(128)} %multiply_add_fusion.2.refs_0_, s32[32]{0:T(128)} %add_multiply_fusion.1.refs_1_, s32[2,12]{1,0:T(2,128)} %copy-done.40, bf16[1536,384]{1,0:T(8,128)(2,1)} %get-tuple-element.249.refs_3_, ...), custom_call_target="tpu_custom_call" | custom-call | flops 3072 | bytes 65536 | tf_op jit(solution)/shard_map/pallas_call | solution.py:344
  616.1 3.2 fusion.18
  627.9 4.3 all-to-all-start.6
  635.0 9.0 %convolution_convert_fusion.left = bf16[1536,2048]{1,0:T(8,128)(2,1)} fusion(bf16[2048,768]{1,0:T(8,128)(2,1)S(1)} %bitcast.220, bf16[1536,384]{1,0:T(8,128)(2,1)} %collective-permute-done.56, bf16[1536,384]{1,0:T(8,128)(2,1)} %get-tuple-element.359), kind=kOutput, calls=%fused_computation.7 | convolution fusion | flops 4839702528 | bytes 11796480 | tf_op jit(solution)/shard_map/dot_general | solution.py:397
  644.0 3.0 pad_maximum_fusion.1.right
  651.1 3.2 fusion.57
  663.1 6.9 shard_map.288
  672.8 3.8 shard_map.287
  684.1 6.9 collective-permute-done.61
  706.7 8.5 %collective-permute-done.66 = bf16[2,64,2048]{2,1,0:T(8,128)(2,1)} collective-permute-done((bf16[2,64,2048]{2,1,0:T(8,128)(2,1)}, bf16[2,64,2048]{2,1,0:T(8,128)(2,1)}, u32[]{:S(2)}, u32[]{:S(2)}) %collective-permute-start.66) | collective-permute-done | bytes 524320 | tf_op jit(solution)/shard_map/ppermute | solution.py:384
  722.9 3.1 shard_map.290
  729.3 5.4 collective-permute-done.68
  735.5 17.4 %collective-permute-done.67 = bf16[1,64,2048]{2,1,0:T(8,128)(2,1)S(1)} collective-permute-done((bf16[1,64,2048]{2,1,0:T(8,128)(2,1)S(1)}, bf16[1,64,2048]{2,1,0:T(8,128)(2,1)S(1)}, u32[]{:S(2)}, u32[]{:S(2)}) %collective-permute-start.67) | collective-permute-done | bytes 262176 | tf_op jit(solution)/shard_map/ppermute | solution.py:384
  755.4 4.4 all-to-all-start.7
  769.8 14.4 %collective-permute-done.72 = bf16[96,2048]{1,0:T(8,128)(2,1)S(1)} collective-permute-done((bf16[96,2048]{1,0:T(8,128)(2,1)S(1)}, bf16[96,2048]{1,0:T(8,128)(2,1)S(1)}, u32[]{:S(2)}, u32[]{:S(2)}) %collective-permute-start.72) | collective-permute-done | bytes 393248 | tf_op jit(solution)/shard_map/ppermute | solution.py:384
  786.0 2.9 all-to-all-start.8
  790.4 5.7 all-to-all-done.8
  (537 shorter events, 258.0 us)
Async XLA Ops:
  9.3 24.9 %collective-permute-start = (bf16[96,2048]{1,0:T(8,128)(2,1)}, bf16[96,2048]{1,0:T(8,128)(2,1)S(1)}, u32[]{:S(2)}, u32[]{:S(2)}) collective-permute-start(bf16[96,2048]{1,0:T(8,128)(2,1)} %get-tuple-element.436), channel_id=1, source_target_pairs={{0,16},{16,0},{1,17},{17,1},{2,18},{18,2},{3,19},{19,3},{4,20},{20... | collective-permute-start | bytes 1179656 | tf_op jit(solution)/shard_map/ppermute | solution.py:384
  19.2 14.8 %all-to-all-start = ((bf16[32,2,320]{2,1,0:T(2,128)(2,1)}), bf16[32,2,320]{2,1,0:T(2,128)(2,1)S(1)}, u32[]{:S(2)}, u32[]{:S(2)}) async-start(bf16[32,2,320]{2,1,0:T(2,128)(2,1)} %reshape.307), calls=%async_computation | async-start | bytes 98304 | tf_op jit(solution)/shard_map/all_to_all | solution.py:563
  34.2 29.2 %all-to-all-start.1 = ((bf16[8,64,768]{2,1,0:T(8,128)(2,1)}), bf16[8,64,768]{2,1,0:T(8,128)(2,1)S(1)}, u32[]{:S(2)}, u32[]{:S(2)}) async-start(bf16[8,64,768]{2,1,0:T(8,128)(2,1)} %shard_map.260), calls=%async_computation.1 | async-start | bytes 1572864 | tf_op jit(solution)/shard_map/all_to_all | solution.py:536
  38.7 21.1 %collective-permute-start.1 = (bf16[1,64,2048]{2,1,0:T(8,128)(2,1)S(1)}, bf16[1,64,2048]{2,1,0:T(8,128)(2,1)S(1)}, u32[]{:S(2)}, u32[]{:S(2)}) collective-permute-start(bf16[1,64,2048]{2,1,0:T(8,128)(2,1)S(1)} %constant_dynamic-slice_fusion.1.refs_0_), channel_id=1, source_target_pairs={{0,8},{8,0},{1,9},{9,1},{2,10},{10,2},{3,11},{11,3},{4,12},{12,4},... | collective-permute-start | bytes 786440 | tf_op jit(solution)/shard_map/ppermute | solution.py:384
  40.8 19.1 %collective-permute-start.2 = (bf16[1,64,2048]{2,1,0:T(8,128)(2,1)S(1)}, bf16[1,64,2048]{2,1,0:T(8,128)(2,1)S(1)}, u32[]{:S(2)}, u32[]{:S(2)}) collective-permute-start(bf16[1,64,2048]{2,1,0:T(8,128)(2,1)S(1)} %get-tuple-element.441.refs_2_), channel_id=1, source_target_pairs={{0,4},{4,0},{1,5},{5,1},{2,6},{6,2},{3,7},{7,3},{8,12},{12,8},{9,1... | collective-permute-start | bytes 786440 | tf_op jit(solution)/shard_map/ppermute | solution.py:384
  42.3 18.2 %collective-permute-start.3 = (bf16[1,64,2048]{2,1,0:T(8,128)(2,1)S(1)}, bf16[1,64,2048]{2,1,0:T(8,128)(2,1)S(1)}, u32[]{:S(2)}, u32[]{:S(2)}) collective-permute-start(bf16[1,64,2048]{2,1,0:T(8,128)(2,1)S(1)} %get-tuple-element.440.refs_4_), channel_id=1, source_target_pairs={{0,2},{2,0},{1,3},{3,1},{4,6},{6,4},{5,7},{7,5},{8,10},{10,8},{9,1... | collective-permute-start | bytes 786440 | tf_op jit(solution)/shard_map/ppermute | solution.py:384
  43.8 19.5 %collective-permute-start.4 = (bf16[64,2048]{1,0:T(8,128)(2,1)}, bf16[64,2048]{1,0:T(8,128)(2,1)}, u32[]{:S(2)}, u32[]{:S(2)}) collective-permute-start(bf16[64,2048]{1,0:T(8,128)(2,1)} %param.26), channel_id=1, source_target_pairs={{0,16},{16,0},{1,17},{17,1},{2,18},{18,2},{3,19},{19,3},{4,20},{20... | collective-permute-start | bytes 786440 | tf_op jit(solution)/shard_map/ppermute | solution.py:384
  63.3 36.1 %collective-permute-start.8 = (bf16[8,64,768]{2,1,0:T(8,128)(2,1)S(1)}, bf16[8,64,768]{2,1,0:T(8,128)(2,1)S(1)}, u32[]{:S(2)}, u32[]{:S(2)}) collective-permute-start(bf16[8,64,768]{2,1,0:T(8,128)(2,1)S(1)} %all-to-all-done.1.refs_0_), channel_id=1, source_target_pairs={{0,16},{16,0},{1,17},{17,1},{2,18},{18,2},{3,19},{19,3},{4,20},{20... | collective-permute-start | bytes 2359304 | tf_op jit(solution)/shard_map/ppermute | solution.py:384
  68.1 23.9 %collective-permute-start.7 = (bf16[2,64,2048]{2,1,0:T(8,128)(2,1)S(1)}, bf16[2,64,2048]{2,1,0:T(8,128)(2,1)S(1)}, u32[]{:S(2)}, u32[]{:S(2)}) collective-permute-start(bf16[2,64,2048]{2,1,0:T(8,128)(2,1)S(1)} %get-tuple-element.214.refs_4_), channel_id=1, source_target_pairs={{0,8},{8,0},{1,9},{9,1},{2,10},{10,2},{3,11},{11,3},{4,12},{12,4},... | collective-permute-start | bytes 1572872 | tf_op jit(solution)/shard_map/ppermute | solution.py:384
  100.3 32.8 %collective-permute-start.10 = (bf16[4,64,2048]{2,1,0:T(8,128)(2,1)}, bf16[4,64,2048]{2,1,0:T(8,128)(2,1)}, u32[]{:S(2)}, u32[]{:S(2)}) collective-permute-start(bf16[4,64,2048]{2,1,0:T(8,128)(2,1)} %get-tuple-element.222.refs_2_), channel_id=1, source_target_pairs={{0,8},{8,0},{1,9},{9,1},{2,10},{10,2},{3,11},{11,3},{4,12},{12,4},... | collective-permute-start | bytes 3145736 | tf_op jit(solution)/shard_map/ppermute | solution.py:384
  100.3 32.8 %collective-permute-start.11 = (bf16[4,64,2048]{2,1,0:T(8,128)(2,1)}, bf16[4,64,2048]{2,1,0:T(8,128)(2,1)}, u32[]{:S(2)}, u32[]{:S(2)}) collective-permute-start(bf16[4,64,2048]{2,1,0:T(8,128)(2,1)} %get-tuple-element.223.refs_4_), channel_id=1, source_target_pairs={{0,4},{4,0},{1,5},{5,1},{2,6},{6,2},{3,7},{7,3},{8,12},{12,8},{9,1... | collective-permute-start | bytes 3145736 | tf_op jit(solution)/shard_map/ppermute | solution.py:384
  101.8 31.4 %collective-permute-start.9 = (bf16[4,64,2048]{2,1,0:T(8,128)(2,1)S(1)}, bf16[4,64,2048]{2,1,0:T(8,128)(2,1)}, u32[]{:S(2)}, u32[]{:S(2)}) collective-permute-start(bf16[4,64,2048]{2,1,0:T(8,128)(2,1)S(1)} %get-tuple-element.221.refs_0_), channel_id=1, source_target_pairs={{0,2},{2,0},{1,3},{3,1},{4,6},{6,4},{5,7},{7,5},{8,10},{10,8},{9,1... | collective-permute-start | bytes 3145736 | tf_op jit(solution)/shard_map/ppermute | solution.py:384
  109.4 27.7 %collective-permute-start.12 = (bf16[96,2048]{1,0:T(8,128)(2,1)S(1)}, bf16[96,2048]{1,0:T(8,128)(2,1)S(1)}, u32[]{:S(2)}, u32[]{:S(2)}) collective-permute-start(bf16[96,2048]{1,0:T(8,128)(2,1)S(1)} %dynamic-slice_bitcast_fusion.5), channel_id=1, source_target_pairs={{0,16},{16,0},{1,17},{17,1},{2,18},{18,2},{3,19},{19,3},{4,20},{20... | collective-permute-start | bytes 1179656 | tf_op jit(solution)/shard_map/ppermute | solution.py:384
  140.5 25.5 %all-to-all-start.2 = ((bf16[8,64,1280]{2,1,0:T(8,128)(2,1)}), bf16[8,64,1280]{2,1,0:T(8,128)(2,1)}, u32[]{:S(2)}, u32[]{:S(2)}) async-start(bf16[8,64,1280]{2,1,0:T(8,128)(2,1)} %shard_map.261), calls=%async_computation.2 | async-start | bytes 2621440 | tf_op jit(solution)/shard_map/all_to_all | solution.py:536
  166.0 81.0 %all-to-all-start.3 = ((bf16[8,2,64,2048]{3,2,1,0:T(8,128)(2,1)}), bf16[8,2,64,2048]{3,2,1,0:T(8,128)(2,1)}, u32[]{:S(2)}, u32[]{:S(2)}) async-start(bf16[8,2,64,2048]{3,2,1,0:T(8,128)(2,1)} %broadcast_in_dim.73), calls=%async_computation.3 | async-start | bytes 8388608 | tf_op jit(solution)/shard_map/all_to_all | solution.py:536
  171.0 71.3 %all-gather.5.cloned.1.call-start = ((), (), s32[]{:S(2)}) async-start(), calls=%async_computation.15 | async-start | bytes 3932160 | tf_op jit(solution)/shard_map/all_gather | solution.py:683
  248.9 16.8 %collective-permute-start.16 = (bf16[8,2,64,2048]{3,2,1,0:T(8,128)(2,1)}, bf16[8,2,64,2048]{3,2,1,0:T(8,128)(2,1)}, u32[]{:S(2)}, u32[]{:S(2)}) collective-permute-start(bf16[8,2,64,2048]{3,2,1,0:T(8,128)(2,1)} %all-to-all-done.3), channel_id=1, source_target_pairs={{0,1},{1,0},{2,3},{3,2},{4,5},{5,4},{6,7},{7,6},{8,9},{9,8},{10,11... | collective-permute-start | bytes 12582920 | tf_op jit(solution)/shard_map/ppermute | solution.py:384
  249.1 24.1 %collective-permute-start.17 = (bf16[2,8,64,1280]{3,2,1,0:T(8,128)(2,1)}, bf16[2,8,64,1280]{3,2,1,0:T(8,128)(2,1)S(1)}, u32[]{:S(2)}, u32[]{:S(2)}) collective-permute-start(bf16[2,8,64,1280]{3,2,1,0:T(8,128)(2,1)} %bitcast.223), channel_id=1, source_target_pairs={{0,1},{1,0},{2,3},{3,2},{4,5},{5,4},{6,7},{7,6},{8,9},{9,8},{10,11... | collective-permute-start | bytes 7864328 | tf_op jit(solution)/shard_map/ppermute | solution.py:384
  251.7 21.5 %all-to-all-start.4 = ((bf16[8,192,256]{2,1,0:T(8,128)(2,1)}), bf16[8,192,256]{2,1,0:T(8,128)(2,1)S(1)}, u32[]{:S(2)}, u32[]{:S(2)}) async-start(bf16[8,192,256]{2,1,0:T(8,128)(2,1)} %maximum_select_fusion), calls=%async_computation.4 | async-start | bytes 1572864 | tf_op jit(solution)/shard_map/all_to_all | solution.py:536
  255.5 47.7 %all-gather.7.cloned.1.call-start = ((), (), s32[]{:S(2)}) async-start(), calls=%async_computation.16 | async-start | bytes 1966080 | tf_op jit(solution)/shard_map/all_gather | solution.py:683
  259.2 14.0 %collective-permute-start.19 = (bf16[1,64,2048]{2,1,0:T(8,128)(2,1)}, bf16[1,64,2048]{2,1,0:T(8,128)(2,1)}, u32[]{:S(2)}, u32[]{:S(2)}) collective-permute-start(bf16[1,64,2048]{2,1,0:T(8,128)(2,1)} %get-tuple-element.439.refs_2_), channel_id=1, source_target_pairs={{0,4},{4,0},{1,5},{5,1},{2,6},{6,2},{3,7},{7,3},{8,12},{12,8},{9,1... | collective-permute-start | bytes 786440 | tf_op jit(solution)/shard_map/ppermute | solution.py:384
  303.2 14.8 %collective-permute-start.24 = (bf16[2,64,2048]{2,1,0:T(8,128)(2,1)S(1)}, bf16[2,64,2048]{2,1,0:T(8,128)(2,1)S(1)}, u32[]{:S(2)}, u32[]{:S(2)}) collective-permute-start(bf16[2,64,2048]{2,1,0:T(8,128)(2,1)S(1)} %get-tuple-element.279.refs_0_), channel_id=1, source_target_pairs={{0,4},{4,0},{1,5},{5,1},{2,6},{6,2},{3,7},{7,3},{8,12},{12,8},{9,1... | collective-permute-start | bytes 1572872 | tf_op jit(solution)/shard_map/ppermute | solution.py:384
  304.7 14.8 %collective-permute-start.25 = (bf16[2,64,2048]{2,1,0:T(8,128)(2,1)S(1)}, bf16[2,64,2048]{2,1,0:T(8,128)(2,1)S(1)}, u32[]{:S(2)}, u32[]{:S(2)}) collective-permute-start(bf16[2,64,2048]{2,1,0:T(8,128)(2,1)S(1)} %get-tuple-element.280.refs_2_), channel_id=1, source_target_pairs={{0,2},{2,0},{1,3},{3,1},{4,6},{6,4},{5,7},{7,5},{8,10},{10,8},{9,1... | collective-permute-start | bytes 1572872 | tf_op jit(solution)/shard_map/ppermute | solution.py:384
  307.6 20.6 %collective-permute-start.27 = (bf16[2,64,2048]{2,1,0:T(8,128)(2,1)S(1)}, bf16[2,64,2048]{2,1,0:T(8,128)(2,1)S(1)}, u32[]{:S(2)}, u32[]{:S(2)}) collective-permute-start(bf16[2,64,2048]{2,1,0:T(8,128)(2,1)S(1)} %get-tuple-element.288.refs_0_), channel_id=1, source_target_pairs={{0,4},{4,0},{1,5},{5,1},{2,6},{6,2},{3,7},{7,3},{8,12},{12,8},{9,1... | collective-permute-start | bytes 1572872 | tf_op jit(solution)/shard_map/ppermute | solution.py:384
  308.2 14.9 %collective-permute-start.26 = (bf16[2,64,2048]{2,1,0:T(8,128)(2,1)S(1)}, bf16[2,64,2048]{2,1,0:T(8,128)(2,1)S(1)}, u32[]{:S(2)}, u32[]{:S(2)}) collective-permute-start(bf16[2,64,2048]{2,1,0:T(8,128)(2,1)S(1)} %get-tuple-element.281.refs_4_), channel_id=1, source_target_pairs={{0,8},{8,0},{1,9},{9,1},{2,10},{10,2},{3,11},{11,3},{4,12},{12,4},... | collective-permute-start | bytes 1572872 | tf_op jit(solution)/shard_map/ppermute | solution.py:384
  308.2 21.1 %collective-permute-start.28 = (bf16[2,64,2048]{2,1,0:T(8,128)(2,1)S(1)}, bf16[2,64,2048]{2,1,0:T(8,128)(2,1)S(1)}, u32[]{:S(2)}, u32[]{:S(2)}) collective-permute-start(bf16[2,64,2048]{2,1,0:T(8,128)(2,1)S(1)} %get-tuple-element.289.refs_2_), channel_id=1, source_target_pairs={{0,2},{2,0},{1,3},{3,1},{4,6},{6,4},{5,7},{7,5},{8,10},{10,8},{9,1... | collective-permute-start | bytes 1572872 | tf_op jit(solution)/shard_map/ppermute | solution.py:384
  318.0 14.2 %collective-permute-start.29 = (bf16[2,64,2048]{2,1,0:T(8,128)(2,1)S(1)}, bf16[2,64,2048]{2,1,0:T(8,128)(2,1)S(1)}, u32[]{:S(2)}, u32[]{:S(2)}) collective-permute-start(bf16[2,64,2048]{2,1,0:T(8,128)(2,1)S(1)} %get-tuple-element.290.refs_4_), channel_id=1, source_target_pairs={{0,8},{8,0},{1,9},{9,1},{2,10},{10,2},{3,11},{11,3},{4,12},{12,4},... | collective-permute-start | bytes 1572872 | tf_op jit(solution)/shard_map/ppermute | solution.py:384
  319.6 16.8 %collective-permute-start.33 = (bf16[2,160,2048]{2,1,0:T(8,128)(2,1)}, bf16[2,160,2048]{2,1,0:T(8,128)(2,1)S(1)}, u32[]{:S(2)}, u32[]{:S(2)}) collective-permute-start(bf16[2,160,2048]{2,1,0:T(8,128)(2,1)} %bitcast.234), channel_id=1, source_target_pairs={{0,1},{1,0},{2,3},{3,2},{4,5},{5,4},{6,7},{7,6},{8,9},{9,8},{10,11... | collective-permute-start | bytes 3932168 | tf_op jit(solution)/shard_map/ppermute | solution.py:384
  332.3 26.1 %collective-permute-start.30 = (bf16[4,64,2048]{2,1,0:T(8,128)(2,1)S(1)}, bf16[4,64,2048]{2,1,0:T(8,128)(2,1)S(1)}, u32[]{:S(2)}, u32[]{:S(2)}) collective-permute-start(bf16[4,64,2048]{2,1,0:T(8,128)(2,1)S(1)} %get-tuple-element.291.refs_0_), channel_id=1, source_target_pairs={{0,2},{2,0},{1,3},{3,1},{4,6},{6,4},{5,7},{7,5},{8,10},{10,8},{9,1... | collective-permute-start | bytes 3145736 | tf_op jit(solution)/shard_map/ppermute | solution.py:384
  332.8 27.0 %collective-permute-start.31 = (bf16[4,64,2048]{2,1,0:T(8,128)(2,1)S(1)}, bf16[4,64,2048]{2,1,0:T(8,128)(2,1)S(1)}, u32[]{:S(2)}, u32[]{:S(2)}) collective-permute-start(bf16[4,64,2048]{2,1,0:T(8,128)(2,1)S(1)} %get-tuple-element.292.refs_2_), channel_id=1, source_target_pairs={{0,8},{8,0},{1,9},{9,1},{2,10},{10,2},{3,11},{11,3},{4,12},{12,4},... | collective-permute-start | bytes 3145736 | tf_op jit(solution)/shard_map/ppermute | solution.py:384
  333.1 26.7 %collective-permute-start.32 = (bf16[4,64,2048]{2,1,0:T(8,128)(2,1)S(1)}, bf16[4,64,2048]{2,1,0:T(8,128)(2,1)S(1)}, u32[]{:S(2)}, u32[]{:S(2)}) collective-permute-start(bf16[4,64,2048]{2,1,0:T(8,128)(2,1)S(1)} %get-tuple-element.293.refs_4_), channel_id=1, source_target_pairs={{0,4},{4,0},{1,5},{5,1},{2,6},{6,2},{3,7},{7,3},{8,12},{12,8},{9,1... | collective-permute-start | bytes 3145736 | tf_op jit(solution)/shard_map/ppermute | solution.py:384
  334.9 43.1 %collective-permute-start.34 = (bf16[4,64,2048]{2,1,0:T(8,128)(2,1)S(1)}, bf16[4,64,2048]{2,1,0:T(8,128)(2,1)}, u32[]{:S(2)}, u32[]{:S(2)}) collective-permute-start(bf16[4,64,2048]{2,1,0:T(8,128)(2,1)S(1)} %get-tuple-element.305.refs_0_), channel_id=1, source_target_pairs={{0,2},{2,0},{1,3},{3,1},{4,6},{6,4},{5,7},{7,5},{8,10},{10,8},{9,1... | collective-permute-start | bytes 3145736 | tf_op jit(solution)/shard_map/ppermute | solution.py:384
  336.4 42.2 %collective-permute-start.35 = (bf16[4,64,2048]{2,1,0:T(8,128)(2,1)S(1)}, bf16[4,64,2048]{2,1,0:T(8,128)(2,1)S(1)}, u32[]{:S(2)}, u32[]{:S(2)}) collective-permute-start(bf16[4,64,2048]{2,1,0:T(8,128)(2,1)S(1)} %get-tuple-element.306.refs_2_), channel_id=1, source_target_pairs={{0,8},{8,0},{1,9},{9,1},{2,10},{10,2},{3,11},{11,3},{4,12},{12,4},... | collective-permute-start | bytes 3145736 | tf_op jit(solution)/shard_map/ppermute | solution.py:384
  358.4 21.2 %collective-permute-start.36 = (bf16[4,64,2048]{2,1,0:T(8,128)(2,1)S(1)}, bf16[4,64,2048]{2,1,0:T(8,128)(2,1)S(1)}, u32[]{:S(2)}, u32[]{:S(2)}) collective-permute-start(bf16[4,64,2048]{2,1,0:T(8,128)(2,1)S(1)} %get-tuple-element.307.refs_4_), channel_id=1, source_target_pairs={{0,4},{4,0},{1,5},{5,1},{2,6},{6,2},{3,7},{7,3},{8,12},{12,8},{9,1... | collective-permute-start | bytes 3145736 | tf_op jit(solution)/shard_map/ppermute | solution.py:384
  409.5 22.8 %collective-permute-start.39 = (bf16[4,64,2048]{2,1,0:T(8,128)(2,1)}, bf16[4,64,2048]{2,1,0:T(8,128)(2,1)}, u32[]{:S(2)}, u32[]{:S(2)}) collective-permute-start(bf16[4,64,2048]{2,1,0:T(8,128)(2,1)} %bitcast.47), channel_id=1, source_target_pairs={{0,4},{4,0},{1,5},{5,1},{2,6},{6,2},{3,7},{7,3},{8,12},{12,8},{9,1... | collective-permute-start | bytes 3145736 | tf_op jit(solution)/shard_map/ppermute | solution.py:384
  411.0 23.0 %collective-permute-start.38 = (bf16[4,64,2048]{2,1,0:T(8,128)(2,1)}, bf16[4,64,2048]{2,1,0:T(8,128)(2,1)S(1)}, u32[]{:S(2)}, u32[]{:S(2)}) collective-permute-start(bf16[4,64,2048]{2,1,0:T(8,128)(2,1)} %bitcast.262), channel_id=1, source_target_pairs={{0,8},{8,0},{1,9},{9,1},{2,10},{10,2},{3,11},{11,3},{4,12},{12,4},... | collective-permute-start | bytes 3145736 | tf_op jit(solution)/shard_map/ppermute | solution.py:384
  411.7 22.6 %collective-permute-start.37 = (bf16[4,64,2048]{2,1,0:T(8,128)(2,1)}, bf16[4,64,2048]{2,1,0:T(8,128)(2,1)S(1)}, u32[]{:S(2)}, u32[]{:S(2)}) collective-permute-start(bf16[4,64,2048]{2,1,0:T(8,128)(2,1)} %bitcast.261), channel_id=1, source_target_pairs={{0,2},{2,0},{1,3},{3,1},{4,6},{6,4},{5,7},{7,5},{8,10},{10,8},{9,1... | collective-permute-start | bytes 3145736 | tf_op jit(solution)/shard_map/ppermute | solution.py:384
  445.2 14.7 %collective-permute-start.43 = (bf16[2,160,2048]{2,1,0:T(8,128)(2,1)S(1)}, bf16[2,160,2048]{2,1,0:T(8,128)(2,1)S(1)}, u32[]{:S(2)}, u32[]{:S(2)}) collective-permute-start(bf16[2,160,2048]{2,1,0:T(8,128)(2,1)S(1)} %dynamic-slice_bitcast_fusion.3), channel_id=1, source_target_pairs={{0,1},{1,0},{2,3},{3,2},{4,5},{5,4},{6,7},{7,6},{8,9},{9,8},{10,11... | collective-permute-start | bytes 3932168 | tf_op jit(solution)/shard_map/ppermute | solution.py:384
  445.4 14.4 %collective-permute-start.40 = (bf16[2,64,2048]{2,1,0:T(8,128)(2,1)S(1)}, bf16[2,64,2048]{2,1,0:T(8,128)(2,1)S(1)}, u32[]{:S(2)}, u32[]{:S(2)}) collective-permute-start(bf16[2,64,2048]{2,1,0:T(8,128)(2,1)S(1)} %slice.372), channel_id=1, source_target_pairs={{0,4},{4,0},{1,5},{5,1},{2,6},{6,2},{3,7},{7,3},{8,12},{12,8},{9,1... | collective-permute-start | bytes 1572872 | tf_op jit(solution)/shard_map/ppermute | solution.py:384
  482.8 21.8 %all-to-all-start.5 = ((bf16[8,192,256]{2,1,0:T(8,128)(2,1)}), bf16[8,192,256]{2,1,0:T(8,128)(2,1)}, u32[]{:S(2)}, u32[]{:S(2)}) async-start(bf16[8,192,256]{2,1,0:T(8,128)(2,1)} %bitcast.201), calls=%async_computation.5 | async-start | bytes 1572864 | tf_op jit(solution)/shard_map/all_to_all | solution.py:536
  487.0 129.1 %reduce-scatter.4.cloned.1.call-start = ((), (), s32[]{:S(2)}) async-start(), calls=%async_computation.12 | async-start | bytes 3932160 | tf_op jit(solution)/shard_map/reduce_scatter | solution.py:687
  521.4 125.7 %reduce-scatter.6.cloned.1.call-start = ((), (), s32[]{:S(2)}) async-start(), calls=%async_computation.13 | async-start | bytes 1966080 | tf_op jit(solution)/shard_map/reduce_scatter | solution.py:687
  526.8 36.8 %collective-permute-start.50 = (bf16[4,96,2048]{2,1,0:T(8,128)(2,1)}, bf16[4,96,2048]{2,1,0:T(8,128)(2,1)}, u32[]{:S(2)}, u32[]{:S(2)}) collective-permute-start(bf16[4,96,2048]{2,1,0:T(8,128)(2,1)} %bitcast.62), channel_id=1, source_target_pairs={{0,2},{2,0},{1,3},{3,1},{4,6},{6,4},{5,7},{7,5},{8,10},{10,8},{9,1... | collective-permute-start | bytes 4718600 | tf_op jit(solution)/shard_map/ppermute | solution.py:384
  528.7 36.5 %collective-permute-start.51 = (bf16[4,96,2048]{2,1,0:T(8,128)(2,1)}, bf16[4,96,2048]{2,1,0:T(8,128)(2,1)}, u32[]{:S(2)}, u32[]{:S(2)}) collective-permute-start(bf16[4,96,2048]{2,1,0:T(8,128)(2,1)} %bitcast.63), channel_id=1, source_target_pairs={{0,4},{4,0},{1,5},{5,1},{2,6},{6,2},{3,7},{7,3},{8,12},{12,8},{9,1... | collective-permute-start | bytes 4718600 | tf_op jit(solution)/shard_map/ppermute | solution.py:384
  572.3 43.7 %collective-permute-start.54 = (bf16[4,64,2048]{2,1,0:T(8,128)(2,1)}, bf16[4,64,2048]{2,1,0:T(8,128)(2,1)}, u32[]{:S(2)}, u32[]{:S(2)}) collective-permute-start(bf16[4,64,2048]{2,1,0:T(8,128)(2,1)} %get-tuple-element.420), channel_id=1, source_target_pairs={{0,2},{2,0},{1,3},{3,1},{4,6},{6,4},{5,7},{7,5},{8,10},{10,8},{9,1... | collective-permute-start | bytes 3145736 | tf_op jit(solution)/shard_map/ppermute | solution.py:384
  572.4 43.6 %collective-permute-start.55 = (bf16[4,64,2048]{2,1,0:T(8,128)(2,1)}, bf16[4,64,2048]{2,1,0:T(8,128)(2,1)}, u32[]{:S(2)}, u32[]{:S(2)}) collective-permute-start(bf16[4,64,2048]{2,1,0:T(8,128)(2,1)} %get-tuple-element.419), channel_id=1, source_target_pairs={{0,4},{4,0},{1,5},{5,1},{2,6},{6,2},{3,7},{7,3},{8,12},{12,8},{9,1... | collective-permute-start | bytes 3145736 | tf_op jit(solution)/shard_map/ppermute | solution.py:384
  577.2 38.7 %collective-permute-start.53 = (bf16[2,96,2048]{2,1,0:T(8,128)(2,1)}, bf16[2,96,2048]{2,1,0:T(8,128)(2,1)}, u32[]{:S(2)}, u32[]{:S(2)}) collective-permute-start(bf16[2,96,2048]{2,1,0:T(8,128)(2,1)} %slice.451), channel_id=1, source_target_pairs={{0,2},{2,0},{1,3},{3,1},{4,6},{6,4},{5,7},{7,5},{8,10},{10,8},{9,1... | collective-permute-start | bytes 2359304 | tf_op jit(solution)/shard_map/ppermute | solution.py:384
  580.9 35.0 %collective-permute-start.52 = (bf16[2,96,2048]{2,1,0:T(8,128)(2,1)S(1)}, bf16[2,96,2048]{2,1,0:T(8,128)(2,1)S(1)}, u32[]{:S(2)}, u32[]{:S(2)}) collective-permute-start(bf16[2,96,2048]{2,1,0:T(8,128)(2,1)S(1)} %slice.450), channel_id=1, source_target_pairs={{0,4},{4,0},{1,5},{5,1},{2,6},{6,2},{3,7},{7,3},{8,12},{12,8},{9,1... | collective-permute-start | bytes 2359304 | tf_op jit(solution)/shard_map/ppermute | solution.py:384
  616.0 19.0 %collective-permute-start.56 = (bf16[1536,384]{1,0:T(8,128)(2,1)}, bf16[1536,384]{1,0:T(8,128)(2,1)}, u32[]{:S(2)}, u32[]{:S(2)}) collective-permute-start(bf16[1536,384]{1,0:T(8,128)(2,1)} %get-tuple-element.360), channel_id=1, source_target_pairs={{0,1},{1,0},{2,3},{3,2},{4,5},{5,4},{6,7},{7,6},{8,9},{9,8},{10,11... | collective-permute-start | bytes 3538952 | tf_op jit(solution)/shard_map/ppermute | solution.py:384
  622.3 24.8 %collective-permute-start.58 = (bf16[2,64,2048]{2,1,0:T(8,128)(2,1)}, bf16[2,64,2048]{2,1,0:T(8,128)(2,1)}, u32[]{:S(2)}, u32[]{:S(2)}) collective-permute-start(bf16[2,64,2048]{2,1,0:T(8,128)(2,1)} %slice.459), channel_id=1, source_target_pairs={{0,4},{4,0},{1,5},{5,1},{2,6},{6,2},{3,7},{7,3},{8,12},{12,8},{9,1... | collective-permute-start | bytes 1572872 | tf_op jit(solution)/shard_map/ppermute | solution.py:384
  624.5 22.5 %collective-permute-start.59 = (bf16[2,64,2048]{2,1,0:T(8,128)(2,1)}, bf16[2,64,2048]{2,1,0:T(8,128)(2,1)}, u32[]{:S(2)}, u32[]{:S(2)}) collective-permute-start(bf16[2,64,2048]{2,1,0:T(8,128)(2,1)} %slice.461), channel_id=1, source_target_pairs={{0,2},{2,0},{1,3},{3,1},{4,6},{6,4},{5,7},{7,5},{8,10},{10,8},{9,1... | collective-permute-start | bytes 1572872 | tf_op jit(solution)/shard_map/ppermute | solution.py:384
  626.4 20.7 %collective-permute-start.57 = (bf16[2,96,2048]{2,1,0:T(8,128)(2,1)}, bf16[2,96,2048]{2,1,0:T(8,128)(2,1)}, u32[]{:S(2)}, u32[]{:S(2)}) collective-permute-start(bf16[2,96,2048]{2,1,0:T(8,128)(2,1)} %fusion.43), channel_id=1, source_target_pairs={{0,8},{8,0},{1,9},{9,1},{2,10},{10,2},{3,11},{11,3},{4,12},{12,4},... | collective-permute-start | bytes 2359304 | tf_op jit(solution)/shard_map/ppermute | solution.py:384
  627.9 68.3 %all-to-all-start.6 = ((bf16[8,64,1280]{2,1,0:T(8,128)(2,1)}), bf16[8,64,1280]{2,1,0:T(8,128)(2,1)}, u32[]{:S(2)}, u32[]{:S(2)}) async-start(bf16[8,64,1280]{2,1,0:T(8,128)(2,1)} %bitcast.70), calls=%async_computation.8 | async-start | bytes 2621440 | tf_op jit(solution)/shard_map/all_to_all | solution.py:536
  632.2 121.6 %reduce-scatter.8.cloned.1.call-start = ((), (), s32[]{:S(2)}) async-start(), calls=%async_computation.14 | async-start | bytes 2359296 | tf_op jit(solution)/shard_map/reduce_scatter | solution.py:687
  649.7 46.5 %collective-permute-start.63 = (bf16[96,2048]{1,0:T(8,128)(2,1)}, bf16[96,2048]{1,0:T(8,128)(2,1)}, u32[]{:S(2)}, u32[]{:S(2)}) collective-permute-start(bf16[96,2048]{1,0:T(8,128)(2,1)} %get-tuple-element.422), channel_id=1, source_target_pairs={{0,16},{16,0},{1,17},{17,1},{2,18},{18,2},{3,19},{19,3},{4,20},{20... | collective-permute-start | bytes 1179656 | tf_op jit(solution)/shard_map/ppermute | solution.py:384
  654.3 27.2 %collective-permute-start.62 = (bf16[4,64,2048]{2,1,0:T(8,128)(2,1)}, bf16[4,64,2048]{2,1,0:T(8,128)(2,1)}, u32[]{:S(2)}, u32[]{:S(2)}) collective-permute-start(bf16[4,64,2048]{2,1,0:T(8,128)(2,1)} %bitcast.85), channel_id=1, source_target_pairs={{0,4},{4,0},{1,5},{5,1},{2,6},{6,2},{3,7},{7,3},{8,12},{12,8},{9,1... | collective-permute-start | bytes 3145736 | tf_op jit(solution)/shard_map/ppermute | solution.py:384
  656.2 34.8 %collective-permute-start.61 = (bf16[4,64,2048]{2,1,0:T(8,128)(2,1)}, bf16[4,64,2048]{2,1,0:T(8,128)(2,1)}, u32[]{:S(2)}, u32[]{:S(2)}) collective-permute-start(bf16[4,64,2048]{2,1,0:T(8,128)(2,1)} %bitcast.83), channel_id=1, source_target_pairs={{0,8},{8,0},{1,9},{9,1},{2,10},{10,2},{3,11},{11,3},{4,12},{12,4},... | collective-permute-start | bytes 3145736 | tf_op jit(solution)/shard_map/ppermute | solution.py:384
  657.7 35.9 %collective-permute-start.60 = (bf16[4,64,2048]{2,1,0:T(8,128)(2,1)}, bf16[4,64,2048]{2,1,0:T(8,128)(2,1)}, u32[]{:S(2)}, u32[]{:S(2)}) collective-permute-start(bf16[4,64,2048]{2,1,0:T(8,128)(2,1)} %bitcast.81), channel_id=1, source_target_pairs={{0,2},{2,0},{1,3},{3,1},{4,6},{6,4},{5,7},{7,5},{8,10},{10,8},{9,1... | collective-permute-start | bytes 3145736 | tf_op jit(solution)/shard_map/ppermute | solution.py:384
  699.6 15.6 %collective-permute-start.66 = (bf16[2,64,2048]{2,1,0:T(8,128)(2,1)}, bf16[2,64,2048]{2,1,0:T(8,128)(2,1)}, u32[]{:S(2)}, u32[]{:S(2)}) collective-permute-start(bf16[2,64,2048]{2,1,0:T(8,128)(2,1)} %slice.422), channel_id=1, source_target_pairs={{0,8},{8,0},{1,9},{9,1},{2,10},{10,2},{3,11},{11,3},{4,12},{12,4},... | collective-permute-start | bytes 1572872 | tf_op jit(solution)/shard_map/ppermute | solution.py:384
  701.9 14.6 %collective-permute-start.65 = (bf16[2,64,2048]{2,1,0:T(8,128)(2,1)}, bf16[2,64,2048]{2,1,0:T(8,128)(2,1)}, u32[]{:S(2)}, u32[]{:S(2)}) collective-permute-start(bf16[2,64,2048]{2,1,0:T(8,128)(2,1)} %slice.420), channel_id=1, source_target_pairs={{0,2},{2,0},{1,3},{3,1},{4,6},{6,4},{5,7},{7,5},{8,10},{10,8},{9,1... | collective-permute-start | bytes 1572872 | tf_op jit(solution)/shard_map/ppermute | solution.py:384
  720.4 33.3 %collective-permute-start.70 = (bf16[2,64,2048]{2,1,0:T(8,128)(2,1)S(1)}, bf16[2,64,2048]{2,1,0:T(8,128)(2,1)S(1)}, u32[]{:S(2)}, u32[]{:S(2)}) collective-permute-start(bf16[2,64,2048]{2,1,0:T(8,128)(2,1)S(1)} %slice_bitcast_fusion.6), channel_id=1, source_target_pairs={{0,8},{8,0},{1,9},{9,1},{2,10},{10,2},{3,11},{11,3},{4,12},{12,4},... | collective-permute-start | bytes 1572872 | tf_op jit(solution)/shard_map/ppermute | solution.py:384
  728.4 24.5 %collective-permute-start.67 = (bf16[1,64,2048]{2,1,0:T(8,128)(2,1)S(1)}, bf16[1,64,2048]{2,1,0:T(8,128)(2,1)S(1)}, u32[]{:S(2)}, u32[]{:S(2)}) collective-permute-start(bf16[1,64,2048]{2,1,0:T(8,128)(2,1)S(1)} %slice.424), channel_id=1, source_target_pairs={{0,8},{8,0},{1,9},{9,1},{2,10},{10,2},{3,11},{11,3},{4,12},{12,4},... | collective-permute-start | bytes 786440 | tf_op jit(solution)/shard_map/ppermute | solution.py:384
  755.4 29.9 %all-to-all-start.7 = ((bf16[8,64,768]{2,1,0:T(8,128)(2,1)}), bf16[8,64,768]{2,1,0:T(8,128)(2,1)S(1)}, u32[]{:S(2)}, u32[]{:S(2)}) async-start(bf16[8,64,768]{2,1,0:T(8,128)(2,1)} %bitcast.263), calls=%async_computation.10 | async-start | bytes 1572864 | tf_op jit(solution)/shard_map/all_to_all | solution.py:536
  763.0 21.2 %collective-permute-start.72 = (bf16[96,2048]{1,0:T(8,128)(2,1)S(1)}, bf16[96,2048]{1,0:T(8,128)(2,1)S(1)}, u32[]{:S(2)}, u32[]{:S(2)}) collective-permute-start(bf16[96,2048]{1,0:T(8,128)(2,1)S(1)} %get-tuple-element.430), channel_id=1, source_target_pairs={{0,16},{16,0},{1,17},{17,1},{2,18},{18,2},{3,19},{19,3},{4,20},{20... | collective-permute-start | bytes 1179656 | tf_op jit(solution)/shard_map/ppermute | solution.py:384
  (138 other events, 1207.1 us)
Sparse Core Ops, SparseCore 0:
  173.4 68.8 all-gather.4
  265.9 37.2 all-gather.6
  521.5 66.7 reduce-scatter.3
  591.1 37.1 reduce-scatter.5
  706.8 41.9 reduce-scatter.7
